TPU v7x, 32 devices: a whole 2x2x4 slice. The times are simulated.
32 devices in a mesh: groups: 2 (over y), hold: 4 (over z), tp: 4 (over x, core).
Axes of the slice: x: 2, y: 2, z: 4, core: 2. Of those that a mesh axis runs over, the one named last changes fastest.
Arguments:
- cache_store: bfloat16 [2, 32, 256, 8, 2, 128], P(None, ('groups', 'hold'), None, 'tp'), parts along dimension 1, may hold values from -6 to 6
- span_lengths: int32 [8, 4], P(('groups', 'hold')), parts along dimension 0, may hold values from 1 to 256, 512 in all within a row
- span_holder: int32 [8, 4], P(('groups', 'hold')), parts along dimension 0, may hold values from 0 to 3, as said below
- rec_pos: int32 [2, 640], P(None, ('groups', 'hold')), parts along dimension 1, may hold values from 0 to 2047, as said below
- hidden: bfloat16 [2, 640, 12288], P(None, ('groups', 'hold')), parts along dimension 1, may hold values from -6 to 6
- norm_gain: bfloat16 [2, 12288], replicated, may hold values from 0.099609375 to 1.8984375
- kv_weight: bfloat16 [2, 12288, 8, 2, 128], P(None, 'hold', 'tp'), may hold values from -0.0546875 to 0.0546875
Outputs:
- united_cache: bfloat16 [2, 4096, 8, 2, 128], P(None, ('groups', 'hold'), 'tp'), parts along dimension 1
- deviation: float32 [2, 640], P(None, ('groups', 'hold')), parts along dimension 1
There are 2 independent parts, one for each index of `groups`. A program takes and returns all parts, laid end to end along the dimension named above; an argument that names none is the same for every part. Nothing has to cross between parts.
Inputs may be any that keep to these rules, and one draw needn't show every extreme that they name: `span_holder`: each row holds 4 distinct holders. `rec_pos`: entries p * 80 to (p + 1) * 80 - 1 of each layer are distinct positions of block p in increasing order, the block's last position among them. `span_lengths`: each row sums to 512.
All inputs are finite; a program needn't handle non-finite values.
Results may differ from a plain program's by a relative error of at most 0.0019.
Values may be sent and summed in bfloat16 or wider, within the bound.
No kernel may reach another device: no remote copies, remote signals or barrier semaphores. Data moves between devices by JAX's collectives and lax.ppermute only.
A program may use at most 128 MiB of HBM per device.

v0:
```python
import jax
import jax.numpy as jnp
from jax import lax
from jax.sharding import PartitionSpec as P

KVH = 8
PROMPT_PER_HOLD = 512
LAYERS = 2


def block_arrangement(lengths, holders_row):
    starts = jnp.cumsum(lengths, axis=1) - lengths
    span_offsets = jnp.arange(PROMPT_PER_HOLD, dtype=jnp.int32)
    which = (
        jnp.sum((span_offsets[None, :, None] >= starts[:, None, :]).astype(jnp.int32), axis=2) - 1
    )
    holder = jnp.take_along_axis(holders_row, which, axis=1)
    within = span_offsets[None, :] - jnp.take_along_axis(starts, which, axis=1)
    return (holder, within)


def local(cache_store, span_lengths, span_holder, rec_pos, hidden, norm_gain, kv_weight):
    my_index = lax.axis_index("hold")
    holder, within = block_arrangement(span_lengths, span_holder)
    holder = holder[0]
    within = within[0]
    heads_here = kv_weight.shape[2]
    head_size = kv_weight.shape[4]
    width = heads_here * 2 * head_size
    rec_count = hidden.shape[1]
    united_list = []
    squares_list = []
    base_list = []
    for layer in range(LAYERS):
        pages = lax.all_to_all(cache_store[layer], "hold", split_axis=0, concat_axis=0, tiled=True)
        cached = pages[holder, within]
        rows_in = hidden[layer].astype(jnp.float32)
        scale = lax.rsqrt(jnp.mean(rows_in * rows_in, axis=1, keepdims=True) + 1e-05)
        normed = (rows_in * scale * norm_gain[layer].astype(jnp.float32)).astype(jnp.bfloat16)
        piece = lax.all_gather(kv_weight[layer], "hold", axis=0, tiled=True)
        fresh_sum = jnp.dot(
            normed, piece.reshape(piece.shape[0], width), preferred_element_type=jnp.float32
        )
        fresh = fresh_sum.astype(jnp.bfloat16).reshape(rec_count, heads_here, 2, head_size)
        span_offsets = rec_pos[layer] - my_index * PROMPT_PER_HOLD
        old = cached[span_offsets].astype(jnp.float32)
        diff = fresh.astype(jnp.float32) - old
        squares = jnp.sum(diff * diff, axis=(1, 2, 3))
        base = jnp.sum(old * old, axis=(1, 2, 3))
        squares, base = lax.psum((squares, base), "tp")
        squares_list.append(squares)
        base_list.append(base)
        united_list.append(cached.at[span_offsets].set(fresh))
    squares_all = jnp.stack(squares_list)
    base_all = jnp.stack(base_list)
    entries = KVH * 2 * head_size
    deviation = squares_all / entries / (base_all / entries + 1e-06)
    return (jnp.stack(united_list), deviation)


def solution(mesh):
    return jax.shard_map(
        local,
        mesh=mesh,
        in_specs=(
            P(None, ("groups", "hold"), None, "tp", None, None),
            P(("groups", "hold"), None),
            P(("groups", "hold"), None),
            P(None, ("groups", "hold")),
            P(None, ("groups", "hold"), None),
            P(),
            P(None, "hold", "tp", None, None),
        ),
        out_specs=(P(None, ("groups", "hold"), "tp", None, None), P(None, ("groups", "hold"))),
        check_vma=False,
    )
```

profile of v0, /device:TPU:0, one launch (start us, length us, event | category | flops | bytes accessed | tf_op | source)
XLA Modules:
  0.0 542.7 jit_solution(13473851679803889867)
XLA Ops:
  7.2 8.4 %slice_bitcast_fusion.1 = (bf16[1,3072,2,2,128]{4,3,2,0,1:T(2,128)(2,1)}, bf16[1,3072,2,2,128]{4,3,2,0,1:T(2,128)(2,1)}) fusion(bf16[2,3072,2,2,128]{4,3,2,1,0:T(2,128)(2,1)} %param.15), kind=kLoop, calls=%fused_computation.17 | loop fusion | bytes 12582912
  15.7 0.7 all-gather.5.cloned.1.call-update
  16.4 0.8 copy-done
  17.3 2.5 slice_bitcast_fusion.3
  19.7 6.4 %all-to-all-start = ((bf16[4,256,2,2,128]{4,3,2,1,0:T(2,128)(2,1)}), bf16[4,256,2,2,128]{4,3,2,1,0:T(2,128)(2,1)S(1)}, u32[]{:S(2)}, u32[]{:S(2)}) async-start(bf16[4,256,2,2,128]{4,3,2,1,0:T(2,128)(2,1)} %get-tuple-element.11), calls=%async_computation | async-start | bytes 2097152 | tf_op jit(solution)/shard_map/all_to_all | solution.py:35
  27.8 3.6 fusion
  31.4 5.2 fusion.29
  36.6 43.5 %all-to-all-done = bf16[4,256,2,2,128]{4,3,2,1,0:T(2,128)(2,1)S(1)} async-done(((bf16[4,256,2,2,128]{4,3,2,1,0:T(2,128)(2,1)}), bf16[4,256,2,2,128]{4,3,2,1,0:T(2,128)(2,1)S(1)}, u32[]{:S(2)}, u32[]{:S(2)}) %all-to-all-start) | async-done | bytes 1048608 | tf_op jit(solution)/shard_map/all_to_all | solution.py:35
  80.1 3.7 all-to-all-start.1
  83.9 3.3 gather_fusion
  87.1 0.7 gather_fusion.2
  87.9 43.8 %all-to-all-done.1 = bf16[4,256,2,2,128]{4,3,2,1,0:T(2,128)(2,1)S(1)} async-done(((bf16[4,256,2,2,128]{4,3,2,1,0:T(2,128)(2,1)}), bf16[4,256,2,2,128]{4,3,2,1,0:T(2,128)(2,1)S(1)}, u32[]{:S(2)}, u32[]{:S(2)}) %all-to-all-start.1) | async-done | bytes 1048608 | tf_op jit(solution)/shard_map/all_to_all | solution.py:35
  131.7 3.3 gather_fusion.1
  135.0 0.7 gather_fusion.3
  137.1 140.2 %all-gather.7.cloned.1.call-done = bf16[1,12288,2,2,128]{4,3,2,0,1:T(2,128)(2,1)} async-done(((bf16[1,3072,2,2,128]{4,3,2,0,1:T(2,128)(2,1)}), bf16[1,12288,2,2,128]{4,3,2,0,1:T(2,128)(2,1)}) %all-gather.7.cloned.1.call-update) | async-done | bytes 12582928 | tf_op jit(solution)/shard_map/all_gather | solution.py:40
  277.3 19.5 %reshape.242 = bf16[12288,512]{1,0:T(8,128)(2,1)} reshape(bf16[1,12288,2,2,128]{4,3,2,0,1:T(2,128)(2,1)} %all-gather.7.cloned.1.call-done) | data formatting | bytes 25165824 | tf_op jit(solution)/shard_map/reshape | solution.py:42
  296.8 7.6 %multiply_reduce_fusion.2 = (f32[80]{0:T(128)S(1)}, bf16[80,512]{1,0:T(8,128)(2,1)S(1)}) fusion(f32[80,512]{1,0:T(8,128)S(1)} %reshape.248, bf16[12288,512]{1,0:T(8,128)(2,1)} %reshape.242, f32[12288]{0:T(1024)S(1)} %bitcast.66, f32[80]{0:T(128)S(1)} %add_rsqrt_fusion, bf16[2,80,12288]{2,1,0:T(8,128)(2,1)} %param.13), kind=kOutput, calls=%fused_computation.35 | convolution fusion | flops 1010769856 | bytes 14844544 | tf_op jit(solution)/shard_map/dot_general | solution.py:41
  304.5 3.1 scatter_fusion.1
  307.6 188.7 %all-gather.5.cloned.1.call-done = bf16[1,12288,2,2,128]{4,3,2,0,1:T(2,128)(2,1)} async-done(((bf16[1,3072,2,2,128]{4,3,2,0,1:T(2,128)(2,1)}), bf16[1,12288,2,2,128]{4,3,2,0,1:T(2,128)(2,1)}) %all-gather.5.cloned.1.call-update) | async-done | bytes 12582928 | tf_op jit(solution)/shard_map/all_gather | solution.py:40
  496.2 19.0 %reshape.240 = bf16[12288,512]{1,0:T(8,128)(2,1)} reshape(bf16[1,12288,2,2,128]{4,3,2,0,1:T(2,128)(2,1)} %all-gather.5.cloned.1.call-done) | data formatting | bytes 25165824 | tf_op jit(solution)/shard_map/reshape | solution.py:42
  515.2 7.6 %multiply_reduce_fusion.3 = (f32[80]{0:T(128)S(1)}, bf16[80,512]{1,0:T(8,128)(2,1)S(1)}) fusion(f32[80,512]{1,0:T(8,128)S(1)} %reshape.247, bf16[12288,512]{1,0:T(8,128)(2,1)} %reshape.240, f32[12288]{0:T(1024)S(1)} %bitcast.65, f32[80]{0:T(128)S(1)} %add_rsqrt_fusion.1, bf16[2,80,12288]{2,1,0:T(8,128)(2,1)} %param.13), kind=kOutput, calls=%fused_computation.36 | convolution fusion | flops 1010769856 | bytes 14844544 | tf_op jit(solution)/shard_map/dot_general | solution.py:41
  522.9 3.1 scatter_fusion
  526.0 2.5 pad_maximum_fusion
  528.5 6.8 %all-reduce = (f32[1,80]{1,0:T(1,128)S(1)}, f32[1,80]{1,0:T(1,128)S(1)}, f32[1,80]{1,0:T(1,128)S(1)}, f32[1,80]{1,0:T(1,128)S(1)}) all-reduce(f32[1,80]{1,0:T(1,128)S(1)} %bitcast.69, f32[1,80]{1,0:T(1,128)S(1)} %bitcast.70, f32[1,80]{1,0:T(1,128)S(1)} %bitcast.71, ...), channel_id=1, replica_groups=mesh['groups'=2,'hold'=4,'tp'=4] {'tp'}, use_global_device_ids=true, to_apply=%region_9.11 | all-reduce | flops 320 | bytes 2560 | tf_op jit(solution)/shard_map/psum | solution.py:50
  (31 shorter events, 3.8 us)
Async XLA Ops:
  7.2 270.1 %all-gather.7.cloned.1.call-start = ((), (), s32[]{:S(2)}) async-start(), calls=%async_computation.3 | async-start | bytes 15728640 | tf_op jit(solution)/shard_map/all_gather | solution.py:40
  15.7 1.6 copy-start
  15.7 480.6 %all-gather.5.cloned.1.call-start = ((), (), s32[]{:S(2)}) async-start(), calls=%async_computation.2 | async-start | bytes 15728640 | tf_op jit(solution)/shard_map/all_gather | solution.py:40
  17.2 8.9 %copy-start.3 = (s32[2,80]{1,0:T(2,128)S(1)}, s32[2,80]{1,0:T(2,128)}, u32[]{:S(2)}) copy-start(s32[2,80]{1,0:T(2,128)} %param.12) | copy-start | bytes 1924
  17.3 9.0 %copy-start.4 = (s32[1,4]{1,0:T(1,128)S(1)}, s32[1,4]{1,0:T(1,128)}, u32[]{:S(2)}) copy-start(s32[1,4]{1,0:T(1,128)} %param.10) | copy-start | bytes 52
  17.3 9.8 %copy-start.2 = (s32[1,4]{1,0:T(1,128)S(1)}, s32[1,4]{1,0:T(1,128)}, u32[]{:S(2)}) copy-start(s32[1,4]{1,0:T(1,128)} %param.11) | copy-start | bytes 52
  19.7 64.1 %copy-start.1 = (bf16[2,12288]{1,0:T(2,128)(2,1)S(1)}, bf16[2,12288]{1,0:T(2,128)(2,1)}, u32[]{:S(2)}) copy-start(bf16[2,12288]{1,0:T(2,128)(2,1)} %param.14) | copy-start | bytes 147460
  19.7 60.4 %all-to-all-start = ((bf16[4,256,2,2,128]{4,3,2,1,0:T(2,128)(2,1)}), bf16[4,256,2,2,128]{4,3,2,1,0:T(2,128)(2,1)S(1)}, u32[]{:S(2)}, u32[]{:S(2)}) async-start(bf16[4,256,2,2,128]{4,3,2,1,0:T(2,128)(2,1)} %get-tuple-element.11), calls=%async_computation | async-start | bytes 2097152 | tf_op jit(solution)/shard_map/all_to_all | solution.py:35
  80.1 51.6 %all-to-all-start.1 = ((bf16[4,256,2,2,128]{4,3,2,1,0:T(2,128)(2,1)}), bf16[4,256,2,2,128]{4,3,2,1,0:T(2,128)(2,1)S(1)}, u32[]{:S(2)}, u32[]{:S(2)}) async-start(bf16[4,256,2,2,128]{4,3,2,1,0:T(2,128)(2,1)} %get-tuple-element.12), calls=%async_computation.1 | async-start | bytes 2097152 | tf_op jit(solution)/shard_map/all_to_all | solution.py:35
Sparse Core Ops, SparseCore 0:
  15.8 261.4 all-gather.6
  278.9 217.3 all-gather.4
where the time goes:
time: 544 us; the launch traced here: 543 us
  waiting for transfers between devices  417 us (77%)
  local copies, waits for them, and re-layouts  65.8 us (12%)
  matrix products  15.3 us (3%)
  between operations  14.2 us (3%)
  other arithmetic  13.6 us (2%)
  starting transfers between devices  10.2 us (2%)
  blocking collectives  6.81 us (1%)
    all_gather x2, waiting for transfers between devices, local(): piece = lax.all_gather(kv_weight[layer], 'hold', axis=0, tiled=True)  329 us
    all_to_all x2, waiting for transfers between devices, local(): lax.all_to_all(cache_store[layer], 'hold', split_axis=0, concat_axis=0, t...  87.2 us
    reshape x2, local copies, waits for them, and re-layouts, local(): piece.reshape(piece.shape[0], width)  38.5 us
    dot_general x2, matrix products, local(): jnp.dot(normed, piece.reshape(piece.shape[0], width), preferred_element_t...  15.3 us
  transfers between devices with their start and end apart: 4, of which 4 were waited for; matrix products, arithmetic and copies ran while one was open for 10% of the time, Pallas kernels for 0%

commit v1 on v0

v1 whole, which is shorter than its diff:
```python
import jax
import jax.numpy as jnp
from jax import lax
from jax.sharding import PartitionSpec as P

KVH = 8
PROMPT_PER_HOLD = 512
LAYERS = 2


def block_arrangement(lengths, holders_row):
    starts = jnp.cumsum(lengths, axis=1) - lengths
    span_offsets = jnp.arange(PROMPT_PER_HOLD, dtype=jnp.int32)
    which = (
        jnp.sum((span_offsets[None, :, None] >= starts[:, None, :]).astype(jnp.int32), axis=2) - 1
    )
    holder = jnp.take_along_axis(holders_row, which, axis=1)
    within = span_offsets[None, :] - jnp.take_along_axis(starts, which, axis=1)
    return (holder, within)


def norm_rows(rows, gain):
    rows = rows.astype(jnp.float32)
    scale = lax.rsqrt(jnp.mean(rows * rows, axis=1, keepdims=True) + 1e-05)
    return (rows * scale * gain.astype(jnp.float32)).astype(jnp.bfloat16)


def make_local(n, tps):
    def shift(value, k):
        return lax.ppermute(value, "hold", [(i, (i + k) % n) for i in range(n)])

    def local(cache_store, span_lengths, span_holder, rec_pos, hidden, norm_gain, kv_weight):
        me = lax.axis_index("hold")
        my_tp = lax.axis_index("tp")
        rec = hidden.shape[1]
        width = hidden.shape[2]
        feats = kv_weight.shape[1]
        heads_here, head_size = kv_weight.shape[2], kv_weight.shape[4]
        cols = heads_here * 2 * head_size
        rows_all = LAYERS * rec
        quarter = rows_all // tps

        flat = hidden.reshape(rows_all, width)
        gain_rows = jnp.repeat(norm_gain, rec, axis=0)
        mine = lax.dynamic_slice_in_dim(flat, my_tp * quarter, quarter, axis=0)
        mine_gain = norm_gain[(my_tp * quarter + jnp.arange(quarter)) // rec]
        normed = norm_rows(mine, mine_gain)
        arrived = []
        for k in range(1, n):
            piece = lax.dynamic_slice_in_dim(normed, ((me + k) % n) * feats, feats, axis=1)
            arrived.append(shift(piece, k))

        pages = [lax.dynamic_index_in_dim(cache_store, me, axis=1, keepdims=False)]
        for k in range(1, n):
            page = lax.dynamic_index_in_dim(cache_store, (me + k) % n, axis=1, keepdims=False)
            pages.append(shift(page, k))

        own_full = norm_rows(flat, gain_rows)
        own = lax.dynamic_slice_in_dim(own_full, me * feats, feats, axis=1)
        weight = kv_weight.reshape(LAYERS, feats, cols)
        stacked = jnp.stack(arrived)
        gathered = lax.all_gather(stacked, "tp", axis=1, tiled=True)
        rows = jnp.concatenate([own[None], gathered]).reshape(n, LAYERS, rec, feats)
        partial = jnp.einsum(
            "klrf,lfc->klrc", rows, weight, preferred_element_type=jnp.float32
        )
        odd = partial[1::2]
        odd = jnp.where(me % 2 == 0, jnp.roll(odd, 1, axis=0), odd)
        pairs = [(i, i ^ 1) for i in range(n)]
        summed = partial[0::2] + lax.ppermute(odd, "hold", pairs)
        total = summed[0]
        for k in range(2, n, 2):
            total = total + shift(summed[k // 2], -k)
        fresh = total.astype(jnp.bfloat16).reshape(LAYERS, rec, heads_here, 2, head_size)

        holder, within = block_arrangement(span_lengths, span_holder)
        place = (me - holder[0]) % n
        within = within[0]
        all_pages = jnp.stack(pages, axis=1)
        united_list, squares_list, base_list = [], [], []
        for layer in range(LAYERS):
            cached = all_pages[layer][place, within]
            span_offsets = rec_pos[layer] - me * PROMPT_PER_HOLD
            old = cached[span_offsets].astype(jnp.float32)
            diff = fresh[layer].astype(jnp.float32) - old
            squares_list.append(jnp.sum(diff * diff, axis=(1, 2, 3)))
            base_list.append(jnp.sum(old * old, axis=(1, 2, 3)))
            united_list.append(cached.at[span_offsets].set(fresh[layer]))
        sums = lax.psum(jnp.stack(squares_list + base_list), "tp")
        entries = KVH * 2 * head_size
        deviation = sums[:LAYERS] / entries / (sums[LAYERS:] / entries + 1e-06)
        return (jnp.stack(united_list), deviation)

    return local


def solution(mesh):
    return jax.shard_map(
        make_local(mesh.shape["hold"], mesh.shape["tp"]),
        mesh=mesh,
        in_specs=(
            P(None, ("groups", "hold"), None, "tp", None, None),
            P(("groups", "hold"), None),
            P(("groups", "hold"), None),
            P(None, ("groups", "hold")),
            P(None, ("groups", "hold"), None),
            P(),
            P(None, "hold", "tp", None, None),
        ),
        out_specs=(P(None, ("groups", "hold"), "tp", None, None), P(None, ("groups", "hold"))),
        check_vma=False,
    )
```

time: 544 us -> 142 us (0.26)
  waiting for transfers between devices: 417 us -> 29.5 us
  local copies, waits for them, and re-layouts: 65.8 us -> 34.5 us
  starting transfers between devices: 10.2 us -> 28.1 us
  other arithmetic: 13.6 us -> 23.1 us
  matrix products: 15.3 us -> 5.88 us
    all_gather x2 -> x1, waiting for transfers between devices: 329 us -> 0.02 us  [local(): gathered = lax.all_gather(stacked, 'tp', axis=1, tiled=True)]
    all_to_all x2 -> x0, waiting for transfers between devices: 87.2 us -> none  [local(): lax.all_to_all(cache_store[layer], 'hold', split_axis=0, concat_axis=0, t...]
    ppermute x0 -> x8, waiting for transfers between devices: none -> 29.5 us  [the longest x7 19.6 us: shift(): return lax.ppermute(value, 'hold', [(i, (i + k) % n) for i in range(n)])]
    reshape x4 -> x1, local copies, waits for them, and re-layouts: 38.6 us -> 10.2 us  [local(): weight = kv_weight.reshape(LAYERS, feats, cols)]
    ppermute x0 -> x8, starting transfers between devices: none -> 28.1 us  [the longest x7 26.8 us: shift(): return lax.ppermute(value, 'hold', [(i, (i + k) % n) for i in range(n)])]
    all_to_all x2 -> x0, starting transfers between devices: 10.1 us -> none  [local(): lax.all_to_all(cache_store[layer], 'hold', split_axis=0, concat_axis=0, t...]
    dot_general x2 -> x1, matrix products: 15.3 us -> 5.88 us  [local(): jnp.einsum('klrf,lfc->klrc', rows, weight, preferred_element_type=jnp.flo...]
    unnamed x11 -> x10, local copies, waits for them, and re-layouts: 9.28 us -> 0.02 us
  transfers between devices with their start and end apart: 4 -> 9, of which waited for: 4 -> 6; matrix products, arithmetic and copies ran while one was open for 10% -> 34% of each run, Pallas kernels for 0% -> 0%
where the time goes in v1:
time: 142 us
  local copies, waits for them, and re-layouts  34.5 us (24%)
  waiting for transfers between devices  29.5 us (21%)
  starting transfers between devices  28.1 us (20%)
  other arithmetic  23.1 us (16%)
  between operations  14.4 us (10%)
  blocking collectives  6.21 us (4%)
  matrix products  5.88 us (4%)
    ppermute x7, starting transfers between devices, shift(): return lax.ppermute(value, 'hold', [(i, (i + k) % n) for i in range(n)])  26.8 us
    ppermute x7, waiting for transfers between devices, shift(): return lax.ppermute(value, 'hold', [(i, (i + k) % n) for i in range(n)])  19.6 us
    reshape x1, local copies, waits for them, and re-layouts, local(): weight = kv_weight.reshape(LAYERS, feats, cols)  10.2 us
    ppermute x1, waiting for transfers between devices, local(): summed = partial[0::2] + lax.ppermute(odd, 'hold', pairs)  9.83 us
    gather x2, local copies, waits for them, and re-layouts, local(): cached = all_pages[layer][place, within]  7.75 us
    psum x1, blocking collectives, local(): sums = lax.psum(jnp.stack(squares_list + base_list), 'tp')  6.21 us
    scatter x2, local copies, waits for them, and re-layouts, local(): united_list.append(cached.at[span_offsets].set(fresh[layer]))  6.04 us
    dot_general x1, matrix products, local(): jnp.einsum('klrf,lfc->klrc', rows, weight, preferred_element_type=jnp.flo...  5.88 us
  transfers between devices with their start and end apart: 9, of which 6 were waited for; matrix products, arithmetic and copies ran while one was open for 34% of the time, Pallas kernels for 0%

profile of v1, /device:TPU:0, one launch (start us, length us, event | category | flops | bytes accessed | tf_op | source)
XLA Modules:
  0.0 141.6 jit_solution(4122499842655888494)
XLA Ops:
  10.0 1.7 %fusion.7 = bf16[40,12288]{1,0:T(8,128)(2,1)S(1)} fusion(bf16[40,12288]{1,0:T(8,128)(2,1)S(1)} %gather_fusion.1, f32[40]{0:T(128)S(1)} %add_rsqrt_fusion.1, bf16[160,12288]{1,0:T(8,128)(2,1)} %bitcast.72, s32[]{:T(128)S(6)} %select_n.160), kind=kLoop, calls=%fused_computation.18 | loop fusion | flops 2457600 | bytes 2949284 | tf_op jit(solution)/shard_map/convert_element_type | solution.py:25
  11.8 3.1 %collective-permute-start.3 = (bf16[40,3072]{1,0:T(8,128)(2,1)S(1)}, bf16[40,3072]{1,0:T(8,128)(2,1)S(1)}, u32[]{:S(2)}, u32[]{:S(2)}) collective-permute-start(bf16[40,3072]{1,0:T(8,128)(2,1)S(1)} %get-tuple-element.11), channel_id=1, source_target_pairs={{0,4},{4,8},{8,12},{12,0},{1,5},{5,9},{9,13},{13,1},{2,6},{6,10},{... | collective-permute-start | bytes 737288 | tf_op jit(solution)/shard_map/ppermute | solution.py:30
  14.9 2.6 %collective-permute-start.4 = (bf16[40,3072]{1,0:T(8,128)(2,1)S(1)}, bf16[40,3072]{1,0:T(8,128)(2,1)S(1)}, u32[]{:S(2)}, u32[]{:S(2)}) collective-permute-start(bf16[40,3072]{1,0:T(8,128)(2,1)S(1)} %get-tuple-element.13), channel_id=1, source_target_pairs={{0,8},{4,12},{8,0},{12,4},{1,9},{5,13},{9,1},{13,5},{2,10},{6,14},... | collective-permute-start | bytes 737288 | tf_op jit(solution)/shard_map/ppermute | solution.py:30
  18.8 5.0 %collective-permute-done.3 = bf16[40,3072]{1,0:T(8,128)(2,1)S(1)} collective-permute-done((bf16[40,3072]{1,0:T(8,128)(2,1)S(1)}, bf16[40,3072]{1,0:T(8,128)(2,1)S(1)}, u32[]{:S(2)}, u32[]{:S(2)}) %collective-permute-start.3) | collective-permute-done | bytes 245792 | tf_op jit(solution)/shard_map/ppermute | solution.py:30
  23.8 9.7 %collective-permute-done.4 = bf16[40,3072]{1,0:T(8,128)(2,1)S(1)} collective-permute-done((bf16[40,3072]{1,0:T(8,128)(2,1)S(1)}, bf16[40,3072]{1,0:T(8,128)(2,1)S(1)}, u32[]{:S(2)}, u32[]{:S(2)}) %collective-permute-start.4) | collective-permute-done | bytes 245792 | tf_op jit(solution)/shard_map/ppermute | solution.py:30
  34.5 2.4 %constant_dynamic-slice_fusion.3 = (bf16[2,1,256,2,2,128]{5,4,3,2,1,0:T(2,128)(2,1)S(1)}, bf16[2,256,2,2,128]{4,3,2,1,0:T(2,128)(2,1)}, bf16[2,256,2,2,128]{4,3,2,1,0:T(2,128)(2,1)}, bf16[2,256,2,2,128]{4,3,2,1,0:T(2,128)(2,1)}) fusion(bf16[2,4,256,2,2,128]{5,4,3,2,1,0:T(2,128)(2,1)S(1)} %copy-done.1, s32[]{:T(128)S(6)} %select_n.148, s32[]{:T(128)S(6)} %select_n.150, ...), kind=kLoop, calls=%fused_computation.63 | loop fusion | bytes 4194320 | tf_op jit(solution)/shard_map/jit(dynamic_index_in_dim)/dynamic_slice | solution.py:53
  36.9 5.7 %collective-permute-start = (bf16[2,256,2,2,128]{4,3,2,1,0:T(2,128)(2,1)}, bf16[2,256,2,2,128]{4,3,2,1,0:T(2,128)(2,1)S(1)}, u32[]{:S(2)}, u32[]{:S(2)}) collective-permute-start(bf16[2,256,2,2,128]{4,3,2,1,0:T(2,128)(2,1)} %get-tuple-element.8), channel_id=1, source_target_pairs={{0,4},{4,8},{8,12},{12,0},{1,5},{5,9},{9,13},{13,1},{2,6},{6,10},{... | collective-permute-start | bytes 1572872 | tf_op jit(solution)/shard_map/ppermute | solution.py:30
  42.7 1.6 %collective-permute-start.1 = (bf16[2,256,2,2,128]{4,3,2,1,0:T(2,128)(2,1)}, bf16[2,256,2,2,128]{4,3,2,1,0:T(2,128)(2,1)S(1)}, u32[]{:S(2)}, u32[]{:S(2)}) collective-permute-start(bf16[2,256,2,2,128]{4,3,2,1,0:T(2,128)(2,1)} %get-tuple-element.10), channel_id=1, source_target_pairs={{0,8},{4,12},{8,0},{12,4},{1,9},{5,13},{9,1},{13,5},{2,10},{6,14},... | collective-permute-start | bytes 1572872 | tf_op jit(solution)/shard_map/ppermute | solution.py:30
  45.0 3.3 %multiply_reduce_fusion = f32[2,80]{1,0:T(2,128)S(1)} fusion(bf16[2,80,12288]{2,1,0:T(8,128)(2,1)} %param.13), kind=kLoop, calls=%fused_computation.7 | loop fusion | flops 5898080 | bytes 3932800 | tf_op jit(solution)/shard_map/reduce_sum | solution.py:24
  48.4 10.2 %reshape.449 = bf16[2,3072,512,1]{2,1,0,3:T(8,128)(2,1)} reshape(bf16[2,3072,2,2,128]{4,3,2,1,0:T(2,128)(2,1)} %param.15) | data formatting | bytes 12582912 | tf_op jit(solution)/shard_map/reshape | solution.py:60
  60.2 5.1 %fusion.22 = s32[512,1]{0,1:T(1,128)S(1)} fusion(s32[1,512]{1,0:T(1,128)S(1)} %bitcast.84, s32[]{:T(128)} %bitcast.17, s32[]{:T(128)} %bitcast.16, s32[]{:T(128)} %bitcast.15, s32[]{:T(128)} %bitcast.14, s32[]{:T(128)} %bitcast.12, s32[]{:T(128)} %bitcast.11, s32[]{:T(128)} %bitcast.10, s32[]{:T(128)} %bitcast.9, s32[]{:T(128)S(6)} %axis_index.23), kind=kLoop, calls=%fused_computation.70 | loop fusion | flops 20992 | bytes 4132 | tf_op jit(solution)/shard_map/concatenate | solution.py:82
  67.7 5.9 %fusion.9 = f32[4,2,80,512]{3,2,0,1:T(8,128)S(1)} fusion(bf16[2,3072,512,1]{2,1,0,3:T(8,128)(2,1)} %reshape.449, bf16[1,2,80,3072]{3,2,0,1:T(8,128)(2,1)S(1)} %bitcast.76, bf16[3,2,80,3072]{3,2,1,0:T(8,128)(2,1)} %bitcast.89), kind=kOutput, calls=%fused_computation.21 | convolution fusion | flops 2021130240 | bytes 11534336 | tf_op jit(solution)/shard_map/klrf,lfc->klrc/dot_general | solution.py:64
  75.1 2.5 %collective-permute-done.1 = bf16[2,256,2,2,128]{4,3,2,1,0:T(2,128)(2,1)S(1)} collective-permute-done((bf16[2,256,2,2,128]{4,3,2,1,0:T(2,128)(2,1)}, bf16[2,256,2,2,128]{4,3,2,1,0:T(2,128)(2,1)S(1)}, u32[]{:S(2)}, u32[]{:S(2)}) %collective-permute-start.1) | collective-permute-done | bytes 524320 | tf_op jit(solution)/shard_map/ppermute | solution.py:30
  77.8 3.9 %pad_maximum_fusion = bf16[2,4,256,2,2,128]{5,4,3,2,1,0:T(2,128)(2,1)S(1)} fusion(bf16[2,1,256,2,2,128]{5,4,3,2,1,0:T(2,128)(2,1)S(1)} %bitcast.79, bf16[2,1,256,2,2,128]{5,4,3,2,1,0:T(2,128)(2,1)S(1)} %bitcast.78, bf16[2,1,256,2,2,128]{5,4,3,2,1,0:T(2,128)(2,1)S(1)} %bitcast.77, bf16[2,1,256,2,2,128]{5,4,3,2,1,0:T(2,128)(2,1)S(1)} %get-tuple-element.7), kind=kLoop, calls=%fused_computation.15 | loop fusion | flops 3145728 | bytes 4194304 | tf_op jit(solution)/shard_map/stack | solution.py:79
  81.7 9.8 %collective-permute-done.6 = f32[2,2,80,512]{3,2,0,1:T(8,128)S(1)} collective-permute-done((f32[2,2,80,512]{3,2,0,1:T(8,128)S(1)}, f32[2,2,80,512]{3,2,0,1:T(8,128)S(1)}, u32[]{:S(2)}, u32[]{:S(2)}) %collective-permute-start.6) | collective-permute-done | bytes 655392 | tf_op jit(solution)/shard_map/ppermute | solution.py:70
  92.4 11.7 %collective-permute-start.7 = (f32[2,80,512]{2,1,0:T(8,128)}, f32[2,80,512]{2,1,0:T(8,128)S(1)}, u32[]{:S(2)}, u32[]{:S(2)}) collective-permute-start(f32[2,80,512]{2,1,0:T(8,128)} %slice_bitcast_fusion.2), channel_id=1, source_target_pairs={{0,8},{4,12},{8,0},{12,4},{1,9},{5,13},{9,1},{13,5},{2,10},{6,14},... | collective-permute-start | bytes 983048 | tf_op jit(solution)/shard_map/ppermute | solution.py:30
  104.0 2.2 %slice_bitcast_fusion.1 = (bf16[4,256,2,2,128]{4,3,2,1,0:T(2,128)(2,1)S(1)}, bf16[4,256,2,2,128]{4,3,2,1,0:T(2,128)(2,1)}) fusion(bf16[2,4,256,2,2,128]{5,4,3,2,1,0:T(2,128)(2,1)S(1)} %pad_maximum_fusion), kind=kLoop, calls=%fused_computation.23 | loop fusion | bytes 4194304 | tf_op jit(solution)/shard_map/squeeze | solution.py:82
  106.3 4.5 %gather_fusion.2 = bf16[512,2,2,128]{3,2,1,0:T(2,128)(2,1)S(1)} fusion(bf16[4,256,2,2,128]{4,3,2,1,0:T(2,128)(2,1)} %get-tuple-element.6, s32[512]{0:T(512)S(1)} %bitcast.68), kind=kCustom, calls=%fused_computation.2 | custom fusion | bytes 1052672 | tf_op jit(solution)/shard_map/gather | solution.py:82
  111.6 3.3 %gather_fusion = bf16[512,2,2,128]{3,2,1,0:T(2,128)(2,1)S(1)} fusion(bf16[4,256,2,2,128]{4,3,2,1,0:T(2,128)(2,1)S(1)} %get-tuple-element.5, s32[512]{0:T(512)S(1)} %bitcast.69), kind=kCustom, calls=%fused_computation | custom fusion | bytes 1052672 | tf_op jit(solution)/shard_map/gather | solution.py:82
  117.0 2.2 %collective-permute-done.7 = f32[2,80,512]{2,1,0:T(8,128)S(1)} collective-permute-done((f32[2,80,512]{2,1,0:T(8,128)}, f32[2,80,512]{2,1,0:T(8,128)S(1)}, u32[]{:S(2)}, u32[]{:S(2)}) %collective-permute-start.7) | collective-permute-done | bytes 327712 | tf_op jit(solution)/shard_map/ppermute | solution.py:30
  119.4 6.2 %psum.7 = f32[4,80]{1,0:T(4,128)S(1)} all-reduce(f32[4,80]{1,0:T(4,128)S(1)} %pad_maximum_fusion.3), channel_id=1, replica_groups=mesh['groups'=2,'hold'=4,'tp'=4] {'tp'}, use_global_device_ids=true, to_apply=%region_10.12 | all-reduce | flops 320 | bytes 2560 | tf_op jit(solution)/shard_map/psum | solution.py:89
  126.2 3.0 %scatter_fusion = bf16[512,2,2,128]{3,2,1,0:T(2,128)(2,1)S(1)} fusion(bf16[512,2,2,128]{3,2,1,0:T(2,128)(2,1)S(1)} %gather_fusion, s32[80]{0:T(128)S(1)} %get-tuple-element.18, bf16[80,2,2,128]{3,2,1,0:T(2,128)(2,1)S(1)} %reshape.375), kind=kCustom, calls=%fused_computation.5 | custom fusion | bytes 246080 | tf_op jit(solution)/shard_map/scatter | solution.py:88
  129.3 3.0 %scatter_fusion.1 = bf16[512,2,2,128]{3,2,1,0:T(2,128)(2,1)S(1)} fusion(bf16[512,2,2,128]{3,2,1,0:T(2,128)(2,1)S(1)} %gather_fusion.2, s32[80]{0:T(128)S(1)} %get-tuple-element.19, bf16[80,2,2,128]{3,2,1,0:T(2,128)(2,1)S(1)} %reshape.383), kind=kCustom, calls=%fused_computation.6 | custom fusion | bytes 246080 | tf_op jit(solution)/shard_map/scatter | solution.py:88
  132.3 2.5 %pad_maximum_fusion.1 = bf16[2,512,2,2,128]{4,3,2,1,0:T(2,128)(2,1)} fusion(bf16[1,512,2,2,128]{4,3,2,1,0:T(2,128)(2,1)S(1)} %bitcast.74, bf16[1,512,2,2,128]{4,3,2,1,0:T(2,128)(2,1)S(1)} %bitcast.75), kind=kLoop, calls=%fused_computation.24 | loop fusion | flops 524288 | bytes 2097152 | tf_op jit(solution)/shard_map/stack | solution.py:92
  (56 shorter events, 16.2 us)
Async XLA Ops:
  7.2 1.7 %copy-start = (bf16[2,12288]{1,0:T(2,128)(2,1)S(1)}, bf16[2,12288]{1,0:T(2,128)(2,1)}, u32[]{:S(2)}) copy-start(bf16[2,12288]{1,0:T(2,128)(2,1)} %param.14) | copy-start | bytes 147460
  7.2 60.5 %all-gather.2.cloned.1.call-start = ((), (), s32[]{:S(2)}) async-start(), calls=%async_computation | async-start | bytes 3686400 | tf_op jit(solution)/shard_map/all_gather | solution.py:62
  10.0 24.5 %copy-start.1 = (bf16[2,4,256,2,2,128]{5,4,3,2,1,0:T(2,128)(2,1)S(1)}, bf16[2,4,256,2,2,128]{5,4,3,2,1,0:T(2,128)(2,1)}, u32[]{:S(2)}) copy-start(bf16[2,4,256,2,2,128]{5,4,3,2,1,0:T(2,128)(2,1)} %param.9) | copy-start | bytes 6291460
  11.8 12.0 %collective-permute-start.3 = (bf16[40,3072]{1,0:T(8,128)(2,1)S(1)}, bf16[40,3072]{1,0:T(8,128)(2,1)S(1)}, u32[]{:S(2)}, u32[]{:S(2)}) collective-permute-start(bf16[40,3072]{1,0:T(8,128)(2,1)S(1)} %get-tuple-element.11), channel_id=1, source_target_pairs={{0,4},{4,8},{8,12},{12,0},{1,5},{5,9},{9,13},{13,1},{2,6},{6,10},{... | collective-permute-start | bytes 737288 | tf_op jit(solution)/shard_map/ppermute | solution.py:30
  14.9 18.6 %collective-permute-start.4 = (bf16[40,3072]{1,0:T(8,128)(2,1)S(1)}, bf16[40,3072]{1,0:T(8,128)(2,1)S(1)}, u32[]{:S(2)}, u32[]{:S(2)}) collective-permute-start(bf16[40,3072]{1,0:T(8,128)(2,1)S(1)} %get-tuple-element.13), channel_id=1, source_target_pairs={{0,8},{4,12},{8,0},{12,4},{1,9},{5,13},{9,1},{13,5},{2,10},{6,14},... | collective-permute-start | bytes 737288 | tf_op jit(solution)/shard_map/ppermute | solution.py:30
  17.5 16.1 %collective-permute-start.5 = (bf16[40,3072]{1,0:T(8,128)(2,1)S(1)}, bf16[40,3072]{1,0:T(8,128)(2,1)S(1)}, u32[]{:S(2)}, u32[]{:S(2)}) collective-permute-start(bf16[40,3072]{1,0:T(8,128)(2,1)S(1)} %get-tuple-element.12), channel_id=1, source_target_pairs={{0,12},{4,0},{8,4},{12,8},{1,13},{5,1},{9,5},{13,9},{2,14},{6,2},{... | collective-permute-start | bytes 737288 | tf_op jit(solution)/shard_map/ppermute | solution.py:30
  36.9 38.2 %collective-permute-start = (bf16[2,256,2,2,128]{4,3,2,1,0:T(2,128)(2,1)}, bf16[2,256,2,2,128]{4,3,2,1,0:T(2,128)(2,1)S(1)}, u32[]{:S(2)}, u32[]{:S(2)}) collective-permute-start(bf16[2,256,2,2,128]{4,3,2,1,0:T(2,128)(2,1)} %get-tuple-element.8), channel_id=1, source_target_pairs={{0,4},{4,8},{8,12},{12,0},{1,5},{5,9},{9,13},{13,1},{2,6},{6,10},{... | collective-permute-start | bytes 1572872 | tf_op jit(solution)/shard_map/ppermute | solution.py:30
  42.7 34.9 %collective-permute-start.1 = (bf16[2,256,2,2,128]{4,3,2,1,0:T(2,128)(2,1)}, bf16[2,256,2,2,128]{4,3,2,1,0:T(2,128)(2,1)S(1)}, u32[]{:S(2)}, u32[]{:S(2)}) collective-permute-start(bf16[2,256,2,2,128]{4,3,2,1,0:T(2,128)(2,1)} %get-tuple-element.10), channel_id=1, source_target_pairs={{0,8},{4,12},{8,0},{12,4},{1,9},{5,13},{9,1},{13,5},{2,10},{6,14},... | collective-permute-start | bytes 1572872 | tf_op jit(solution)/shard_map/ppermute | solution.py:30
  44.3 33.5 %collective-permute-start.2 = (bf16[2,256,2,2,128]{4,3,2,1,0:T(2,128)(2,1)}, bf16[2,256,2,2,128]{4,3,2,1,0:T(2,128)(2,1)S(1)}, u32[]{:S(2)}, u32[]{:S(2)}) collective-permute-start(bf16[2,256,2,2,128]{4,3,2,1,0:T(2,128)(2,1)} %get-tuple-element.9), channel_id=1, source_target_pairs={{0,12},{4,0},{8,4},{12,8},{1,13},{5,1},{9,5},{13,9},{2,14},{6,2},{... | collective-permute-start | bytes 1572872 | tf_op jit(solution)/shard_map/ppermute | solution.py:30
  48.4 10.2 %copy-start.4 = (s32[1,4]{1,0:T(1,128)S(1)}, s32[1,4]{1,0:T(1,128)}, u32[]{:S(2)}) copy-start(s32[1,4]{1,0:T(1,128)} %param.10) | copy-start | bytes 52
  48.4 10.4 %copy-start.3 = (s32[2,80]{1,0:T(2,128)S(1)}, s32[2,80]{1,0:T(2,128)}, u32[]{:S(2)}) copy-start(s32[2,80]{1,0:T(2,128)} %param.12) | copy-start | bytes 1924
  48.4 11.1 %copy-start.2 = (s32[1,4]{1,0:T(1,128)S(1)}, s32[1,4]{1,0:T(1,128)}, u32[]{:S(2)}) copy-start(s32[1,4]{1,0:T(1,128)} %param.11) | copy-start | bytes 52
  73.8 17.7 %collective-permute-start.6 = (f32[2,2,80,512]{3,2,0,1:T(8,128)S(1)}, f32[2,2,80,512]{3,2,0,1:T(8,128)S(1)}, u32[]{:S(2)}, u32[]{:S(2)}) collective-permute-start(f32[2,2,80,512]{3,2,0,1:T(8,128)S(1)} %maximum_select_fusion), channel_id=1, source_target_pairs={{0,4},{4,0},{8,12},{12,8},{1,5},{5,1},{9,13},{13,9},{2,6},{6,2},{1... | collective-permute-start | bytes 1966088 | tf_op jit(solution)/shard_map/ppermute | solution.py:70
  92.4 26.8 %collective-permute-start.7 = (f32[2,80,512]{2,1,0:T(8,128)}, f32[2,80,512]{2,1,0:T(8,128)S(1)}, u32[]{:S(2)}, u32[]{:S(2)}) collective-permute-start(f32[2,80,512]{2,1,0:T(8,128)} %slice_bitcast_fusion.2), channel_id=1, source_target_pairs={{0,8},{4,12},{8,0},{12,4},{1,9},{5,13},{9,1},{13,5},{2,10},{6,14},... | collective-permute-start | bytes 983048 | tf_op jit(solution)/shard_map/ppermute | solution.py:30
Sparse Core Ops, SparseCore 0:
  34.6 31.8 all-gather.1

commit v2 on v1

v2 whole, which is shorter than its diff:
```python
import functools

import jax
import jax.numpy as jnp
from jax import lax
from jax.experimental import pallas as pl
from jax.experimental.pallas import tpu as pltpu
from jax.sharding import PartitionSpec as P

KVH = 8
PROMPT_PER_HOLD = 512
LAYERS = 2
CHUNK = 8
VMEM_BYTES = 40 * 1024 * 1024
PARAMS = pltpu.CompilerParams(vmem_limit_bytes=VMEM_BYTES)
ANY = pl.BlockSpec(memory_space=pl.ANY)
VMEM = pl.BlockSpec(memory_space=pltpu.VMEM)
SMEM = pl.BlockSpec(memory_space=pltpu.SMEM)


def norm_rows(rows, gain):
    rows = rows.astype(jnp.float32)
    scale = lax.rsqrt(jnp.mean(rows * rows, axis=1, keepdims=True) + 1e-05)
    return (rows * scale * gain.astype(jnp.float32)).astype(jnp.bfloat16)


def norm_kernel(at, rows_ref, gain_ref, *refs):
    outs, held = refs[:-1], refs[-1]
    quarter, feats = outs[0].shape
    rows = rows_ref[0].astype(jnp.float32)
    mine = rows[:quarter]
    for part in range(1, rows.shape[0] // quarter):
        mine = jnp.where(at[1] == part, rows[part * quarter : (part + 1) * quarter], mine)
    gain = jnp.where(at[0] == 0, gain_ref[0:1], gain_ref[1:2])
    held[...] = norm_rows(mine, gain)
    for k, out in enumerate(outs, 1):
        start = pl.multiple_of(at[1 + k], 128)
        out[...] = held[:, pl.ds(start, feats)]


def normed_share(hidden, gain, me, my_tp, n, tps, feats):
    layers, rec, width = hidden.shape
    quarter = layers * rec // tps
    per_layer = rec // quarter
    at = jnp.stack(
        [my_tp // per_layer, my_tp % per_layer] + [((me + k) % n) * feats for k in range(1, n)]
    ).astype(jnp.int32)
    return pl.pallas_call(
        norm_kernel,
        grid_spec=pltpu.PrefetchScalarGridSpec(
            num_scalar_prefetch=1,
            grid=(1,),
            in_specs=[
                pl.BlockSpec((1, rec, width), lambda i, at: (at[0], 0, 0)),
                pl.BlockSpec(gain.shape, lambda i, at: (0, 0)),
            ],
            out_specs=[pl.BlockSpec((quarter, feats), lambda i, at: (0, 0))] * (n - 1),
            scratch_shapes=[pltpu.VMEM((quarter, width), jnp.bfloat16)],
        ),
        out_shape=[jax.ShapeDtypeStruct((quarter, feats), jnp.bfloat16)] * (n - 1),
        compiler_params=PARAMS,
    )(at, hidden, gain)


def pick_kernel(at, store, *refs):
    out, sem = refs[-2:]
    copy = pltpu.make_async_copy(store.at[:, at[0]], out, sem)
    copy.start()
    copy.wait()


def pick(store, at, after):
    shape = store.shape[:1] + store.shape[2:]
    after = () if after is None else (after,)
    return pl.pallas_call(
        pick_kernel,
        grid_spec=pltpu.PrefetchScalarGridSpec(
            num_scalar_prefetch=1,
            grid=(),
            in_specs=[ANY] * (1 + len(after)),
            out_specs=ANY,
            scratch_shapes=[pltpu.SemaphoreType.DMA],
        ),
        out_shape=jax.ShapeDtypeStruct(shape, store.dtype),
        compiler_params=pltpu.CompilerParams(vmem_limit_bytes=1 << 20),
    )(at.astype(jnp.int32).reshape(1), store, *after)


def unite_kernel(n, starts, lengths, spots, *refs):
    pages, fresh, out, sums, held = refs[:n], refs[n], refs[n + 1], refs[n + 2], refs[n + 3]
    layers, rec = fresh.shape[:2]
    for slot, page in enumerate(pages):
        start, length = starts[slot], lengths[slot]
        whole = length // CHUNK

        def many(i, carry, page=page, start=start):
            for layer in range(layers):
                out[layer, pl.ds(start + i * CHUNK, CHUNK)] = page[layer, pl.ds(i * CHUNK, CHUNK)]
            return carry

        def one(i, carry, page=page, start=start):
            for layer in range(layers):
                out[layer, start + i] = page[layer, i]
            return carry

        lax.fori_loop(0, whole, many, 0)
        lax.fori_loop(whole * CHUNK, length, one, 0)
    for layer in range(layers):

        def renew(j, carry, layer=layer):
            at = layer * rec + j
            spot = spots[at]
            old = out[layer, spot].astype(jnp.float32)
            new = fresh[layer, j]
            diff = new.astype(jnp.float32) - old
            held[pl.ds(at, 1), :] = jnp.sum(jnp.sum(diff * diff, axis=0), axis=0, keepdims=True)
            held[pl.ds(layers * rec + at, 1), :] = jnp.sum(
                jnp.sum(old * old, axis=0), axis=0, keepdims=True
            )
            out[layer, spot] = new
            return carry

        lax.fori_loop(0, rec, renew, 0, unroll=4)
    ones = jnp.ones((8, held.shape[1]), jnp.float32)
    both = lax.dot_general(
        ones,
        held[...],
        (((1,), (1,)), ((), ())),
        precision=lax.Precision.HIGHEST,
        preferred_element_type=jnp.float32,
    )
    sums[...] = both[0:1]


def unite(pages, fresh, starts, lengths, spots):
    n = len(pages)
    layers, rec = fresh.shape[:2]
    row = fresh.shape[2:]
    return pl.pallas_call(
        functools.partial(unite_kernel, n),
        in_specs=[SMEM] * 3 + [VMEM] * (n + 1),
        out_specs=[VMEM, VMEM],
        out_shape=[
            jax.ShapeDtypeStruct((layers, PROMPT_PER_HOLD) + row, fresh.dtype),
            jax.ShapeDtypeStruct((1, 2 * layers * rec), jnp.float32),
        ],
        scratch_shapes=[pltpu.VMEM((2 * layers * rec, row[-1]), jnp.float32)],
        compiler_params=PARAMS,
    )(starts, lengths, spots, *pages, fresh)


def make_local(n, tps):
    def shift(value, k):
        return lax.ppermute(value, "hold", [(i, (i + k) % n) for i in range(n)])

    def swap(value, axis, size, bit):
        return lax.ppermute(value, axis, [(i, i ^ bit) for i in range(size)])

    def local(cache_store, span_lengths, span_holder, rec_pos, hidden, norm_gain, kv_weight):
        me = lax.axis_index("hold")
        my_tp = lax.axis_index("tp")
        rec, width = hidden.shape[1:]
        feats = kv_weight.shape[1]
        heads_here, head_size = kv_weight.shape[2], kv_weight.shape[4]
        cols = heads_here * 2 * head_size
        order = sorted(range(1, n), key=lambda k: (k % 2 == 0, min(k, n - k), k))

        pieces = normed_share(hidden, norm_gain, me, my_tp, n, tps, feats)
        arrived = {k: shift(pieces[k - 1], k) for k in order}

        pages = {0: lax.dynamic_index_in_dim(cache_store, me, axis=1, keepdims=False)}
        sent = []
        for i, k in enumerate(order):
            page = pick(cache_store, (me + k) % n, sent[i - 2] if i >= 2 else None)
            pages[k] = shift(page, k)
            sent.append(pages[k])

        own_full = norm_rows(
            hidden.reshape(LAYERS * rec, width), jnp.repeat(norm_gain, rec, axis=0)
        )
        own = lax.dynamic_slice_in_dim(own_full, me * feats, feats, axis=1)
        weight = kv_weight.reshape(LAYERS, feats, cols)

        def everyone(piece):
            shares = [piece]
            bit = tps // 2
            while bit:
                shares = shares + [swap(share, "tp", tps, bit) for share in shares]
                bit //= 2
            masks = [0]
            bit = tps // 2
            while bit:
                masks = masks + [mask ^ bit for mask in masks]
                bit //= 2
            shares = [shares[masks.index(m)] for m in range(tps)]
            bit = 1
            while bit < tps:
                flip = (my_tp & bit) != 0
                shares = [
                    jnp.where(flip, shares[m ^ bit], shares[m]) for m in range(tps)
                ]
                bit *= 2
            return jnp.concatenate(shares)

        def product(rows):
            return jnp.einsum(
                "lrf,lfc->lrc",
                rows.reshape(LAYERS, rec, feats),
                weight,
                preferred_element_type=jnp.float32,
            )

        partial = {k: product(everyone(arrived[k])) for k in order}
        partial[0] = product(own)
        even = me % 2 == 0
        total = None
        for k in list(range(2, n, 2)) + [0]:
            away = jnp.where(even, partial[(k - 1) % n], partial[(k + 1) % n])
            pair = partial[k] + swap(away, "hold", n, 1)
            pair = shift(pair, -k) if k else pair
            total = pair if total is None else total + pair
        fresh = total.astype(jnp.bfloat16).reshape(LAYERS, rec, heads_here, 2, head_size)

        lengths = span_lengths[0]
        starts = jnp.cumsum(lengths) - lengths
        holders = (me - jnp.arange(n, dtype=jnp.int32)) % n
        held_here = span_holder[0][None, :] == holders[:, None]
        slot_starts = jnp.sum(jnp.where(held_here, starts[None, :], 0), axis=1)
        slot_lengths = jnp.sum(jnp.where(held_here, lengths[None, :], 0), axis=1)
        spots = (rec_pos - me * PROMPT_PER_HOLD).reshape(-1)
        united, sums = unite(
            [pages[k] for k in range(n)], fresh, slot_starts, slot_lengths, spots
        )
        sums = lax.psum(sums, "tp").reshape(2, LAYERS, rec)
        entries = KVH * 2 * head_size
        deviation = sums[0] / entries / (sums[1] / entries + 1e-06)
        return (united, deviation)

    return local


def solution(mesh):
    return jax.shard_map(
        make_local(mesh.shape["hold"], mesh.shape["tp"]),
        mesh=mesh,
        in_specs=(
            P(None, ("groups", "hold"), None, "tp", None, None),
            P(("groups", "hold"), None),
            P(("groups", "hold"), None),
            P(None, ("groups", "hold")),
            P(None, ("groups", "hold"), None),
            P(),
            P(None, "hold", "tp", None, None),
        ),
        out_specs=(P(None, ("groups", "hold"), "tp", None, None), P(None, ("groups", "hold"))),
        check_vma=False,
    )
```

time: 142 us -> 130 us (0.915)
  waiting for transfers between devices: 29.5 us -> 53.6 us
  local copies, waits for them, and re-layouts: 34.5 us -> 15.7 us
  between operations: 14.4 us -> 0.92 us
  other arithmetic: 23.1 us -> 13.6 us
  Pallas kernels: 0 us -> 7.04 us
  starting transfers between devices: 28.1 us -> 24.5 us
  matrix products: 5.88 us -> 7.75 us
    ppermute x1 -> x11, waiting for transfers between devices: 9.83 us -> 24.6 us  [swap(): return lax.ppermute(value, axis, [(i, i ^ bit) for i in range(size)])]
    gather x7 -> x0, local copies, waits for them, and re-layouts: 11.6 us -> none  [the longest x2 7.75 us: local(): cached = all_pages[layer][place, within]]
    ppermute x7, waiting for transfers between devices: 19.6 us -> 29 us  [shift(): return lax.ppermute(value, 'hold', [(i, (i + k) % n) for i in range(n)])]
    ppermute x7, starting transfers between devices: 26.8 us -> 17.7 us  [shift(): return lax.ppermute(value, 'hold', [(i, (i + k) % n) for i in range(n)])]
    another operation x5 -> x1, other arithmetic: 7.5 us -> 0.18 us  [the longest x1 3.87 us: local(): all_pages = jnp.stack(pages, axis=1)]
    pallas_call x0 -> x5, Pallas kernels: none -> 7.04 us  [the longest x1 3.16 us: unite(): pl.pallas_call(functools.partial(unite_kernel, n), in_specs=[SMEM] * 3 +...]
    convert_element_type x0 -> x1, other arithmetic: none -> 6.27 us  [norm_rows(): rows = rows.astype(jnp.float32)]
    scatter x2 -> x0, local copies, waits for them, and re-layouts: 6.04 us -> none  [local(): united_list.append(cached.at[span_offsets].set(fresh[layer]))]
  transfers between devices with their start and end apart: 9 -> 18, of which waited for: 6 -> 3; matrix products, arithmetic and copies ran while one was open for 34% -> 25% of each run, Pallas kernels for 0% -> 1%
where the time goes in v2:
time: 130 us
  waiting for transfers between devices  53.6 us (41%)
  starting transfers between devices  24.5 us (19%)
  local copies, waits for them, and re-layouts  15.7 us (12%)
  other arithmetic  13.6 us (10%)
  matrix products  7.75 us (6%)
  Pallas kernels  7.04 us (5%)
  blocking collectives  6.83 us (5%)
    ppermute x7, waiting for transfers between devices, shift(): return lax.ppermute(value, 'hold', [(i, (i + k) % n) for i in range(n)])  29 us
    ppermute x11, waiting for transfers between devices, swap(): return lax.ppermute(value, axis, [(i, i ^ bit) for i in range(size)])  24.6 us
    ppermute x7, starting transfers between devices, shift(): return lax.ppermute(value, 'hold', [(i, (i + k) % n) for i in range(n)])  17.7 us
    reshape x1, local copies, waits for them, and re-layouts, local(): weight = kv_weight.reshape(LAYERS, feats, cols)  10.2 us
    dot_general x4, matrix products, product(): jnp.einsum('lrf,lfc->lrc', rows.reshape(LAYERS, rec, feats), weight, pref...  7.75 us
    psum x1, blocking collectives, local(): sums = lax.psum(sums, 'tp').reshape(2, LAYERS, rec)  6.83 us
    ppermute x11, starting transfers between devices, swap(): return lax.ppermute(value, axis, [(i, i ^ bit) for i in range(size)])  6.76 us
    convert_element_type x1, other arithmetic, norm_rows(): rows = rows.astype(jnp.float32)  6.27 us
  transfers between devices with their start and end apart: 18, of which 3 were waited for; matrix products, arithmetic and copies ran while one was open for 25% of the time, Pallas kernels for 1%

profile of v2, /device:TPU:0, one launch (start us, length us, event | category | flops | bytes accessed | tf_op | source)
XLA Modules:
  0.0 129.9 jit_solution(43876460509742677)
XLA Ops:
  0.8 2.1 %copy-done = bf16[2,80,12288]{2,1,0:T(8,128)(2,1)S(1)} copy-done((bf16[2,80,12288]{2,1,0:T(8,128)(2,1)S(1)}, bf16[2,80,12288]{2,1,0:T(8,128)(2,1)}, u32[]{:S(2)}) %copy-start) | copy-done | bytes 3932184
  3.7 2.2 %shard_map.89 = (bf16[40,3072]{1,0:T(8,128)(2,1)}, bf16[40,3072]{1,0:T(8,128)(2,1)S(1)}, bf16[40,3072]{1,0:T(8,128)(2,1)}) custom-call(s32[5]{0:T(128)S(1)} %stack.23.at, bf16[2,80,12288]{2,1,0:T(8,128)(2,1)S(1)} %copy-done, bf16[2,12288]{1,0:T(2,128)(2,1)S(1)} %copy-done.3), custom_call_target="tpu_custom_call" | custom-call | tf_op jit(solution)/shard_map/pallas_call | solution.py:48
  5.9 5.0 %collective-permute-start.11 = (bf16[40,3072]{1,0:T(8,128)(2,1)}, bf16[40,3072]{1,0:T(8,128)(2,1)}, u32[]{:S(2)}, u32[]{:S(2)}) collective-permute-start(bf16[40,3072]{1,0:T(8,128)(2,1)} %get-tuple-element.9), channel_id=1, source_target_pairs={{0,12},{4,0},{8,4},{12,8},{1,13},{5,1},{9,5},{13,9},{2,14},{6,2},{... | collective-permute-start | bytes 737288 | tf_op jit(solution)/shard_map/ppermute | solution.py:154
  10.9 1.0 collective-permute-start.3
  12.0 3.4 %collective-permute-start = (bf16[2,256,2,2,128]{4,3,2,1,0:T(2,128)(2,1)S(1)}, bf16[2,256,2,2,128]{4,3,2,1,0:T(2,128)(2,1)S(1)}, u32[]{:S(2)}, u32[]{:S(2)}) collective-permute-start(bf16[2,256,2,2,128]{4,3,2,1,0:T(2,128)(2,1)S(1)} %shard_map.86), channel_id=1, source_target_pairs={{0,4},{4,8},{8,12},{12,0},{1,5},{5,9},{9,13},{13,1},{2,6},{6,10},{... | collective-permute-start | bytes 1572872 | tf_op jit(solution)/shard_map/ppermute | solution.py:154
  15.4 6.3 %bitcast_convert_fusion = f32[160,12288]{1,0:T(8,128)} fusion(bf16[2,80,12288]{2,1,0:T(8,128)(2,1)} %rows_ref.1), kind=kLoop, calls=%fused_computation.53 | loop fusion | flops 1966080 | bytes 11796480 | tf_op jit(solution)/shard_map/convert_element_type | solution.py:22
  21.7 0.9 multiply_reduce_fusion
  23.5 2.8 %fusion = bf16[160,3072]{1,0:T(8,128)(2,1)} fusion(f32[160,12288]{1,0:T(8,128)S(1)} %bitcast.36, s32[]{:T(128)S(6)} %select_n.209, f32[160,12288]{1,0:T(8,128)} %bitcast_convert_fusion, f32[160]{0:T(256)S(1)} %rsqrt.12), kind=kLoop, calls=%fused_computation.2 | loop fusion | flops 1474560 | bytes 4915844 | tf_op jit(solution)/shard_map/convert_element_type | solution.py:24
  26.6 1.5 %collective-permute-start.12 = (bf16[40,3072]{1,0:T(8,128)(2,1)}, bf16[40,3072]{1,0:T(8,128)(2,1)}, u32[]{:S(2)}, u32[]{:S(2)}) collective-permute-start(bf16[40,3072]{1,0:T(8,128)(2,1)} %collective-permute-done.11), channel_id=1, source_target_pairs={{0,2},{1,3},{2,0},{3,1},{4,6},{5,7},{6,4},{7,5},{8,10},{9,11},{10,... | collective-permute-start | bytes 737288 | tf_op jit(solution)/shard_map/ppermute | solution.py:157
  28.7 14.7 %collective-permute-done.3 = bf16[40,3072]{1,0:T(8,128)(2,1)} collective-permute-done((bf16[40,3072]{1,0:T(8,128)(2,1)S(1)}, bf16[40,3072]{1,0:T(8,128)(2,1)}, u32[]{:S(2)}, u32[]{:S(2)}) %collective-permute-start.3) | collective-permute-done | bytes 245792 | tf_op jit(solution)/shard_map/ppermute | solution.py:154
  43.4 1.5 %collective-permute-start.4 = (bf16[40,3072]{1,0:T(8,128)(2,1)}, bf16[40,3072]{1,0:T(8,128)(2,1)}, u32[]{:S(2)}, u32[]{:S(2)}) collective-permute-start(bf16[40,3072]{1,0:T(8,128)(2,1)} %collective-permute-done.3), channel_id=1, source_target_pairs={{0,2},{1,3},{2,0},{3,1},{4,6},{5,7},{6,4},{7,5},{8,10},{9,11},{10,... | collective-permute-start | bytes 737288 | tf_op jit(solution)/shard_map/ppermute | solution.py:157
  45.4 10.2 %reshape.94 = bf16[2,3072,512]{2,1,0:T(8,128)(2,1)} reshape(bf16[2,3072,2,2,128]{4,3,2,1,0:T(2,128)(2,1)} %param.13) | data formatting | bytes 12582912 | tf_op jit(solution)/shard_map/reshape | solution.py:182
  58.6 8.1 %collective-permute-start.1 = (bf16[2,256,2,2,128]{4,3,2,1,0:T(2,128)(2,1)}, bf16[2,256,2,2,128]{4,3,2,1,0:T(2,128)(2,1)S(1)}, u32[]{:S(2)}, u32[]{:S(2)}) collective-permute-start(bf16[2,256,2,2,128]{4,3,2,1,0:T(2,128)(2,1)} %shard_map.87), channel_id=1, source_target_pairs={{0,8},{4,12},{8,0},{12,4},{1,9},{5,13},{9,1},{13,5},{2,10},{6,14},... | collective-permute-start | bytes 1572872 | tf_op jit(solution)/shard_map/ppermute | solution.py:154
  66.7 1.7 %broadcast_select_fusion.15 = (bf16[40,3072]{1,0:T(8,128)(2,1)S(1)}, bf16[40,3072]{1,0:T(8,128)(2,1)S(1)}, bf16[40,3072]{1,0:T(8,128)(2,1)S(1)}, bf16[40,3072]{1...) fusion(pred[]{:T(512)S(6)} %ne.64, ...), kind=kLoop, calls=%fused_computation.26 | loop fusion | flops 1966080 | bytes 3932162 | tf_op jit(solution)/shard_map/jit(_where)/select_n | solution.py:200
  68.5 4.1 %fusion.7 = f32[2,80,512]{2,1,0:T(8,128)S(1)} fusion(bf16[2,80,3072]{2,1,0:T(8,128)(2,1)S(1)} %bitcast.34, bf16[2,3072,512]{2,1,0:T(8,128)(2,1)} %reshape.94), kind=kOutput, calls=%fused_computation.54 | convolution fusion | flops 503316480 | bytes 7602176 | tf_op jit(solution)/shard_map/lrf,lfc->lrc/dot_general | solution.py:206
  73.1 1.2 broadcast_select_fusion.24
  74.4 2.0 %collective-permute-start.15 = (f32[2,80,512]{2,1,0:T(8,128)S(1)}, f32[2,80,512]{2,1,0:T(8,128)S(1)}, u32[]{:S(2)}, u32[]{:S(2)}) collective-permute-start(f32[2,80,512]{2,1,0:T(8,128)S(1)} %get-tuple-element.27), channel_id=1, source_target_pairs={{0,4},{4,0},{8,12},{12,8},{1,5},{5,1},{9,13},{13,9},{2,6},{6,2},{1... | collective-permute-start | bytes 983048 | tf_op jit(solution)/shard_map/ppermute | solution.py:157
  76.4 1.1 broadcast_select_fusion.23
  77.7 24.6 %collective-permute-done.15 = f32[2,80,512]{2,1,0:T(8,128)S(1)} collective-permute-done((f32[2,80,512]{2,1,0:T(8,128)S(1)}, f32[2,80,512]{2,1,0:T(8,128)S(1)}, u32[]{:S(2)}, u32[]{:S(2)}) %collective-permute-start.15) | collective-permute-done | bytes 327712 | tf_op jit(solution)/shard_map/ppermute | solution.py:157
  102.3 1.2 convolution_add_fusion.1
  103.6 1.2 convolution_add_fusion
  104.8 14.3 %collective-permute-done.16 = f32[2,80,512]{2,1,0:T(8,128)S(1)} collective-permute-done((f32[2,80,512]{2,1,0:T(8,128)S(1)}, f32[2,80,512]{2,1,0:T(8,128)S(1)}, u32[]{:S(2)}, u32[]{:S(2)}) %collective-permute-start.16) | collective-permute-done | bytes 327712 | tf_op jit(solution)/shard_map/ppermute | solution.py:154
  119.2 3.2 %shard_map.90 = (bf16[2,512,2,2,128]{4,3,2,1,0:T(2,128)(2,1)}, f32[1,320]{1,0:T(1,128)S(1)}) custom-call(s32[4]{0:T(128)S(1)} %get-tuple-element.13.starts, s32[4]{0:T(128)S(1)} %get-tuple-element.12.lengths, s32[160]{0:T(256)S(1)} %reshape.89.spots, bf16[2,256,2,2,128]{4,3,2,1,0:T(2,128)(2,1)S(1)} %dynamic-slice_bitcast_fusion.refs_0_, ...), custom_call_target="tpu_custom_call" | custom-call | tf_op jit(solution)/shard_map/pallas_call | solution.py:139
  122.3 6.8 %psum.7 = f32[1,320]{1,0:T(1,128)S(1)} all-reduce(f32[1,320]{1,0:T(1,128)S(1)} %get-tuple-element.11), channel_id=1, replica_groups=mesh['groups'=2,'hold'=4,'tp'=4] {'tp'}, use_global_device_ids=true, to_apply=%region_4.5 | all-reduce | flops 320 | bytes 2560 | tf_op jit(solution)/shard_map/psum | solution.py:234
  (69 shorter events, 7.7 us)
Async XLA Ops:
  3.7 8.3 %copy-start.2 = (bf16[2,4,256,2,2,128]{5,4,3,2,1,0:T(2,128)(2,1)S(1)}, bf16[2,4,256,2,2,128]{5,4,3,2,1,0:T(2,128)(2,1)}, u32[]{:S(2)}) copy-start(bf16[2,4,256,2,2,128]{5,4,3,2,1,0:T(2,128)(2,1)} %store.5) | copy-start | bytes 6291460
  5.9 20.7 %collective-permute-start.11 = (bf16[40,3072]{1,0:T(8,128)(2,1)}, bf16[40,3072]{1,0:T(8,128)(2,1)}, u32[]{:S(2)}, u32[]{:S(2)}) collective-permute-start(bf16[40,3072]{1,0:T(8,128)(2,1)} %get-tuple-element.9), channel_id=1, source_target_pairs={{0,12},{4,0},{8,4},{12,8},{1,13},{5,1},{9,5},{13,9},{2,14},{6,2},{... | collective-permute-start | bytes 737288 | tf_op jit(solution)/shard_map/ppermute | solution.py:154
  10.9 17.1 %collective-permute-start.7 = (bf16[40,3072]{1,0:T(8,128)(2,1)}, bf16[40,3072]{1,0:T(8,128)(2,1)}, u32[]{:S(2)}, u32[]{:S(2)}) collective-permute-start(bf16[40,3072]{1,0:T(8,128)(2,1)} %get-tuple-element.8), channel_id=1, source_target_pairs={{0,4},{4,8},{8,12},{12,0},{1,5},{5,9},{9,13},{13,1},{2,6},{6,10},{... | collective-permute-start | bytes 737288 | tf_op jit(solution)/shard_map/ppermute | solution.py:154
  10.9 32.5 %collective-permute-start.3 = (bf16[40,3072]{1,0:T(8,128)(2,1)S(1)}, bf16[40,3072]{1,0:T(8,128)(2,1)}, u32[]{:S(2)}, u32[]{:S(2)}) collective-permute-start(bf16[40,3072]{1,0:T(8,128)(2,1)S(1)} %get-tuple-element.7), channel_id=1, source_target_pairs={{0,8},{4,12},{8,0},{12,4},{1,9},{5,13},{9,1},{13,5},{2,10},{6,14},... | collective-permute-start | bytes 737288 | tf_op jit(solution)/shard_map/ppermute | solution.py:154
  12.0 33.1 %collective-permute-start = (bf16[2,256,2,2,128]{4,3,2,1,0:T(2,128)(2,1)S(1)}, bf16[2,256,2,2,128]{4,3,2,1,0:T(2,128)(2,1)S(1)}, u32[]{:S(2)}, u32[]{:S(2)}) collective-permute-start(bf16[2,256,2,2,128]{4,3,2,1,0:T(2,128)(2,1)S(1)} %shard_map.86), channel_id=1, source_target_pairs={{0,4},{4,8},{8,12},{12,0},{1,5},{5,9},{9,13},{13,1},{2,6},{6,10},{... | collective-permute-start | bytes 1572872 | tf_op jit(solution)/shard_map/ppermute | solution.py:154
  15.4 6.3 %copy-start.1 = (bf16[2,80,12288]{2,1,0:T(8,128)(2,1)S(1)}, bf16[2,80,12288]{2,1,0:T(8,128)(2,1)}, u32[]{:S(2)}) copy-start(bf16[2,80,12288]{2,1,0:T(8,128)(2,1)} %rows_ref.1) | copy-start | bytes 11796484
  23.5 2.9 %copy-start.7 = (s32[1,4]{1,0:T(1,128)S(1)}, s32[1,4]{1,0:T(1,128)}, u32[]{:S(2)}) copy-start(s32[1,4]{1,0:T(1,128)} %param.8) | copy-start | bytes 52
  23.5 5.1 %copy-start.6 = (s32[2,80]{1,0:T(2,128)S(1)}, s32[2,80]{1,0:T(2,128)}, u32[]{:S(2)}) copy-start(s32[2,80]{1,0:T(2,128)} %param.10) | copy-start | bytes 1924
  26.6 16.8 %collective-permute-start.12 = (bf16[40,3072]{1,0:T(8,128)(2,1)}, bf16[40,3072]{1,0:T(8,128)(2,1)}, u32[]{:S(2)}, u32[]{:S(2)}) collective-permute-start(bf16[40,3072]{1,0:T(8,128)(2,1)} %collective-permute-done.11), channel_id=1, source_target_pairs={{0,2},{1,3},{2,0},{3,1},{4,6},{5,7},{6,4},{7,5},{8,10},{9,11},{10,... | collective-permute-start | bytes 737288 | tf_op jit(solution)/shard_map/ppermute | solution.py:157
  28.1 16.8 %collective-permute-start.8 = (bf16[40,3072]{1,0:T(8,128)(2,1)}, bf16[40,3072]{1,0:T(8,128)(2,1)}, u32[]{:S(2)}, u32[]{:S(2)}) collective-permute-start(bf16[40,3072]{1,0:T(8,128)(2,1)} %collective-permute-done.7), channel_id=1, source_target_pairs={{0,2},{1,3},{2,0},{3,1},{4,6},{5,7},{6,4},{7,5},{8,10},{9,11},{10,... | collective-permute-start | bytes 737288 | tf_op jit(solution)/shard_map/ppermute | solution.py:157
  28.6 29.3 %collective-permute-start.10 = (bf16[40,3072]{1,0:T(8,128)(2,1)}, bf16[40,3072]{1,0:T(8,128)(2,1)}, u32[]{:S(2)}, u32[]{:S(2)}) collective-permute-start(bf16[40,3072]{1,0:T(8,128)(2,1)} %collective-permute-done.7), channel_id=1, source_target_pairs={{0,1},{1,0},{2,3},{3,2},{4,5},{5,4},{6,7},{7,6},{8,9},{9,8},{10,11... | collective-permute-start | bytes 737288 | tf_op jit(solution)/shard_map/ppermute | solution.py:157
  43.4 14.6 %collective-permute-start.14 = (bf16[40,3072]{1,0:T(8,128)(2,1)}, bf16[40,3072]{1,0:T(8,128)(2,1)}, u32[]{:S(2)}, u32[]{:S(2)}) collective-permute-start(bf16[40,3072]{1,0:T(8,128)(2,1)} %collective-permute-done.11), channel_id=1, source_target_pairs={{0,1},{1,0},{2,3},{3,2},{4,5},{5,4},{6,7},{7,6},{8,9},{9,8},{10,11... | collective-permute-start | bytes 737288 | tf_op jit(solution)/shard_map/ppermute | solution.py:157
  43.4 14.9 %collective-permute-start.4 = (bf16[40,3072]{1,0:T(8,128)(2,1)}, bf16[40,3072]{1,0:T(8,128)(2,1)}, u32[]{:S(2)}, u32[]{:S(2)}) collective-permute-start(bf16[40,3072]{1,0:T(8,128)(2,1)} %collective-permute-done.3), channel_id=1, source_target_pairs={{0,2},{1,3},{2,0},{3,1},{4,6},{5,7},{6,4},{7,5},{8,10},{9,11},{10,... | collective-permute-start | bytes 737288 | tf_op jit(solution)/shard_map/ppermute | solution.py:157
  44.9 13.7 %collective-permute-start.13 = (bf16[40,3072]{1,0:T(8,128)(2,1)}, bf16[40,3072]{1,0:T(8,128)(2,1)}, u32[]{:S(2)}, u32[]{:S(2)}) collective-permute-start(bf16[40,3072]{1,0:T(8,128)(2,1)} %collective-permute-done.12), channel_id=1, source_target_pairs={{0,1},{1,0},{2,3},{3,2},{4,5},{5,4},{6,7},{7,6},{8,9},{9,8},{10,11... | collective-permute-start | bytes 737288 | tf_op jit(solution)/shard_map/ppermute | solution.py:157
  45.1 21.6 %collective-permute-start.9 = (bf16[40,3072]{1,0:T(8,128)(2,1)}, bf16[40,3072]{1,0:T(8,128)(2,1)S(1)}, u32[]{:S(2)}, u32[]{:S(2)}) collective-permute-start(bf16[40,3072]{1,0:T(8,128)(2,1)} %collective-permute-done.8), channel_id=1, source_target_pairs={{0,1},{1,0},{2,3},{3,2},{4,5},{5,4},{6,7},{7,6},{8,9},{9,8},{10,11... | collective-permute-start | bytes 737288 | tf_op jit(solution)/shard_map/ppermute | solution.py:157
  57.9 61.2 %collective-permute-start.2 = (bf16[2,256,2,2,128]{4,3,2,1,0:T(2,128)(2,1)}, bf16[2,256,2,2,128]{4,3,2,1,0:T(2,128)(2,1)S(1)}, u32[]{:S(2)}, u32[]{:S(2)}) collective-permute-start(bf16[2,256,2,2,128]{4,3,2,1,0:T(2,128)(2,1)} %shard_map.88), channel_id=1, source_target_pairs={{0,12},{4,0},{8,4},{12,8},{1,13},{5,1},{9,5},{13,9},{2,14},{6,2},{... | collective-permute-start | bytes 1572872 | tf_op jit(solution)/shard_map/ppermute | solution.py:154
  58.0 16.4 %collective-permute-start.6 = (bf16[40,3072]{1,0:T(8,128)(2,1)}, bf16[40,3072]{1,0:T(8,128)(2,1)S(1)}, u32[]{:S(2)}, u32[]{:S(2)}) collective-permute-start(bf16[40,3072]{1,0:T(8,128)(2,1)} %collective-permute-done.3), channel_id=1, source_target_pairs={{0,1},{1,0},{2,3},{3,2},{4,5},{5,4},{6,7},{7,6},{8,9},{9,8},{10,11... | collective-permute-start | bytes 737288 | tf_op jit(solution)/shard_map/ppermute | solution.py:157
  58.3 18.2 %collective-permute-start.5 = (bf16[40,3072]{1,0:T(8,128)(2,1)}, bf16[40,3072]{1,0:T(8,128)(2,1)S(1)}, u32[]{:S(2)}, u32[]{:S(2)}) collective-permute-start(bf16[40,3072]{1,0:T(8,128)(2,1)} %collective-permute-done.4), channel_id=1, source_target_pairs={{0,1},{1,0},{2,3},{3,2},{4,5},{5,4},{6,7},{7,6},{8,9},{9,8},{10,11... | collective-permute-start | bytes 737288 | tf_op jit(solution)/shard_map/ppermute | solution.py:157
  58.6 60.6 %collective-permute-start.1 = (bf16[2,256,2,2,128]{4,3,2,1,0:T(2,128)(2,1)}, bf16[2,256,2,2,128]{4,3,2,1,0:T(2,128)(2,1)S(1)}, u32[]{:S(2)}, u32[]{:S(2)}) collective-permute-start(bf16[2,256,2,2,128]{4,3,2,1,0:T(2,128)(2,1)} %shard_map.87), channel_id=1, source_target_pairs={{0,8},{4,12},{8,0},{12,4},{1,9},{5,13},{9,1},{13,5},{2,10},{6,14},... | collective-permute-start | bytes 1572872 | tf_op jit(solution)/shard_map/ppermute | solution.py:154
  68.4 4.2 %slice-start = ((s8[6291456]{0:T(1024)(128)(4,1)}), s8[4194304]{0:T(1024)(128)(4,1)S(1)}, s32[]{:S(2)}) async-start(s8[6291456]{0:T(1024)(128)(4,1)} %bitcast.30), calls=%async_computation | async-start | bytes 8388608
  68.5 4.7 %slice-start.1 = ((s8[6291456]{0:T(1024)(128)(4,1)}), s8[2097152]{0:T(1024)(128)(4,1)S(1)}, s32[]{:S(2)}) async-start(s8[6291456]{0:T(1024)(128)(4,1)} %bitcast.30), calls=%async_computation.1 | async-start | bytes 4194304
  74.3 29.2 %collective-permute-start.17 = (f32[2,80,512]{2,1,0:T(8,128)S(1)}, f32[2,80,512]{2,1,0:T(8,128)S(1)}, u32[]{:S(2)}, u32[]{:S(2)}) collective-permute-start(f32[2,80,512]{2,1,0:T(8,128)S(1)} %get-tuple-element.26), channel_id=1, source_target_pairs={{0,4},{4,0},{8,12},{12,8},{1,5},{5,1},{9,13},{13,9},{2,6},{6,2},{1... | collective-permute-start | bytes 983048 | tf_op jit(solution)/shard_map/ppermute | solution.py:157
  74.4 27.9 %collective-permute-start.15 = (f32[2,80,512]{2,1,0:T(8,128)S(1)}, f32[2,80,512]{2,1,0:T(8,128)S(1)}, u32[]{:S(2)}, u32[]{:S(2)}) collective-permute-start(f32[2,80,512]{2,1,0:T(8,128)S(1)} %get-tuple-element.27), channel_id=1, source_target_pairs={{0,4},{4,0},{8,12},{12,8},{1,5},{5,1},{9,13},{13,9},{2,6},{6,2},{1... | collective-permute-start | bytes 983048 | tf_op jit(solution)/shard_map/ppermute | solution.py:157
  103.5 15.6 %collective-permute-start.16 = (f32[2,80,512]{2,1,0:T(8,128)S(1)}, f32[2,80,512]{2,1,0:T(8,128)S(1)}, u32[]{:S(2)}, u32[]{:S(2)}) collective-permute-start(f32[2,80,512]{2,1,0:T(8,128)S(1)} %convolution_add_fusion.1), channel_id=1, source_target_pairs={{0,8},{4,12},{8,0},{12,4},{1,9},{5,13},{9,1},{13,5},{2,10},{6,14},... | collective-permute-start | bytes 983048 | tf_op jit(solution)/shard_map/ppermute | solution.py:154
  (5 other events, 6.1 us)

commit v3 on v2

v3 whole, which is shorter than its diff:
```python
import functools

import jax
import jax.numpy as jnp
from jax import lax
from jax.experimental import pallas as pl
from jax.experimental.pallas import tpu as pltpu
from jax.sharding import PartitionSpec as P

KVH = 8
PROMPT_PER_HOLD = 512
LAYERS = 2
CHUNK = 8
ROWS = 16
VMEM_BYTES = 40 * 1024 * 1024
PARAMS = pltpu.CompilerParams(vmem_limit_bytes=VMEM_BYTES)
HBM = pl.BlockSpec(memory_space=pltpu.HBM)
VMEM = pl.BlockSpec(memory_space=pltpu.VMEM)
SMEM = pl.BlockSpec(memory_space=pltpu.SMEM)


def norm_kernel(at, rows_ref, gain_ref, *refs):
    own, outs, held = refs[0], refs[1:-1], refs[-1]
    rows = rows_ref[...].astype(jnp.float32)
    held[...] = lax.rsqrt(jnp.mean(rows * rows, axis=1, keepdims=True) + 1e-05)
    layer = pl.program_id(0) // (pl.num_programs(0) // gain_ref.shape[0])
    for i, out in enumerate((own,) + outs):
        columns = pl.ds(pl.multiple_of(at[i], 128), out.shape[1])
        gain = gain_ref[0:1, columns].astype(jnp.float32)
        for other in range(1, gain_ref.shape[0]):
            gain = jnp.where(
                layer == other, gain_ref[other : other + 1, columns].astype(jnp.float32), gain
            )
        part = rows_ref[:, columns].astype(jnp.float32)
        out[...] = (part * held[...] * gain).astype(jnp.bfloat16)


def normed_shares(hidden, gain, me, share, n, feats, part):
    layers, rec, width = hidden.shape
    rows = layers * rec
    at = jnp.stack([me * feats] + [((me + k) % n) * feats + share * part for k in range(1, n)])
    sizes = [feats] + [part] * (n - 1)
    return pl.pallas_call(
        norm_kernel,
        grid_spec=pltpu.PrefetchScalarGridSpec(
            num_scalar_prefetch=1,
            grid=(rows // ROWS,),
            in_specs=[
                pl.BlockSpec((ROWS, width), lambda i, at: (i, 0)),
                pl.BlockSpec(gain.shape, lambda i, at: (0, 0)),
            ],
            out_specs=[pl.BlockSpec((ROWS, size), lambda i, at: (i, 0)) for size in sizes],
            scratch_shapes=[pltpu.VMEM((ROWS, 1), jnp.float32)],
        ),
        out_shape=[jax.ShapeDtypeStruct((rows, size), jnp.bfloat16) for size in sizes],
        compiler_params=PARAMS,
    )(at.astype(jnp.int32), hidden.reshape(rows, width), gain)


def pick_kernel(at, store, *refs):
    outs, sems = refs[:-1], refs[-1]
    copies = [
        pltpu.make_async_copy(store.at[:, at[i]], out, sems.at[i]) for i, out in enumerate(outs)
    ]
    for copy in copies:
        copy.start()
    for copy in copies:
        copy.wait()


def pick(store, at):
    shape = store.shape[:1] + store.shape[2:]
    return pl.pallas_call(
        pick_kernel,
        grid_spec=pltpu.PrefetchScalarGridSpec(
            num_scalar_prefetch=1,
            grid=(),
            in_specs=[HBM],
            out_specs=[HBM] * len(at),
            scratch_shapes=[pltpu.SemaphoreType.DMA((len(at),))],
        ),
        out_shape=[jax.ShapeDtypeStruct(shape, store.dtype)] * len(at),
        compiler_params=PARAMS,
    )(jnp.stack(at).astype(jnp.int32), store)


def product_kernel(counts, at, *refs):
    shares, refs = refs[: sum(counts)], refs[sum(counts) :]
    weight, refs = refs[0], refs[1:]
    held, outs = refs[-1], refs[-1 - len(counts) : -1]
    layers, rec, _ = outs[0].shape
    base = 0
    for i, count in enumerate(counts):
        row = pl.multiple_of(at[i] * rec, 16)
        for j in range(count):
            piece = shares[base + j]
            column = pl.multiple_of(at[len(counts) + base + j], 128)
            for layer in range(layers):
                held[layer, pl.ds(row, rec), pl.ds(column, piece.shape[1])] = piece[
                    layer * rec : (layer + 1) * rec
                ]
        base += count
    for layer in range(layers):
        result = jnp.dot(held[layer], weight[layer], preferred_element_type=jnp.float32)
        for i, out in enumerate(outs):
            out[layer] = result[i * rec : (i + 1) * rec]


def products(blocks, weight, order, columns, rec, after):
    counts = tuple(len(block) for block in blocks)
    at = jnp.stack(list(order) + [c for cs in columns for c in cs]).astype(jnp.int32)
    layers, feats, cols = weight.shape
    flat = [share for block in blocks for share in block]
    return pl.pallas_call(
        functools.partial(product_kernel, counts),
        in_specs=[SMEM] + [VMEM] * (len(flat) + 1) + [HBM] * len(after),
        out_specs=[VMEM] * len(blocks),
        out_shape=[jax.ShapeDtypeStruct((layers, rec, cols), jnp.float32)] * len(blocks),
        scratch_shapes=[pltpu.VMEM((layers, len(blocks) * rec, feats), jnp.bfloat16)],
        compiler_params=PARAMS,
    )(at, *flat, weight, *after)


def add_kernel(count, *refs):
    outs = refs[len(refs) - count :]
    for left, right, out in zip(refs[:count], refs[count : 2 * count], outs):
        out[...] = left[...] + right[...]


def add_pairs(left, right, after):
    count = len(left)
    return pl.pallas_call(
        functools.partial(add_kernel, count),
        in_specs=[VMEM] * (2 * count) + [HBM] * len(after),
        out_specs=[VMEM] * count,
        out_shape=[jax.ShapeDtypeStruct(value.shape, value.dtype) for value in left],
        compiler_params=PARAMS,
    )(*left, *right, *after)


def unite_kernel(n, starts, lengths, spots, *refs):
    pages, fresh, out, sums, held = refs[:n], refs[n], refs[n + 1], refs[n + 2], refs[n + 3]
    layers, rec = fresh.shape[:2]
    for slot, page in enumerate(pages):
        start, length = starts[slot], lengths[slot]
        whole = length // CHUNK

        def many(i, carry, page=page, start=start):
            for layer in range(layers):
                out[layer, pl.ds(start + i * CHUNK, CHUNK)] = page[layer, pl.ds(i * CHUNK, CHUNK)]
            return carry

        def one(i, carry, page=page, start=start):
            for layer in range(layers):
                out[layer, start + i] = page[layer, i]
            return carry

        lax.fori_loop(0, whole, many, 0)
        lax.fori_loop(whole * CHUNK, length, one, 0)
    for layer in range(layers):

        def renew(j, carry, layer=layer):
            at = layer * rec + j
            spot = spots[at]
            old = out[layer, spot].astype(jnp.float32)
            new = fresh[layer, j]
            diff = new.astype(jnp.float32) - old
            held[pl.ds(at, 1), :] = jnp.sum(jnp.sum(diff * diff, axis=0), axis=0, keepdims=True)
            held[pl.ds(layers * rec + at, 1), :] = jnp.sum(
                jnp.sum(old * old, axis=0), axis=0, keepdims=True
            )
            out[layer, spot] = new
            return carry

        lax.fori_loop(0, rec, renew, 0, unroll=4)
    ones = jnp.ones((8, held.shape[1]), jnp.float32)
    both = lax.dot_general(
        ones,
        held[...],
        (((1,), (1,)), ((), ())),
        precision=lax.Precision.HIGHEST,
        preferred_element_type=jnp.float32,
    )
    sums[...] = both[0:1]


def unite(pages, fresh, starts, lengths, spots):
    n = len(pages)
    layers, rec = fresh.shape[:2]
    row = fresh.shape[2:]
    return pl.pallas_call(
        functools.partial(unite_kernel, n),
        in_specs=[SMEM] * 3 + [VMEM] * (n + 1),
        out_specs=[VMEM, VMEM],
        out_shape=[
            jax.ShapeDtypeStruct((layers, PROMPT_PER_HOLD) + row, fresh.dtype),
            jax.ShapeDtypeStruct((1, 2 * layers * rec), jnp.float32),
        ],
        scratch_shapes=[pltpu.VMEM((2 * layers * rec, row[-1]), jnp.float32)],
        compiler_params=PARAMS,
    )(starts, lengths, spots, *pages, fresh)


def make_local(n, tps):
    def shift(value, k):
        return lax.ppermute(value, "hold", [(i, (i + k) % n) for i in range(n)])

    def swap(value, axis, size, bit):
        return lax.ppermute(value, axis, [(i, i ^ bit) for i in range(size)])

    def local(cache_store, span_lengths, span_holder, rec_pos, hidden, norm_gain, kv_weight):
        me = lax.axis_index("hold")
        my_tp = lax.axis_index("tp")
        rec = hidden.shape[1]
        feats = kv_weight.shape[1]
        heads_here, head_size = kv_weight.shape[2], kv_weight.shape[4]
        cols = heads_here * 2 * head_size
        odds = sorted(range(1, n, 2), key=lambda k: min(k, n - k))
        evens = sorted(range(2, n, 2), key=lambda k: min(k, n - k))
        cuts = tps
        while feats % (cuts * 128):
            cuts //= 2
        part = feats // cuts
        share = my_tp % cuts

        own, *pieces = normed_shares(hidden, norm_gain, me, share, n, feats, part)
        arrived = {k: shift(pieces[k - 1], k) for k in odds + evens}

        sent = pick(cache_store, [(me + k) % n for k in range(1, n)])
        pages = {k: shift(sent[k - 1], k) for k in odds + evens}
        pages[0] = lax.dynamic_index_in_dim(cache_store, me, axis=1, keepdims=False)

        weight = kv_weight.reshape(LAYERS, feats, cols)

        def everyone(piece):
            shares, masks, bit = [piece], [0], cuts // 2
            while bit:
                shares = shares + [swap(value, "tp", tps, bit) for value in shares]
                masks = masks + [mask ^ bit for mask in masks]
                bit //= 2
            return shares, [(share ^ mask) * part for mask in masks]

        even = me % 2 == 0
        away = [everyone(arrived[k]) for k in odds]
        spot = [jnp.where(even, (k + 1) // 2 % (n // 2), (k - 1) // 2) for k in odds]
        away = products(
            [a[0] for a in away], weight, spot, [a[1] for a in away], rec, [pages[k] for k in odds]
        )
        theirs = [swap(away[i % (n // 2)], "hold", n, 1) for i in range(1, n // 2 + 1)]
        mine = [everyone(arrived[k]) for k in range(2, n, 2)] + [([own], [jnp.int32(0)])]
        mine = products(
            [a[0] for a in mine],
            weight,
            [jnp.int32(i) for i in range(n // 2)],
            [a[1] for a in mine],
            rec,
            [],
        )
        total = mine[-1] + theirs[-1]
        if n > 2:
            pairs = add_pairs(mine[:-1], theirs[:-1], [pages[k] for k in evens])
            for k, pair in zip(range(2, n, 2), pairs):
                total = total + shift(pair, -k)
        fresh = total.astype(jnp.bfloat16).reshape(LAYERS, rec, heads_here, 2, head_size)

        lengths = span_lengths[0]
        starts = jnp.cumsum(lengths) - lengths
        holders = (me - jnp.arange(n, dtype=jnp.int32)) % n
        held_here = span_holder[0][None, :] == holders[:, None]
        slot_starts = jnp.sum(jnp.where(held_here, starts[None, :], 0), axis=1)
        slot_lengths = jnp.sum(jnp.where(held_here, lengths[None, :], 0), axis=1)
        spots = (rec_pos - me * PROMPT_PER_HOLD).reshape(-1)
        united, sums = unite(
            [pages[k] for k in range(n)], fresh, slot_starts, slot_lengths, spots
        )
        sums = lax.psum(sums, "tp").reshape(2, LAYERS, rec)
        entries = KVH * 2 * head_size
        deviation = sums[0] / entries / (sums[1] / entries + 1e-06)
        return (united, deviation)

    return local


def solution(mesh):
    return jax.shard_map(
        make_local(mesh.shape["hold"], mesh.shape["tp"]),
        mesh=mesh,
        in_specs=(
            P(None, ("groups", "hold"), None, "tp", None, None),
            P(("groups", "hold"), None),
            P(("groups", "hold"), None),
            P(None, ("groups", "hold")),
            P(None, ("groups", "hold"), None),
            P(),
            P(None, "hold", "tp", None, None),
        ),
        out_specs=(P(None, ("groups", "hold"), "tp", None, None), P(None, ("groups", "hold"))),
        check_vma=False,
    )
```

time: 130 us -> 123 us (0.946)
  waiting for transfers between devices: 53.6 us -> 32.9 us
  starting transfers between devices: 24.5 us -> 38.1 us
  local copies, waits for them, and re-layouts: 15.7 us -> 28.7 us
  other arithmetic: 13.6 us -> 0.71 us
  Pallas kernels: 7.04 us -> 15.2 us
  matrix products: 7.75 us -> 0 us
    unnamed x22 -> x36, local copies, waits for them, and re-layouts: 3.39 us -> 16.4 us
    ppermute x11, starting transfers between devices: 6.76 us -> 18.1 us  [swap(): return lax.ppermute(value, axis, [(i, i ^ bit) for i in range(size)])]
    ppermute x7, waiting for transfers between devices: 29 us -> 18.3 us  [shift(): return lax.ppermute(value, 'hold', [(i, (i + k) % n) for i in range(n)])]
    ppermute x11, waiting for transfers between devices: 24.6 us -> 14.6 us  [swap(): return lax.ppermute(value, axis, [(i, i ^ bit) for i in range(size)])]
    convert_element_type x2 -> x0, other arithmetic: 9.11 us -> none  [the longest x1 6.27 us: norm_rows(): rows = rows.astype(jnp.float32)]
    dot_general x4 -> x0, matrix products: 7.75 us -> none  [product(): jnp.einsum('lrf,lfc->lrc', rows.reshape(LAYERS, rec, feats), weight, pref...]
    pallas_call x1 -> x4, Pallas kernels: 2.2 us -> 9.82 us  [the longest x2 5.96 us: products(): pl.pallas_call(functools.partial(product_kernel, counts), in_specs=[SMEM]...]
    select_n x2 -> x0, other arithmetic: 2.84 us -> none  [everyone(): shares = [jnp.where(flip, shares[m ^ bit], shares[m]) for m in range(tps)]]
  transfers between devices with their start and end apart: 18 -> 18, of which waited for: 3 -> 8; matrix products, arithmetic and copies ran while one was open for 25% -> 10% of each run, Pallas kernels for 1% -> 6%
where the time goes in v3:
time: 123 us; the launch traced here: 122 us
  starting transfers between devices  38.1 us (31%)
  waiting for transfers between devices  32.9 us (27%)
  local copies, waits for them, and re-layouts  28.7 us (23%)
  Pallas kernels  15.2 us (12%)
  blocking collectives  5.88 us (5%)
    ppermute x7, starting transfers between devices, shift(): return lax.ppermute(value, 'hold', [(i, (i + k) % n) for i in range(n)])  20 us
    ppermute x7, waiting for transfers between devices, shift(): return lax.ppermute(value, 'hold', [(i, (i + k) % n) for i in range(n)])  18.3 us
    ppermute x11, starting transfers between devices, swap(): return lax.ppermute(value, axis, [(i, i ^ bit) for i in range(size)])  18.1 us
    unnamed x36, local copies, waits for them, and re-layouts  16.4 us
    ppermute x11, waiting for transfers between devices, swap(): return lax.ppermute(value, axis, [(i, i ^ bit) for i in range(size)])  14.6 us
    reshape x1, local copies, waits for them, and re-layouts, local(): weight = kv_weight.reshape(LAYERS, feats, cols)  10.2 us
    pallas_call x2, Pallas kernels, products(): pl.pallas_call(functools.partial(product_kernel, counts), in_specs=[SMEM]...  5.96 us
    psum x1, blocking collectives, local(): sums = lax.psum(sums, 'tp').reshape(2, LAYERS, rec)  5.88 us
  transfers between devices with their start and end apart: 18, of which 8 were waited for; matrix products, arithmetic and copies ran while one was open for 10% of the time, Pallas kernels for 6%

profile of v3, /device:TPU:0, one launch (start us, length us, event | category | flops | bytes accessed | tf_op | source)
XLA Modules:
  0.0 122.3 jit_solution(6899060326882502035)
XLA Ops:
  0.8 2.1 %copy-done.2 = bf16[2,80,12288]{2,1,0:T(8,128)(2,1)S(1)} copy-done((bf16[2,80,12288]{2,1,0:T(8,128)(2,1)S(1)}, bf16[2,80,12288]{2,1,0:T(8,128)(2,1)}, u32[]{:S(2)}) %copy-start.2) | copy-done | bytes 3932184
  3.7 3.8 %shard_map.87 = (bf16[160,3072]{1,0:T(8,128)(2,1)S(1)}, bf16[160,768]{1,0:T(8,128)(2,1)S(1)}, bf16[160,768]{1,0:T(8,128)(2,1)S(1)}, bf16[160,768]{1,0:T(8,128)(2,1)S(1)}) custom-call(s32[4]{0:T(128)S(1)} %pad_add_fusion.1.at, bf16[160,12288]{1,0:T(8,128)(2,1)S(1)} %bitcast.20, bf16[2,12288]{1,0:T(2,128)(2,1)S(1)} %copy-done.13), custom_call_target="tpu_custom_call" | custom-call | tf_op jit(solution)/shard_map/pallas_call | solution.py:43
  7.5 4.1 %collective-permute-start.3 = (bf16[160,768]{1,0:T(8,128)(2,1)S(1)}, bf16[160,768]{1,0:T(8,128)(2,1)}, u32[]{:S(2)}, u32[]{:S(2)}) collective-permute-start(bf16[160,768]{1,0:T(8,128)(2,1)S(1)} %get-tuple-element.18), channel_id=1, source_target_pairs={{0,8},{4,12},{8,0},{12,4},{1,9},{5,13},{9,1},{13,5},{2,10},{6,14},... | collective-permute-start | bytes 737288 | tf_op jit(solution)/shard_map/ppermute | solution.py:206
  11.6 1.6 %collective-permute-start.7 = (bf16[160,768]{1,0:T(8,128)(2,1)S(1)}, bf16[160,768]{1,0:T(8,128)(2,1)S(1)}, u32[]{:S(2)}, u32[]{:S(2)}) collective-permute-start(bf16[160,768]{1,0:T(8,128)(2,1)S(1)} %get-tuple-element.21), channel_id=1, source_target_pairs={{0,4},{4,8},{8,12},{12,0},{1,5},{5,9},{9,13},{13,1},{2,6},{6,10},{... | collective-permute-start | bytes 737288 | tf_op jit(solution)/shard_map/ppermute | solution.py:206
  13.2 2.2 %collective-permute-start.11 = (bf16[160,768]{1,0:T(8,128)(2,1)S(1)}, bf16[160,768]{1,0:T(8,128)(2,1)S(1)}, u32[]{:S(2)}, u32[]{:S(2)}) collective-permute-start(bf16[160,768]{1,0:T(8,128)(2,1)S(1)} %get-tuple-element.22), channel_id=1, source_target_pairs={{0,12},{4,0},{8,4},{12,8},{1,13},{5,1},{9,5},{13,9},{2,14},{6,2},{... | collective-permute-start | bytes 737288 | tf_op jit(solution)/shard_map/ppermute | solution.py:206
  15.4 13.6 %collective-permute-done.3.refs_0_ = bf16[160,768]{1,0:T(8,128)(2,1)} collective-permute-done((bf16[160,768]{1,0:T(8,128)(2,1)S(1)}, bf16[160,768]{1,0:T(8,128)(2,1)}, u32[]{:S(2)}, u32[]{:S(2)}) %collective-permute-start.3) | collective-permute-done | bytes 245792 | tf_op jit(solution)/shard_map/ppermute | solution.py:206
  29.1 1.8 %collective-permute-start.4 = (bf16[160,768]{1,0:T(8,128)(2,1)}, bf16[160,768]{1,0:T(8,128)(2,1)}, u32[]{:S(2)}, u32[]{:S(2)}) collective-permute-start(bf16[160,768]{1,0:T(8,128)(2,1)} %collective-permute-done.3.refs_0_), channel_id=1, source_target_pairs={{0,2},{1,3},{2,0},{3,1},{4,6},{5,7},{6,4},{7,5},{8,10},{9,11},{10,... | collective-permute-start | bytes 737288 | tf_op jit(solution)/shard_map/ppermute | solution.py:209
  31.2 1.7 %shard_map.86 = (bf16[2,256,2,2,128]{4,3,2,1,0:T(2,128)(2,1)}, bf16[2,256,2,2,128]{4,3,2,1,0:T(2,128)(2,1)}, bf16[2,256,2,2,128]{4,3,2,1,0:T(2,128)(2,1)}) custom-call(s32[3]{0:T(128)S(1)} %pad_add_fusion.at, bf16[2,4,256,2,2,128]{5,4,3,2,1,0:T(2,128)(2,1)S(1)} %copy-done.3), custom_call_target="tpu_custom_call" | custom-call | tf_op jit(solution)/shard_map/pallas_call | solution.py:73
  32.9 4.5 %collective-permute-start = (bf16[2,256,2,2,128]{4,3,2,1,0:T(2,128)(2,1)}, bf16[2,256,2,2,128]{4,3,2,1,0:T(2,128)(2,1)S(1)}, u32[]{:S(2)}, u32[]{:S(2)}) collective-permute-start(bf16[2,256,2,2,128]{4,3,2,1,0:T(2,128)(2,1)} %get-tuple-element.15), channel_id=1, source_target_pairs={{0,4},{4,8},{8,12},{12,0},{1,5},{5,9},{9,13},{13,1},{2,6},{6,10},{... | collective-permute-start | bytes 1572872 | tf_op jit(solution)/shard_map/ppermute | solution.py:206
  39.6 1.6 %collective-permute-done.8.refs_1_ = bf16[160,768]{1,0:T(8,128)(2,1)} collective-permute-done((bf16[160,768]{1,0:T(8,128)(2,1)S(1)}, bf16[160,768]{1,0:T(8,128)(2,1)}, u32[]{:S(2)}, u32[]{:S(2)}) %collective-permute-start.8) | collective-permute-done | bytes 245792 | tf_op jit(solution)/shard_map/ppermute | solution.py:209
  43.1 3.1 %collective-permute-done.12.refs_5_ = bf16[160,768]{1,0:T(8,128)(2,1)} collective-permute-done((bf16[160,768]{1,0:T(8,128)(2,1)S(1)}, bf16[160,768]{1,0:T(8,128)(2,1)}, u32[]{:S(2)}, u32[]{:S(2)}) %collective-permute-start.12) | collective-permute-done | bytes 245792 | tf_op jit(solution)/shard_map/ppermute | solution.py:209
  47.0 3.6 %collective-permute-start.1 = (bf16[2,256,2,2,128]{4,3,2,1,0:T(2,128)(2,1)}, bf16[2,256,2,2,128]{4,3,2,1,0:T(2,128)(2,1)}, u32[]{:S(2)}, u32[]{:S(2)}) collective-permute-start(bf16[2,256,2,2,128]{4,3,2,1,0:T(2,128)(2,1)} %get-tuple-element.16), channel_id=1, source_target_pairs={{0,8},{4,12},{8,0},{12,4},{1,9},{5,13},{9,1},{13,5},{2,10},{6,14},... | collective-permute-start | bytes 1572872 | tf_op jit(solution)/shard_map/ppermute | solution.py:206
  50.6 10.2 %reshape.51.refs_5_.refs_8_ = bf16[2,3072,512]{2,1,0:T(8,128)(2,1)} reshape(bf16[2,3072,2,2,128]{4,3,2,1,0:T(2,128)(2,1)} %param.13) | data formatting | bytes 12582912 | tf_op jit(solution)/shard_map/reshape | solution.py:233
  61.4 2.8 %copy-done = bf16[2,3072,512]{2,1,0:T(8,128)(2,1)S(1)} copy-done((bf16[2,3072,512]{2,1,0:T(8,128)(2,1)S(1)}, bf16[2,3072,512]{2,1,0:T(8,128)(2,1)}, u32[]{:S(2)}) %copy-start) | copy-done | bytes 6291480
  67.0 3.3 %shard_map.89 = (f32[2,80,512]{2,1,0:T(8,128)S(1)}, f32[2,80,512]{2,1,0:T(8,128)}) custom-call(s32[10]{0:T(128)S(1)} %stack.75.at, bf16[160,768]{1,0:T(8,128)(2,1)S(1)} %collective-permute-done.7.refs_0_, bf16[160,768]{1,0:T(8,128)(2,1)} %collective-permute-done.8.refs_1_, bf16[160,768]{1,0:T(8,128)(2,1)S(1)} %copy-done.10, ...), custom_call_target="tpu_custom_call" | custom-call | tf_op jit(solution)/shard_map/pallas_call | solution.py:114
  71.1 13.8 %collective-permute-start.16 = (f32[2,80,512]{2,1,0:T(8,128)}, f32[2,80,512]{2,1,0:T(8,128)S(1)}, u32[]{:S(2)}, u32[]{:S(2)}) collective-permute-start(f32[2,80,512]{2,1,0:T(8,128)} %get-tuple-element.25), channel_id=1, source_target_pairs={{0,4},{4,0},{8,12},{12,8},{1,5},{5,1},{9,13},{13,9},{2,6},{6,2},{1... | collective-permute-start | bytes 983048 | tf_op jit(solution)/shard_map/ppermute | solution.py:209
  85.4 2.8 %copy-done.1 = bf16[2,3072,512]{2,1,0:T(8,128)(2,1)S(1)} copy-done((bf16[2,3072,512]{2,1,0:T(8,128)(2,1)S(1)}, bf16[2,3072,512]{2,1,0:T(8,128)(2,1)}, u32[]{:S(2)}) %copy-start.1) | copy-done | bytes 6291480
  89.4 2.6 %shard_map.88 = (f32[2,80,512]{2,1,0:T(8,128)S(1)}, f32[2,80,512]{2,1,0:T(8,128)S(1)}) custom-call(s32[7]{0:T(128)S(1)} %stack.67.at, bf16[160,768]{1,0:T(8,128)(2,1)} %collective-permute-done.3.refs_0_, bf16[160,768]{1,0:T(8,128)(2,1)} %collective-permute-done.4.refs_1_, bf16[160,768]{1,0:T(8,128)(2,1)} %collective-permute-done.5.refs_2_, ...), custom_call_target="tpu_custom_call" | custom-call | tf_op jit(solution)/shard_map/pallas_call | solution.py:114
  92.0 1.7 %collective-permute-done.16.refs_1_ = f32[2,80,512]{2,1,0:T(8,128)S(1)} collective-permute-done((f32[2,80,512]{2,1,0:T(8,128)}, f32[2,80,512]{2,1,0:T(8,128)S(1)}, u32[]{:S(2)}, u32[]{:S(2)}) %collective-permute-start.16) | collective-permute-done | bytes 327712 | tf_op jit(solution)/shard_map/ppermute | solution.py:209
  93.7 3.9 %collective-permute-start.17 = (f32[2,80,512]{2,1,0:T(8,128)S(1)}, f32[2,80,512]{2,1,0:T(8,128)S(1)}, u32[]{:S(2)}, u32[]{:S(2)}) collective-permute-start(f32[2,80,512]{2,1,0:T(8,128)S(1)} %shard_map.90), channel_id=1, source_target_pairs={{0,8},{4,12},{8,0},{12,4},{1,9},{5,13},{9,1},{13,5},{2,10},{6,14},... | collective-permute-start | bytes 983048 | tf_op jit(solution)/shard_map/ppermute | solution.py:206
  99.0 7.4 %collective-permute-done.15 = f32[2,80,512]{2,1,0:T(8,128)S(1)} collective-permute-done((f32[2,80,512]{2,1,0:T(8,128)}, f32[2,80,512]{2,1,0:T(8,128)S(1)}, u32[]{:S(2)}, u32[]{:S(2)}) %collective-permute-start.15) | collective-permute-done | bytes 327712 | tf_op jit(solution)/shard_map/ppermute | solution.py:209
  106.4 4.4 %collective-permute-done.17 = f32[2,80,512]{2,1,0:T(8,128)S(1)} collective-permute-done((f32[2,80,512]{2,1,0:T(8,128)S(1)}, f32[2,80,512]{2,1,0:T(8,128)S(1)}, u32[]{:S(2)}, u32[]{:S(2)}) %collective-permute-start.17) | collective-permute-done | bytes 327712 | tf_op jit(solution)/shard_map/ppermute | solution.py:206
  112.0 3.7 %shard_map.91 = (bf16[2,512,2,2,128]{4,3,2,1,0:T(2,128)(2,1)}, f32[1,320]{1,0:T(1,128)S(1)}) custom-call(s32[4]{0:T(128)S(1)} %get-tuple-element.29.starts, s32[4]{0:T(128)S(1)} %get-tuple-element.28.lengths, s32[160]{0:T(256)S(1)} %reshape.49.spots, bf16[2,256,2,2,128]{4,3,2,1,0:T(2,128)(2,1)S(1)} %copy-done.4, ...), custom_call_target="tpu_custom_call" | custom-call | tf_op jit(solution)/shard_map/pallas_call | solution.py:191
  115.6 5.9 %psum.7 = f32[1,320]{1,0:T(1,128)S(1)} all-reduce(f32[1,320]{1,0:T(1,128)S(1)} %get-tuple-element.27), channel_id=1, replica_groups=mesh['groups'=2,'hold'=4,'tp'=4] {'tp'}, use_global_device_ids=true, to_apply=%region_3.4 | all-reduce | flops 320 | bytes 2560 | tf_op jit(solution)/shard_map/psum | solution.py:276
  (71 shorter events, 15.1 us)
Async XLA Ops:
  3.7 27.5 %copy-start.3 = (bf16[2,4,256,2,2,128]{5,4,3,2,1,0:T(2,128)(2,1)S(1)}, bf16[2,4,256,2,2,128]{5,4,3,2,1,0:T(2,128)(2,1)}, u32[]{:S(2)}) copy-start(bf16[2,4,256,2,2,128]{5,4,3,2,1,0:T(2,128)(2,1)} %store.1) | copy-start | bytes 6291460
  7.5 29.9 %copy-start.5 = (bf16[160,3072]{1,0:T(8,128)(2,1)}, bf16[160,3072]{1,0:T(8,128)(2,1)S(1)}, u32[]{:S(2)}) copy-start(bf16[160,3072]{1,0:T(8,128)(2,1)S(1)} %get-tuple-element.19.refs_4_) | copy-start | bytes 2949124
  7.5 21.6 %collective-permute-start.3 = (bf16[160,768]{1,0:T(8,128)(2,1)S(1)}, bf16[160,768]{1,0:T(8,128)(2,1)}, u32[]{:S(2)}, u32[]{:S(2)}) collective-permute-start(bf16[160,768]{1,0:T(8,128)(2,1)S(1)} %get-tuple-element.18), channel_id=1, source_target_pairs={{0,8},{4,12},{8,0},{12,4},{1,9},{5,13},{9,1},{13,5},{2,10},{6,14},... | collective-permute-start | bytes 737288 | tf_op jit(solution)/shard_map/ppermute | solution.py:206
  11.6 19.3 %collective-permute-start.7 = (bf16[160,768]{1,0:T(8,128)(2,1)S(1)}, bf16[160,768]{1,0:T(8,128)(2,1)S(1)}, u32[]{:S(2)}, u32[]{:S(2)}) collective-permute-start(bf16[160,768]{1,0:T(8,128)(2,1)S(1)} %get-tuple-element.21), channel_id=1, source_target_pairs={{0,4},{4,8},{8,12},{12,0},{1,5},{5,9},{9,13},{13,1},{2,6},{6,10},{... | collective-permute-start | bytes 737288 | tf_op jit(solution)/shard_map/ppermute | solution.py:206
  13.2 24.3 %collective-permute-start.11 = (bf16[160,768]{1,0:T(8,128)(2,1)S(1)}, bf16[160,768]{1,0:T(8,128)(2,1)S(1)}, u32[]{:S(2)}, u32[]{:S(2)}) collective-permute-start(bf16[160,768]{1,0:T(8,128)(2,1)S(1)} %get-tuple-element.22), channel_id=1, source_target_pairs={{0,12},{4,0},{8,4},{12,8},{1,13},{5,1},{9,5},{13,9},{2,14},{6,2},{... | collective-permute-start | bytes 737288 | tf_op jit(solution)/shard_map/ppermute | solution.py:206
  29.1 9.2 %collective-permute-start.4 = (bf16[160,768]{1,0:T(8,128)(2,1)}, bf16[160,768]{1,0:T(8,128)(2,1)}, u32[]{:S(2)}, u32[]{:S(2)}) collective-permute-start(bf16[160,768]{1,0:T(8,128)(2,1)} %collective-permute-done.3.refs_0_), channel_id=1, source_target_pairs={{0,2},{1,3},{2,0},{3,1},{4,6},{5,7},{6,4},{7,5},{8,10},{9,11},{10,... | collective-permute-start | bytes 737288 | tf_op jit(solution)/shard_map/ppermute | solution.py:209
  30.9 10.3 %collective-permute-start.8 = (bf16[160,768]{1,0:T(8,128)(2,1)S(1)}, bf16[160,768]{1,0:T(8,128)(2,1)}, u32[]{:S(2)}, u32[]{:S(2)}) collective-permute-start(bf16[160,768]{1,0:T(8,128)(2,1)S(1)} %collective-permute-done.7.refs_0_), channel_id=1, source_target_pairs={{0,2},{1,3},{2,0},{3,1},{4,6},{5,7},{6,4},{7,5},{8,10},{9,11},{10,... | collective-permute-start | bytes 737288 | tf_op jit(solution)/shard_map/ppermute | solution.py:209
  32.9 27.9 %collective-permute-start = (bf16[2,256,2,2,128]{4,3,2,1,0:T(2,128)(2,1)}, bf16[2,256,2,2,128]{4,3,2,1,0:T(2,128)(2,1)S(1)}, u32[]{:S(2)}, u32[]{:S(2)}) collective-permute-start(bf16[2,256,2,2,128]{4,3,2,1,0:T(2,128)(2,1)} %get-tuple-element.15), channel_id=1, source_target_pairs={{0,4},{4,8},{8,12},{12,0},{1,5},{5,9},{9,13},{13,1},{2,6},{6,10},{... | collective-permute-start | bytes 1572872 | tf_op jit(solution)/shard_map/ppermute | solution.py:206
  37.4 23.9 %collective-permute-start.2 = (bf16[2,256,2,2,128]{4,3,2,1,0:T(2,128)(2,1)}, bf16[2,256,2,2,128]{4,3,2,1,0:T(2,128)(2,1)S(1)}, u32[]{:S(2)}, u32[]{:S(2)}) collective-permute-start(bf16[2,256,2,2,128]{4,3,2,1,0:T(2,128)(2,1)} %get-tuple-element.17), channel_id=1, source_target_pairs={{0,12},{4,0},{8,4},{12,8},{1,13},{5,1},{9,5},{13,9},{2,14},{6,2},{... | collective-permute-start | bytes 1572872 | tf_op jit(solution)/shard_map/ppermute | solution.py:206
  37.4 4.5 %collective-permute-start.9 = (bf16[160,768]{1,0:T(8,128)(2,1)S(1)}, bf16[160,768]{1,0:T(8,128)(2,1)S(1)}, u32[]{:S(2)}, u32[]{:S(2)}) collective-permute-start(bf16[160,768]{1,0:T(8,128)(2,1)S(1)} %collective-permute-done.7.refs_0_), channel_id=1, source_target_pairs={{0,1},{1,0},{2,3},{3,2},{4,5},{5,4},{6,7},{7,6},{8,9},{9,8},{10,11... | collective-permute-start | bytes 737288 | tf_op jit(solution)/shard_map/ppermute | solution.py:209
  38.3 8.0 %collective-permute-start.12 = (bf16[160,768]{1,0:T(8,128)(2,1)S(1)}, bf16[160,768]{1,0:T(8,128)(2,1)}, u32[]{:S(2)}, u32[]{:S(2)}) collective-permute-start(bf16[160,768]{1,0:T(8,128)(2,1)S(1)} %collective-permute-done.11.refs_4_), channel_id=1, source_target_pairs={{0,2},{1,3},{2,0},{3,1},{4,6},{5,7},{6,4},{7,5},{8,10},{9,11},{10,... | collective-permute-start | bytes 737288 | tf_op jit(solution)/shard_map/ppermute | solution.py:209
  41.2 5.1 %collective-permute-start.13 = (bf16[160,768]{1,0:T(8,128)(2,1)S(1)}, bf16[160,768]{1,0:T(8,128)(2,1)S(1)}, u32[]{:S(2)}, u32[]{:S(2)}) collective-permute-start(bf16[160,768]{1,0:T(8,128)(2,1)S(1)} %collective-permute-done.11.refs_4_), channel_id=1, source_target_pairs={{0,1},{1,0},{2,3},{3,2},{4,5},{5,4},{6,7},{7,6},{8,9},{9,8},{10,11... | collective-permute-start | bytes 737288 | tf_op jit(solution)/shard_map/ppermute | solution.py:209
  42.6 18.8 %collective-permute-start.10 = (bf16[160,768]{1,0:T(8,128)(2,1)}, bf16[160,768]{1,0:T(8,128)(2,1)}, u32[]{:S(2)}, u32[]{:S(2)}) collective-permute-start(bf16[160,768]{1,0:T(8,128)(2,1)} %collective-permute-done.8.refs_1_), channel_id=1, source_target_pairs={{0,1},{1,0},{2,3},{3,2},{4,5},{5,4},{6,7},{7,6},{8,9},{9,8},{10,11... | collective-permute-start | bytes 737288 | tf_op jit(solution)/shard_map/ppermute | solution.py:209
  46.3 15.2 %collective-permute-start.14 = (bf16[160,768]{1,0:T(8,128)(2,1)}, bf16[160,768]{1,0:T(8,128)(2,1)}, u32[]{:S(2)}, u32[]{:S(2)}) collective-permute-start(bf16[160,768]{1,0:T(8,128)(2,1)} %collective-permute-done.12.refs_5_), channel_id=1, source_target_pairs={{0,1},{1,0},{2,3},{3,2},{4,5},{5,4},{6,7},{7,6},{8,9},{9,8},{10,11... | collective-permute-start | bytes 737288 | tf_op jit(solution)/shard_map/ppermute | solution.py:209
  47.0 45.0 %collective-permute-start.1 = (bf16[2,256,2,2,128]{4,3,2,1,0:T(2,128)(2,1)}, bf16[2,256,2,2,128]{4,3,2,1,0:T(2,128)(2,1)}, u32[]{:S(2)}, u32[]{:S(2)}) collective-permute-start(bf16[2,256,2,2,128]{4,3,2,1,0:T(2,128)(2,1)} %get-tuple-element.16), channel_id=1, source_target_pairs={{0,8},{4,12},{8,0},{12,4},{1,9},{5,13},{9,1},{13,5},{2,10},{6,14},... | collective-permute-start | bytes 1572872 | tf_op jit(solution)/shard_map/ppermute | solution.py:206
  60.7 24.2 %copy-start.15 = (s32[2,80]{1,0:T(2,128)S(1)}, s32[2,80]{1,0:T(2,128)}, u32[]{:S(2)}) copy-start(s32[2,80]{1,0:T(2,128)} %param.10) | copy-start | bytes 1924
  60.7 24.2 %copy-start.16 = (s32[1,4]{1,0:T(1,128)S(1)}, s32[1,4]{1,0:T(1,128)}, u32[]{:S(2)}) copy-start(s32[1,4]{1,0:T(1,128)} %param.8) | copy-start | bytes 52
  60.8 24.5 %collective-permute-start.5 = (bf16[160,768]{1,0:T(8,128)(2,1)}, bf16[160,768]{1,0:T(8,128)(2,1)}, u32[]{:S(2)}, u32[]{:S(2)}) collective-permute-start(bf16[160,768]{1,0:T(8,128)(2,1)} %collective-permute-done.3.refs_0_), channel_id=1, source_target_pairs={{0,1},{1,0},{2,3},{3,2},{4,5},{5,4},{6,7},{7,6},{8,9},{9,8},{10,11... | collective-permute-start | bytes 737288 | tf_op jit(solution)/shard_map/ppermute | solution.py:209
  61.4 24.0 %collective-permute-start.6 = (bf16[160,768]{1,0:T(8,128)(2,1)}, bf16[160,768]{1,0:T(8,128)(2,1)}, u32[]{:S(2)}, u32[]{:S(2)}) collective-permute-start(bf16[160,768]{1,0:T(8,128)(2,1)} %collective-permute-done.4.refs_1_), channel_id=1, source_target_pairs={{0,1},{1,0},{2,3},{3,2},{4,5},{5,4},{6,7},{7,6},{8,9},{9,8},{10,11... | collective-permute-start | bytes 737288 | tf_op jit(solution)/shard_map/ppermute | solution.py:209
  61.4 2.8 %copy-start = (bf16[2,3072,512]{2,1,0:T(8,128)(2,1)S(1)}, bf16[2,3072,512]{2,1,0:T(8,128)(2,1)}, u32[]{:S(2)}) copy-start(bf16[2,3072,512]{2,1,0:T(8,128)(2,1)} %reshape.51.refs_5_.refs_8_) | copy-start | bytes 18874372
  71.1 22.5 %collective-permute-start.16 = (f32[2,80,512]{2,1,0:T(8,128)}, f32[2,80,512]{2,1,0:T(8,128)S(1)}, u32[]{:S(2)}, u32[]{:S(2)}) collective-permute-start(f32[2,80,512]{2,1,0:T(8,128)} %get-tuple-element.25), channel_id=1, source_target_pairs={{0,4},{4,0},{8,12},{12,8},{1,5},{5,1},{9,13},{13,9},{2,6},{6,2},{1... | collective-permute-start | bytes 983048 | tf_op jit(solution)/shard_map/ppermute | solution.py:209
  85.3 21.1 %collective-permute-start.15 = (f32[2,80,512]{2,1,0:T(8,128)}, f32[2,80,512]{2,1,0:T(8,128)S(1)}, u32[]{:S(2)}, u32[]{:S(2)}) collective-permute-start(f32[2,80,512]{2,1,0:T(8,128)} %copy-done.14), channel_id=1, source_target_pairs={{0,4},{4,0},{8,12},{12,8},{1,5},{5,1},{9,13},{13,9},{2,6},{6,2},{1... | collective-permute-start | bytes 983048 | tf_op jit(solution)/shard_map/ppermute | solution.py:209
  89.4 8.3 %copy-start.17 = (s32[1,4]{1,0:T(1,128)S(1)}, s32[1,4]{1,0:T(1,128)}, u32[]{:S(2)}) copy-start(s32[1,4]{1,0:T(1,128)} %param.9) | copy-start | bytes 52
  93.7 17.1 %collective-permute-start.17 = (f32[2,80,512]{2,1,0:T(8,128)S(1)}, f32[2,80,512]{2,1,0:T(8,128)S(1)}, u32[]{:S(2)}, u32[]{:S(2)}) collective-permute-start(f32[2,80,512]{2,1,0:T(8,128)S(1)} %shard_map.90), channel_id=1, source_target_pairs={{0,8},{4,12},{8,0},{12,4},{1,9},{5,13},{9,1},{13,5},{2,10},{6,14},... | collective-permute-start | bytes 983048 | tf_op jit(solution)/shard_map/ppermute | solution.py:206
  (12 other events, 13.6 us)

commit v4 on v3

--- a/solution.py
+++ b/solution.py
@@ -20,19 +20,36 @@
 
 
 def norm_kernel(at, rows_ref, gain_ref, *refs):
-    own, outs, held = refs[0], refs[1:-1], refs[-1]
-    rows = rows_ref[...].astype(jnp.float32)
-    held[...] = lax.rsqrt(jnp.mean(rows * rows, axis=1, keepdims=True) + 1e-05)
-    layer = pl.program_id(0) // (pl.num_programs(0) // gain_ref.shape[0])
-    for i, out in enumerate((own,) + outs):
-        columns = pl.ds(pl.multiple_of(at[i], 128), out.shape[1])
+    outs, (held, sems) = refs[:-2], refs[-2:]
+    step, rec = pl.program_id(0), outs[0].shape[0]
+    total = rows_ref.shape[0]
+
+    def fetch(i):
+        rows = pl.ds(i * ROWS, ROWS)
+        return pltpu.make_async_copy(rows_ref.at[rows], held.at[rows], sems.at[i])
+
+    @pl.when(step == 0)
+    def _():
+        for i in range(total // ROWS):
+            fetch(i).start()
+
+    def gain_of(columns):
         gain = gain_ref[0:1, columns].astype(jnp.float32)
         for other in range(1, gain_ref.shape[0]):
             gain = jnp.where(
-                layer == other, gain_ref[other : other + 1, columns].astype(jnp.float32), gain
+                step == other, gain_ref[other : other + 1, columns].astype(jnp.float32), gain
             )
-        part = rows_ref[:, columns].astype(jnp.float32)
-        out[...] = (part * held[...] * gain).astype(jnp.bfloat16)
+        return gain
+
+    columns = [pl.ds(pl.multiple_of(at[i], 128), out.shape[1]) for i, out in enumerate(outs)]
+    for i in range(rec // ROWS):
+        fetch(step * (rec // ROWS) + i).wait()
+        here = pl.ds(pl.multiple_of(step * rec + i * ROWS, ROWS), ROWS)
+        rows = held[here].astype(jnp.float32)
+        scale = lax.rsqrt(jnp.mean(rows * rows, axis=1, keepdims=True) + 1e-05)
+        for out, column in zip(outs, columns):
+            part = held[here, column].astype(jnp.float32)
+            out[i * ROWS : (i + 1) * ROWS] = (part * scale * gain_of(column)).astype(jnp.bfloat16)
 
 
 def normed_shares(hidden, gain, me, share, n, feats, part):
@@ -44,64 +61,92 @@
         norm_kernel,
         grid_spec=pltpu.PrefetchScalarGridSpec(
             num_scalar_prefetch=1,
-            grid=(rows // ROWS,),
-            in_specs=[
-                pl.BlockSpec((ROWS, width), lambda i, at: (i, 0)),
-                pl.BlockSpec(gain.shape, lambda i, at: (0, 0)),
+            grid=(layers,),
+            in_specs=[HBM, pl.BlockSpec(gain.shape, lambda i, at: (0, 0))],
+            out_specs=[pl.BlockSpec((rec, size), lambda i, at: (i, 0)) for size in sizes],
+            scratch_shapes=[
+                pltpu.VMEM((rows, width), jnp.bfloat16),
+                pltpu.SemaphoreType.DMA((rows // ROWS,)),
             ],
-            out_specs=[pl.BlockSpec((ROWS, size), lambda i, at: (i, 0)) for size in sizes],
-            scratch_shapes=[pltpu.VMEM((ROWS, 1), jnp.float32)],
         ),
         out_shape=[jax.ShapeDtypeStruct((rows, size), jnp.bfloat16) for size in sizes],
         compiler_params=PARAMS,
     )(at.astype(jnp.int32), hidden.reshape(rows, width), gain)
 
 
-def pick_kernel(at, store, *refs):
+def tie_kernel(*refs):
+    pass
+
+
+def tie(value, *after):
+    return pl.pallas_call(
+        tie_kernel,
+        in_specs=[HBM] * (1 + len(after)),
+        out_specs=HBM,
+        out_shape=jax.ShapeDtypeStruct(value.shape, value.dtype),
+        input_output_aliases={0: 0},
+        compiler_params=PARAMS,
+    )(value, *after)
+
+
+def pick_kernel(wanted, at, store, *refs):
     outs, sems = refs[:-1], refs[-1]
-    copies = [
-        pltpu.make_async_copy(store.at[:, at[i]], out, sems.at[i]) for i, out in enumerate(outs)
-    ]
+    copies = []
+    for i, (out, (k, layer)) in enumerate(zip(outs, wanted)):
+        layers = pl.ds(0, out.shape[0]) if layer is None else pl.ds(layer, 1)
+        copies.append(pltpu.make_async_copy(store.at[layers, at[k]], out, sems.at[i]))
     for copy in copies:
         copy.start()
     for copy in copies:
         copy.wait()
 
 
-def pick(store, at):
-    shape = store.shape[:1] + store.shape[2:]
-    return pl.pallas_call(
-        pick_kernel,
+def pick(store, at, wanted):
+    shapes = [
+        (store.shape[0] if layer is None else 1,) + store.shape[2:] for _, layer in wanted
+    ]
+    return pl.pallas_call(
+        functools.partial(pick_kernel, wanted),
         grid_spec=pltpu.PrefetchScalarGridSpec(
             num_scalar_prefetch=1,
             grid=(),
             in_specs=[HBM],
-            out_specs=[HBM] * len(at),
-            scratch_shapes=[pltpu.SemaphoreType.DMA((len(at),))],
+            out_specs=[HBM] * len(wanted),
+            scratch_shapes=[pltpu.SemaphoreType.DMA((len(wanted),))],
         ),
-        out_shape=[jax.ShapeDtypeStruct(shape, store.dtype)] * len(at),
+        out_shape=[jax.ShapeDtypeStruct(shape, store.dtype) for shape in shapes],
         compiler_params=PARAMS,
     )(jnp.stack(at).astype(jnp.int32), store)
 
 
 def product_kernel(counts, at, *refs):
-    shares, refs = refs[: sum(counts)], refs[sum(counts) :]
-    weight, refs = refs[0], refs[1:]
-    held, outs = refs[-1], refs[-1 - len(counts) : -1]
+    shares, weight = refs[: sum(counts)], refs[sum(counts)]
+    held, loaded, sems = refs[-3:]
+    outs = refs[-3 - len(counts) : -3]
     layers, rec, _ = outs[0].shape
-    base = 0
-    for i, count in enumerate(counts):
-        row = pl.multiple_of(at[i] * rec, 16)
-        for j in range(count):
-            piece = shares[base + j]
-            column = pl.multiple_of(at[len(counts) + base + j], 128)
-            for layer in range(layers):
-                held[layer, pl.ds(row, rec), pl.ds(column, piece.shape[1])] = piece[
-                    layer * rec : (layer + 1) * rec
-                ]
-        base += count
+    weights = [
+        pltpu.make_async_copy(weight.at[layer], loaded.at[layer], sems.at[0, layer])
+        for layer in range(layers)
+    ]
+    placed = [[] for _ in range(layers)]
+    blocks = [i for i, count in enumerate(counts) for _ in range(count)]
     for layer in range(layers):
-        result = jnp.dot(held[layer], weight[layer], preferred_element_type=jnp.float32)
+        for j, (share, i) in enumerate(zip(shares, blocks)):
+            row = pl.ds(pl.multiple_of(at[i] * rec, 16), rec)
+            column = pl.ds(pl.multiple_of(at[len(counts) + j], 128), share.shape[1])
+            placed[layer].append(
+                pltpu.make_async_copy(
+                    share.at[layer * rec : (layer + 1) * rec],
+                    held.at[layer, row, column],
+                    sems.at[1 + j, layer],
+                )
+            )
+        for copy in placed[layer] + [weights[layer]]:
+            copy.start()
+    for layer in range(layers):
+        for copy in placed[layer] + [weights[layer]]:
+            copy.wait()
+        result = jnp.dot(held[layer], loaded[layer], preferred_element_type=jnp.float32)
         for i, out in enumerate(outs):
             out[layer] = result[i * rec : (i + 1) * rec]
 
@@ -113,10 +158,14 @@
     flat = [share for block in blocks for share in block]
     return pl.pallas_call(
         functools.partial(product_kernel, counts),
-        in_specs=[SMEM] + [VMEM] * (len(flat) + 1) + [HBM] * len(after),
+        in_specs=[SMEM] + [HBM] * (len(flat) + 1 + len(after)),
         out_specs=[VMEM] * len(blocks),
         out_shape=[jax.ShapeDtypeStruct((layers, rec, cols), jnp.float32)] * len(blocks),
-        scratch_shapes=[pltpu.VMEM((layers, len(blocks) * rec, feats), jnp.bfloat16)],
+        scratch_shapes=[
+            pltpu.VMEM((layers, len(blocks) * rec, feats), jnp.bfloat16),
+            pltpu.VMEM((layers, feats, cols), jnp.bfloat16),
+            pltpu.SemaphoreType.DMA((1 + len(flat), layers)),
+        ],
         compiler_params=PARAMS,
     )(at, *flat, weight, *after)
 
@@ -138,21 +187,28 @@
     )(*left, *right, *after)
 
 
-def unite_kernel(n, starts, lengths, spots, *refs):
-    pages, fresh, out, sums, held = refs[:n], refs[n], refs[n + 1], refs[n + 2], refs[n + 3]
+def unite_kernel(counts, starts, lengths, spots, *refs):
+    total = sum(counts)
+    fresh, out, sums, held = refs[total:]
     layers, rec = fresh.shape[:2]
-    for slot, page in enumerate(pages):
+    base = 0
+    for slot, count in enumerate(counts):
+        pages = refs[base : base + count]
+        base += count
         start, length = starts[slot], lengths[slot]
         whole = length // CHUNK
 
-        def many(i, carry, page=page, start=start):
+        def rows_of(layer, pages=pages):
+            return pages[0].at[layer] if len(pages) == 1 else pages[layer].at[0]
+
+        def many(i, carry, rows_of=rows_of, start=start):
             for layer in range(layers):
-                out[layer, pl.ds(start + i * CHUNK, CHUNK)] = page[layer, pl.ds(i * CHUNK, CHUNK)]
+                out[layer, pl.ds(start + i * CHUNK, CHUNK)] = rows_of(layer)[pl.ds(i * CHUNK, CHUNK)]
             return carry
 
-        def one(i, carry, page=page, start=start):
+        def one(i, carry, rows_of=rows_of, start=start):
             for layer in range(layers):
-                out[layer, start + i] = page[layer, i]
+                out[layer, start + i] = rows_of(layer)[i]
             return carry
 
         lax.fori_loop(0, whole, many, 0)
@@ -185,12 +241,13 @@
 
 
 def unite(pages, fresh, starts, lengths, spots):
-    n = len(pages)
+    counts = tuple(len(page) for page in pages)
+    flat = [piece for page in pages for piece in page]
     layers, rec = fresh.shape[:2]
     row = fresh.shape[2:]
     return pl.pallas_call(
-        functools.partial(unite_kernel, n),
-        in_specs=[SMEM] * 3 + [VMEM] * (n + 1),
+        functools.partial(unite_kernel, counts),
+        in_specs=[SMEM] * 3 + [VMEM] * (len(flat) + 1),
         out_specs=[VMEM, VMEM],
         out_shape=[
             jax.ShapeDtypeStruct((layers, PROMPT_PER_HOLD) + row, fresh.dtype),
@@ -198,7 +255,7 @@
         ],
         scratch_shapes=[pltpu.VMEM((2 * layers * rec, row[-1]), jnp.float32)],
         compiler_params=PARAMS,
-    )(starts, lengths, spots, *pages, fresh)
+    )(starts, lengths, spots, *flat, fresh)
 
 
 def make_local(n, tps):
@@ -223,14 +280,19 @@
         part = feats // cuts
         share = my_tp % cuts
 
+        wanted = [(k, None) for k in odds] + [(k, layer) for k in evens for layer in range(LAYERS)]
+        sent = pick(cache_store, [(me + k) % n for k in range(n)], wanted)
+        pages = {k: [] for k in range(n)}
+        for (k, _), page in zip(wanted, sent):
+            pages[k].append(shift(page, k))
+        pages[0] = [lax.dynamic_index_in_dim(cache_store, me, axis=1, keepdims=False)]
+
         own, *pieces = normed_shares(hidden, norm_gain, me, share, n, feats, part)
         arrived = {k: shift(pieces[k - 1], k) for k in odds + evens}
-
-        sent = pick(cache_store, [(me + k) % n for k in range(1, n)])
-        pages = {k: shift(sent[k - 1], k) for k in odds + evens}
-        pages[0] = lax.dynamic_index_in_dim(cache_store, me, axis=1, keepdims=False)
-
         weight = kv_weight.reshape(LAYERS, feats, cols)
+        arrived[odds[0]] = tie(arrived[odds[0]], weight, *pages[odds[0]])
+        early = [page for k in odds[1:] for page in pages[k]]
+        halves = [[pages[k][layer] for k in evens] for layer in range(LAYERS)]
 
         def everyone(piece):
             shares, masks, bit = [piece], [0], cuts // 2
@@ -244,7 +306,7 @@
         away = [everyone(arrived[k]) for k in odds]
         spot = [jnp.where(even, (k + 1) // 2 % (n // 2), (k - 1) // 2) for k in odds]
         away = products(
-            [a[0] for a in away], weight, spot, [a[1] for a in away], rec, [pages[k] for k in odds]
+            [a[0] for a in away], weight, spot, [a[1] for a in away], rec, early
         )
         theirs = [swap(away[i % (n // 2)], "hold", n, 1) for i in range(1, n // 2 + 1)]
         mine = [everyone(arrived[k]) for k in range(2, n, 2)] + [([own], [jnp.int32(0)])]
@@ -254,11 +316,11 @@
             [jnp.int32(i) for i in range(n // 2)],
             [a[1] for a in mine],
             rec,
-            [],
+            halves[0],
         )
         total = mine[-1] + theirs[-1]
         if n > 2:
-            pairs = add_pairs(mine[:-1], theirs[:-1], [pages[k] for k in evens])
+            pairs = add_pairs(mine[:-1], theirs[:-1], halves[1])
             for k, pair in zip(range(2, n, 2), pairs):
                 total = total + shift(pair, -k)
         fresh = total.astype(jnp.bfloat16).reshape(LAYERS, rec, heads_here, 2, head_size)

time: 123 us -> 123 us (level)
  starting transfers between devices: 38.1 us -> 29.7 us
  waiting for transfers between devices: 32.9 us -> 38.6 us
  Pallas kernels: 15.2 us -> 17.6 us
    ppermute x11, starting transfers between devices: 18.1 us -> 5.63 us  [swap(): return lax.ppermute(value, axis, [(i, i ^ bit) for i in range(size)])]
    ppermute x7 -> x8, starting transfers between devices: 20 us -> 24.1 us  [shift(): return lax.ppermute(value, 'hold', [(i, (i + k) % n) for i in range(n)])]
    ppermute x11, waiting for transfers between devices: 14.6 us -> 18.5 us  [swap(): return lax.ppermute(value, axis, [(i, i ^ bit) for i in range(size)])]
    pallas_call x1, Pallas kernels: 3.81 us -> 5.85 us  [normed_shares(): pl.pallas_call(norm_kernel, grid_spec=pltpu.PrefetchScalarGridSpec(num_sc...]
    ppermute x7 -> x8, waiting for transfers between devices: 18.3 us -> 20.1 us  [shift(): return lax.ppermute(value, 'hold', [(i, (i + k) % n) for i in range(n)])]
    pallas_call x2 -> x3, Pallas kernels: 5.37 us -> 4.62 us  [the longest x1 3.21 us: unite(): pl.pallas_call(functools.partial(unite_kernel, counts), in_specs=[SMEM] *...]
    unnamed x36 -> x30, local copies, waits for them, and re-layouts: 16.4 us -> 16.6 us
  transfers between devices with their start and end apart: 18 -> 19, of which waited for: 8 -> 7; matrix products, arithmetic and copies ran while one was open for 10% -> 10% of each run, Pallas kernels for 6% -> 11%
where the time goes in v4:
time: 123 us
  waiting for transfers between devices  38.6 us (31%)
  starting transfers between devices  29.7 us (24%)
  local copies, waits for them, and re-layouts  29.1 us (24%)
  Pallas kernels  17.6 us (14%)
  blocking collectives  6.17 us (5%)
    ppermute x8, starting transfers between devices, shift(): return lax.ppermute(value, 'hold', [(i, (i + k) % n) for i in range(n)])  24.1 us
    ppermute x8, waiting for transfers between devices, shift(): return lax.ppermute(value, 'hold', [(i, (i + k) % n) for i in range(n)])  20.1 us
    ppermute x11, waiting for transfers between devices, swap(): return lax.ppermute(value, axis, [(i, i ^ bit) for i in range(size)])  18.5 us
    unnamed x30, local copies, waits for them, and re-layouts  16.6 us
    reshape x1, local copies, waits for them, and re-layouts, local(): weight = kv_weight.reshape(LAYERS, feats, cols)  10.1 us
    pallas_call x2, Pallas kernels, products(): pl.pallas_call(functools.partial(product_kernel, counts), in_specs=[SMEM]...  7.1 us
    psum x1, blocking collectives, local(): sums = lax.psum(sums, 'tp').reshape(2, LAYERS, rec)  6.17 us
    pallas_call x1, Pallas kernels, normed_shares(): pl.pallas_call(norm_kernel, grid_spec=pltpu.PrefetchScalarGridSpec(num_sc...  5.85 us
  transfers between devices with their start and end apart: 19, of which 7 were waited for; matrix products, arithmetic and copies ran while one was open for 10% of the time, Pallas kernels for 11%

profile of v4, /device:TPU:0, one launch (start us, length us, event | category | flops | bytes accessed | tf_op | source)
XLA Modules:
  0.0 122.8 jit_solution(17433341619239401510)
XLA Ops:
  0.8 1.6 %copy-done.4 = bf16[2,4,256,2,2,128]{5,4,3,2,1,0:T(2,128)(2,1)S(1)} copy-done((bf16[2,4,256,2,2,128]{5,4,3,2,1,0:T(2,128)(2,1)S(1)}, bf16[2,4,256,2,2,128]{5,4,3,2,1,0:T(2,128)(2,1)}, u32[]{:S(2)}) %copy-start.4) | copy-done | bytes 2097176
  5.2 3.0 %collective-permute-start = (bf16[2,256,2,2,128]{4,3,2,1,0:T(2,128)(2,1)S(1)}, bf16[2,256,2,2,128]{4,3,2,1,0:T(2,128)(2,1)S(1)}, u32[]{:S(2)}, u32[]{:S(2)}) collective-permute-start(bf16[2,256,2,2,128]{4,3,2,1,0:T(2,128)(2,1)S(1)} %get-tuple-element.16), channel_id=1, source_target_pairs={{0,4},{4,8},{8,12},{12,0},{1,5},{5,9},{9,13},{13,1},{2,6},{6,10},{... | collective-permute-start | bytes 1572872 | tf_op jit(solution)/shard_map/ppermute | solution.py:263
  8.3 2.1 %copy-done.3 = bf16[2,80,12288]{2,1,0:T(8,128)(2,1)S(1)} copy-done((bf16[2,80,12288]{2,1,0:T(8,128)(2,1)S(1)}, bf16[2,80,12288]{2,1,0:T(8,128)(2,1)}, u32[]{:S(2)}) %copy-start.3) | copy-done | bytes 3932184
  11.2 5.8 %shard_map.87 = (bf16[160,3072]{1,0:T(8,128)(2,1)S(1)}, bf16[160,768]{1,0:T(8,128)(2,1)S(1)}, bf16[160,768]{1,0:T(8,128)(2,1)}, bf16[160,768]{1,0:T(8,128)(2,1)}) custom-call(s32[4]{0:T(128)S(1)} %pad_add_fusion.1.at, bf16[160,12288]{1,0:T(8,128)(2,1)S(1)} %bitcast.21, bf16[2,12288]{1,0:T(2,128)(2,1)S(1)} %copy-done.7), custom_call_target="tpu_custom_call" | custom-call | tf_op jit(solution)/shard_map/pallas_call | solution.py:60
  17.0 2.7 %collective-permute-start.4 = (bf16[160,768]{1,0:T(8,128)(2,1)}, bf16[160,768]{1,0:T(8,128)(2,1)S(1)}, u32[]{:S(2)}, u32[]{:S(2)}) collective-permute-start(bf16[160,768]{1,0:T(8,128)(2,1)} %get-tuple-element.20), channel_id=1, source_target_pairs={{0,8},{4,12},{8,0},{12,4},{1,9},{5,13},{9,1},{13,5},{2,10},{6,14},... | collective-permute-start | bytes 737288 | tf_op jit(solution)/shard_map/ppermute | solution.py:263
  21.7 3.1 %collective-permute-start.3 = (bf16[2,256,2,2,128]{4,3,2,1,0:T(2,128)(2,1)}, bf16[2,256,2,2,128]{4,3,2,1,0:T(2,128)(2,1)S(1)}, u32[]{:S(2)}, u32[]{:S(2)}) collective-permute-start(bf16[2,256,2,2,128]{4,3,2,1,0:T(2,128)(2,1)} %get-tuple-element.19), channel_id=1, source_target_pairs={{0,12},{4,0},{8,4},{12,8},{1,13},{5,1},{9,5},{13,9},{2,14},{6,2},{... | collective-permute-start | bytes 1572872 | tf_op jit(solution)/shard_map/ppermute | solution.py:263
  24.9 10.1 %reshape.51.refs_5_.refs_1_.refs_8_ = bf16[2,3072,512]{2,1,0:T(8,128)(2,1)} reshape(bf16[2,3072,2,2,128]{4,3,2,1,0:T(2,128)(2,1)} %param.13) | data formatting | bytes 12582912 | tf_op jit(solution)/shard_map/reshape | solution.py:292
  35.0 1.5 %collective-permute-start.5 = (bf16[160,768]{1,0:T(8,128)(2,1)S(1)}, bf16[160,768]{1,0:T(8,128)(2,1)}, u32[]{:S(2)}, u32[]{:S(2)}) collective-permute-start(bf16[160,768]{1,0:T(8,128)(2,1)S(1)} %collective-permute-done.4.refs_0_), channel_id=1, source_target_pairs={{0,2},{1,3},{2,0},{3,1},{4,6},{5,7},{6,4},{7,5},{8,10},{9,11},{10,... | collective-permute-start | bytes 737288 | tf_op jit(solution)/shard_map/ppermute | solution.py:266
  36.5 2.7 %collective-permute-done.12.refs_4_ = bf16[160,768]{1,0:T(8,128)(2,1)S(1)} collective-permute-done((bf16[160,768]{1,0:T(8,128)(2,1)}, bf16[160,768]{1,0:T(8,128)(2,1)S(1)}, u32[]{:S(2)}, u32[]{:S(2)}) %collective-permute-start.12) | collective-permute-done | bytes 245792 | tf_op jit(solution)/shard_map/ppermute | solution.py:263
  39.2 1.5 %collective-permute-start.13 = (bf16[160,768]{1,0:T(8,128)(2,1)S(1)}, bf16[160,768]{1,0:T(8,128)(2,1)}, u32[]{:S(2)}, u32[]{:S(2)}) collective-permute-start(bf16[160,768]{1,0:T(8,128)(2,1)S(1)} %collective-permute-done.12.refs_4_), channel_id=1, source_target_pairs={{0,2},{1,3},{2,0},{3,1},{4,6},{5,7},{6,4},{7,5},{8,10},{9,11},{10,... | collective-permute-start | bytes 737288 | tf_op jit(solution)/shard_map/ppermute | solution.py:266
  40.7 2.8 %copy-done = bf16[2,3072,512]{2,1,0:T(8,128)(2,1)S(1)} copy-done((bf16[2,3072,512]{2,1,0:T(8,128)(2,1)S(1)}, bf16[2,3072,512]{2,1,0:T(8,128)(2,1)}, u32[]{:S(2)}) %copy-start) | copy-done | bytes 6291480
  44.1 5.2 %collective-permute-done.13.refs_5_ = bf16[160,768]{1,0:T(8,128)(2,1)} collective-permute-done((bf16[160,768]{1,0:T(8,128)(2,1)S(1)}, bf16[160,768]{1,0:T(8,128)(2,1)}, u32[]{:S(2)}, u32[]{:S(2)}) %collective-permute-start.13) | collective-permute-done | bytes 245792 | tf_op jit(solution)/shard_map/ppermute | solution.py:266
  49.8 2.2 %collective-permute-done.9.refs_1_ = bf16[160,768]{1,0:T(8,128)(2,1)} collective-permute-done((bf16[160,768]{1,0:T(8,128)(2,1)S(1)}, bf16[160,768]{1,0:T(8,128)(2,1)}, u32[]{:S(2)}, u32[]{:S(2)}) %collective-permute-start.9) | collective-permute-done | bytes 245792 | tf_op jit(solution)/shard_map/ppermute | solution.py:266
  52.7 13.1 %collective-permute-start.1 = (bf16[1,256,2,2,128]{4,3,2,1,0:T(2,128)(2,1)}, bf16[1,256,2,2,128]{4,3,2,1,0:T(2,128)(2,1)S(1)}, u32[]{:S(2)}, u32[]{:S(2)}) collective-permute-start(bf16[1,256,2,2,128]{4,3,2,1,0:T(2,128)(2,1)} %copy-done.11), channel_id=1, source_target_pairs={{0,8},{4,12},{8,0},{12,4},{1,9},{5,13},{9,1},{13,5},{2,10},{6,14},... | collective-permute-start | bytes 786440 | tf_op jit(solution)/shard_map/ppermute | solution.py:263
  66.5 2.8 %copy-done.1 = bf16[2,3072,512]{2,1,0:T(8,128)(2,1)S(1)} copy-done((bf16[2,3072,512]{2,1,0:T(8,128)(2,1)S(1)}, bf16[2,3072,512]{2,1,0:T(8,128)(2,1)}, u32[]{:S(2)}) %copy-start.1) | copy-done | bytes 6291480
  70.2 4.0 %shard_map.90 = (f32[2,80,512]{2,1,0:T(8,128)S(1)}, f32[2,80,512]{2,1,0:T(8,128)}) custom-call(s32[10]{0:T(128)S(1)} %stack.79.at, bf16[160,768]{1,0:T(8,128)(2,1)S(1)} %shard_map.89.refs_0_, bf16[160,768]{1,0:T(8,128)(2,1)} %collective-permute-done.9.refs_1_, bf16[160,768]{1,0:T(8,128)(2,1)} %collective-permute-done.10.refs_2_, ...), custom_call_target="tpu_custom_call" | custom-call | tf_op jit(solution)/shard_map/pallas_call | solution.py:159
  76.3 8.3 %collective-permute-done.1.refs_6_.refs_2_ = bf16[1,256,2,2,128]{4,3,2,1,0:T(2,128)(2,1)S(1)} collective-permute-done((bf16[1,256,2,2,128]{4,3,2,1,0:T(2,128)(2,1)}, bf16[1,256,2,2,128]{4,3,2,1,0:T(2,128)(2,1)S(1)}, u32[]{:S(2)}, u32[]{:S(2)}) %collective-permute-start.1) | collective-permute-done | bytes 262176 | tf_op jit(solution)/shard_map/ppermute | solution.py:263
  84.6 2.8 %copy-done.2 = bf16[2,3072,512]{2,1,0:T(8,128)(2,1)S(1)} copy-done((bf16[2,3072,512]{2,1,0:T(8,128)(2,1)S(1)}, bf16[2,3072,512]{2,1,0:T(8,128)(2,1)}, u32[]{:S(2)}) %copy-start.2) | copy-done | bytes 6291480
  87.4 3.1 %shard_map.88 = (f32[2,80,512]{2,1,0:T(8,128)S(1)}, f32[2,80,512]{2,1,0:T(8,128)S(1)}) custom-call(s32[7]{0:T(128)S(1)} %stack.71.at, bf16[160,768]{1,0:T(8,128)(2,1)S(1)} %collective-permute-done.4.refs_0_, bf16[160,768]{1,0:T(8,128)(2,1)} %collective-permute-done.5.refs_1_, bf16[160,768]{1,0:T(8,128)(2,1)} %collective-permute-done.6.refs_2_, ...), custom_call_target="tpu_custom_call" | custom-call | tf_op jit(solution)/shard_map/pallas_call | solution.py:159
  90.6 5.9 %collective-permute-done.17.refs_1_ = f32[2,80,512]{2,1,0:T(8,128)S(1)} collective-permute-done((f32[2,80,512]{2,1,0:T(8,128)}, f32[2,80,512]{2,1,0:T(8,128)S(1)}, u32[]{:S(2)}, u32[]{:S(2)}) %collective-permute-start.17) | collective-permute-done | bytes 327712 | tf_op jit(solution)/shard_map/ppermute | solution.py:266
  98.3 5.2 %collective-permute-done.16 = f32[2,80,512]{2,1,0:T(8,128)S(1)} collective-permute-done((f32[2,80,512]{2,1,0:T(8,128)S(1)}, f32[2,80,512]{2,1,0:T(8,128)S(1)}, u32[]{:S(2)}, u32[]{:S(2)}) %collective-permute-start.16) | collective-permute-done | bytes 327712 | tf_op jit(solution)/shard_map/ppermute | solution.py:266
  103.5 9.0 %collective-permute-done.18 = f32[2,80,512]{2,1,0:T(8,128)S(1)} collective-permute-done((f32[2,80,512]{2,1,0:T(8,128)S(1)}, f32[2,80,512]{2,1,0:T(8,128)S(1)}, u32[]{:S(2)}, u32[]{:S(2)}) %collective-permute-start.18) | collective-permute-done | bytes 327712 | tf_op jit(solution)/shard_map/ppermute | solution.py:263
  112.6 3.2 %shard_map.92 = (bf16[2,512,2,2,128]{4,3,2,1,0:T(2,128)(2,1)}, f32[1,320]{1,0:T(1,128)S(1)}) custom-call(s32[4]{0:T(128)S(1)} %get-tuple-element.31.starts, s32[4]{0:T(128)S(1)} %get-tuple-element.30.lengths, s32[160]{0:T(256)S(1)} %reshape.49.spots, bf16[2,256,2,2,128]{4,3,2,1,0:T(2,128)(2,1)S(1)} %dynamic-slice_bitcast_fusion.refs_0_, ...), custom_call_target="tpu_custom_call" | custom-call | tf_op jit(solution)/shard_map/pallas_call | solution.py:248
  115.8 6.2 %psum.7 = f32[1,320]{1,0:T(1,128)S(1)} all-reduce(f32[1,320]{1,0:T(1,128)S(1)} %get-tuple-element.29), channel_id=1, replica_groups=mesh['groups'=2,'hold'=4,'tp'=4] {'tp'}, use_global_device_ids=true, to_apply=%region_3.4 | all-reduce | flops 320 | bytes 2560 | tf_op jit(solution)/shard_map/psum | solution.py:338
  (68 shorter events, 13.9 us)
Async XLA Ops:
  5.2 35.6 %collective-permute-start = (bf16[2,256,2,2,128]{4,3,2,1,0:T(2,128)(2,1)S(1)}, bf16[2,256,2,2,128]{4,3,2,1,0:T(2,128)(2,1)S(1)}, u32[]{:S(2)}, u32[]{:S(2)}) collective-permute-start(bf16[2,256,2,2,128]{4,3,2,1,0:T(2,128)(2,1)S(1)} %get-tuple-element.16), channel_id=1, source_target_pairs={{0,4},{4,8},{8,12},{12,0},{1,5},{5,9},{9,13},{13,1},{2,6},{6,10},{... | collective-permute-start | bytes 1572872 | tf_op jit(solution)/shard_map/ppermute | solution.py:263
  17.0 18.0 %collective-permute-start.4 = (bf16[160,768]{1,0:T(8,128)(2,1)}, bf16[160,768]{1,0:T(8,128)(2,1)S(1)}, u32[]{:S(2)}, u32[]{:S(2)}) collective-permute-start(bf16[160,768]{1,0:T(8,128)(2,1)} %get-tuple-element.20), channel_id=1, source_target_pairs={{0,8},{4,12},{8,0},{12,4},{1,9},{5,13},{9,1},{13,5},{2,10},{6,14},... | collective-permute-start | bytes 737288 | tf_op jit(solution)/shard_map/ppermute | solution.py:263
  19.7 19.5 %collective-permute-start.12 = (bf16[160,768]{1,0:T(8,128)(2,1)}, bf16[160,768]{1,0:T(8,128)(2,1)S(1)}, u32[]{:S(2)}, u32[]{:S(2)}) collective-permute-start(bf16[160,768]{1,0:T(8,128)(2,1)} %get-tuple-element.24), channel_id=1, source_target_pairs={{0,12},{4,0},{8,4},{12,8},{1,13},{5,1},{9,5},{13,9},{2,14},{6,2},{... | collective-permute-start | bytes 737288 | tf_op jit(solution)/shard_map/ppermute | solution.py:263
  21.0 19.7 %collective-permute-start.8 = (bf16[160,768]{1,0:T(8,128)(2,1)S(1)}, bf16[160,768]{1,0:T(8,128)(2,1)S(1)}, u32[]{:S(2)}, u32[]{:S(2)}) collective-permute-start(bf16[160,768]{1,0:T(8,128)(2,1)S(1)} %get-tuple-element.23), channel_id=1, source_target_pairs={{0,4},{4,8},{8,12},{12,0},{1,5},{5,9},{9,13},{13,1},{2,6},{6,10},{... | collective-permute-start | bytes 737288 | tf_op jit(solution)/shard_map/ppermute | solution.py:263
  21.7 44.1 %collective-permute-start.3 = (bf16[2,256,2,2,128]{4,3,2,1,0:T(2,128)(2,1)}, bf16[2,256,2,2,128]{4,3,2,1,0:T(2,128)(2,1)S(1)}, u32[]{:S(2)}, u32[]{:S(2)}) collective-permute-start(bf16[2,256,2,2,128]{4,3,2,1,0:T(2,128)(2,1)} %get-tuple-element.19), channel_id=1, source_target_pairs={{0,12},{4,0},{8,4},{12,8},{1,13},{5,1},{9,5},{13,9},{2,14},{6,2},{... | collective-permute-start | bytes 1572872 | tf_op jit(solution)/shard_map/ppermute | solution.py:263
  35.0 14.3 %collective-permute-start.5 = (bf16[160,768]{1,0:T(8,128)(2,1)S(1)}, bf16[160,768]{1,0:T(8,128)(2,1)}, u32[]{:S(2)}, u32[]{:S(2)}) collective-permute-start(bf16[160,768]{1,0:T(8,128)(2,1)S(1)} %collective-permute-done.4.refs_0_), channel_id=1, source_target_pairs={{0,2},{1,3},{2,0},{3,1},{4,6},{5,7},{6,4},{7,5},{8,10},{9,11},{10,... | collective-permute-start | bytes 737288 | tf_op jit(solution)/shard_map/ppermute | solution.py:266
  39.2 10.0 %collective-permute-start.13 = (bf16[160,768]{1,0:T(8,128)(2,1)S(1)}, bf16[160,768]{1,0:T(8,128)(2,1)}, u32[]{:S(2)}, u32[]{:S(2)}) collective-permute-start(bf16[160,768]{1,0:T(8,128)(2,1)S(1)} %collective-permute-done.12.refs_4_), channel_id=1, source_target_pairs={{0,2},{1,3},{2,0},{3,1},{4,6},{5,7},{6,4},{7,5},{8,10},{9,11},{10,... | collective-permute-start | bytes 737288 | tf_op jit(solution)/shard_map/ppermute | solution.py:266
  43.5 8.4 %collective-permute-start.9 = (bf16[160,768]{1,0:T(8,128)(2,1)S(1)}, bf16[160,768]{1,0:T(8,128)(2,1)}, u32[]{:S(2)}, u32[]{:S(2)}) collective-permute-start(bf16[160,768]{1,0:T(8,128)(2,1)S(1)} %shard_map.89.refs_0_), channel_id=1, source_target_pairs={{0,2},{1,3},{2,0},{3,1},{4,6},{5,7},{6,4},{7,5},{8,10},{9,11},{10,... | collective-permute-start | bytes 737288 | tf_op jit(solution)/shard_map/ppermute | solution.py:266
  44.1 8.0 %collective-permute-start.14 = (bf16[160,768]{1,0:T(8,128)(2,1)S(1)}, bf16[160,768]{1,0:T(8,128)(2,1)S(1)}, u32[]{:S(2)}, u32[]{:S(2)}) collective-permute-start(bf16[160,768]{1,0:T(8,128)(2,1)S(1)} %collective-permute-done.12.refs_4_), channel_id=1, source_target_pairs={{0,1},{1,0},{2,3},{3,2},{4,5},{5,4},{6,7},{7,6},{8,9},{9,8},{10,11... | collective-permute-start | bytes 737288 | tf_op jit(solution)/shard_map/ppermute | solution.py:266
  49.3 16.7 %collective-permute-start.15 = (bf16[160,768]{1,0:T(8,128)(2,1)}, bf16[160,768]{1,0:T(8,128)(2,1)}, u32[]{:S(2)}, u32[]{:S(2)}) collective-permute-start(bf16[160,768]{1,0:T(8,128)(2,1)} %collective-permute-done.13.refs_5_), channel_id=1, source_target_pairs={{0,1},{1,0},{2,3},{3,2},{4,5},{5,4},{6,7},{7,6},{8,9},{9,8},{10,11... | collective-permute-start | bytes 737288 | tf_op jit(solution)/shard_map/ppermute | solution.py:266
  49.3 16.9 %collective-permute-start.10 = (bf16[160,768]{1,0:T(8,128)(2,1)S(1)}, bf16[160,768]{1,0:T(8,128)(2,1)}, u32[]{:S(2)}, u32[]{:S(2)}) collective-permute-start(bf16[160,768]{1,0:T(8,128)(2,1)S(1)} %shard_map.89.refs_0_), channel_id=1, source_target_pairs={{0,1},{1,0},{2,3},{3,2},{4,5},{5,4},{6,7},{7,6},{8,9},{9,8},{10,11... | collective-permute-start | bytes 737288 | tf_op jit(solution)/shard_map/ppermute | solution.py:266
  51.9 14.5 %collective-permute-start.11 = (bf16[160,768]{1,0:T(8,128)(2,1)}, bf16[160,768]{1,0:T(8,128)(2,1)}, u32[]{:S(2)}, u32[]{:S(2)}) collective-permute-start(bf16[160,768]{1,0:T(8,128)(2,1)} %collective-permute-done.9.refs_1_), channel_id=1, source_target_pairs={{0,1},{1,0},{2,3},{3,2},{4,5},{5,4},{6,7},{7,6},{8,9},{9,8},{10,11... | collective-permute-start | bytes 737288 | tf_op jit(solution)/shard_map/ppermute | solution.py:266
  52.7 31.8 %collective-permute-start.1 = (bf16[1,256,2,2,128]{4,3,2,1,0:T(2,128)(2,1)}, bf16[1,256,2,2,128]{4,3,2,1,0:T(2,128)(2,1)S(1)}, u32[]{:S(2)}, u32[]{:S(2)}) collective-permute-start(bf16[1,256,2,2,128]{4,3,2,1,0:T(2,128)(2,1)} %copy-done.11), channel_id=1, source_target_pairs={{0,8},{4,12},{8,0},{12,4},{1,9},{5,13},{9,1},{13,5},{2,10},{6,14},... | collective-permute-start | bytes 786440 | tf_op jit(solution)/shard_map/ppermute | solution.py:263
  65.9 10.0 %copy-start.12 = (s32[2,80]{1,0:T(2,128)S(1)}, s32[2,80]{1,0:T(2,128)}, u32[]{:S(2)}) copy-start(s32[2,80]{1,0:T(2,128)} %param.10) | copy-start | bytes 1924
  65.9 10.0 %copy-start.13 = (s32[1,4]{1,0:T(1,128)S(1)}, s32[1,4]{1,0:T(1,128)}, u32[]{:S(2)}) copy-start(s32[1,4]{1,0:T(1,128)} %param.8) | copy-start | bytes 52
  65.9 24.7 %collective-permute-start.2 = (bf16[1,256,2,2,128]{4,3,2,1,0:T(2,128)(2,1)}, bf16[1,256,2,2,128]{4,3,2,1,0:T(2,128)(2,1)S(1)}, u32[]{:S(2)}, u32[]{:S(2)}) collective-permute-start(bf16[1,256,2,2,128]{4,3,2,1,0:T(2,128)(2,1)} %copy-done.10), channel_id=1, source_target_pairs={{0,8},{4,12},{8,0},{12,4},{1,9},{5,13},{9,1},{13,5},{2,10},{6,14},... | collective-permute-start | bytes 786440 | tf_op jit(solution)/shard_map/ppermute | solution.py:263
  66.0 18.6 %collective-permute-start.6 = (bf16[160,768]{1,0:T(8,128)(2,1)S(1)}, bf16[160,768]{1,0:T(8,128)(2,1)}, u32[]{:S(2)}, u32[]{:S(2)}) collective-permute-start(bf16[160,768]{1,0:T(8,128)(2,1)S(1)} %collective-permute-done.4.refs_0_), channel_id=1, source_target_pairs={{0,1},{1,0},{2,3},{3,2},{4,5},{5,4},{6,7},{7,6},{8,9},{9,8},{10,11... | collective-permute-start | bytes 737288 | tf_op jit(solution)/shard_map/ppermute | solution.py:266
  66.2 18.4 %collective-permute-start.7 = (bf16[160,768]{1,0:T(8,128)(2,1)}, bf16[160,768]{1,0:T(8,128)(2,1)}, u32[]{:S(2)}, u32[]{:S(2)}) collective-permute-start(bf16[160,768]{1,0:T(8,128)(2,1)} %collective-permute-done.5.refs_1_), channel_id=1, source_target_pairs={{0,1},{1,0},{2,3},{3,2},{4,5},{5,4},{6,7},{7,6},{8,9},{9,8},{10,11... | collective-permute-start | bytes 737288 | tf_op jit(solution)/shard_map/ppermute | solution.py:266
  74.9 21.6 %collective-permute-start.17 = (f32[2,80,512]{2,1,0:T(8,128)}, f32[2,80,512]{2,1,0:T(8,128)S(1)}, u32[]{:S(2)}, u32[]{:S(2)}) collective-permute-start(f32[2,80,512]{2,1,0:T(8,128)} %get-tuple-element.27), channel_id=1, source_target_pairs={{0,4},{4,0},{8,12},{12,8},{1,5},{5,1},{9,13},{13,9},{2,6},{6,2},{1... | collective-permute-start | bytes 983048 | tf_op jit(solution)/shard_map/ppermute | solution.py:266
  84.6 2.8 %copy-start.2 = (bf16[2,3072,512]{2,1,0:T(8,128)(2,1)S(1)}, bf16[2,3072,512]{2,1,0:T(8,128)(2,1)}, u32[]{:S(2)}) copy-start(bf16[2,3072,512]{2,1,0:T(8,128)(2,1)} %reshape.51.refs_5_.refs_1_.refs_8_) | copy-start | bytes 18874372
  87.4 3.1 %copy-start.9 = (f32[2,80,512]{2,1,0:T(8,128)S(1)}, f32[2,80,512]{2,1,0:T(8,128)}, u32[]{:S(2)}) copy-start(f32[2,80,512]{2,1,0:T(8,128)} %copy-done.8) | copy-start | bytes 983044
  87.4 9.3 %copy-start.14 = (s32[1,4]{1,0:T(1,128)S(1)}, s32[1,4]{1,0:T(1,128)}, u32[]{:S(2)}) copy-start(s32[1,4]{1,0:T(1,128)} %param.9) | copy-start | bytes 52
  90.5 13.0 %collective-permute-start.16 = (f32[2,80,512]{2,1,0:T(8,128)S(1)}, f32[2,80,512]{2,1,0:T(8,128)S(1)}, u32[]{:S(2)}, u32[]{:S(2)}) collective-permute-start(f32[2,80,512]{2,1,0:T(8,128)S(1)} %copy-done.9), channel_id=1, source_target_pairs={{0,4},{4,0},{8,12},{12,8},{1,5},{5,1},{9,13},{13,9},{2,6},{6,2},{1... | collective-permute-start | bytes 983048 | tf_op jit(solution)/shard_map/ppermute | solution.py:266
  96.6 15.9 %collective-permute-start.18 = (f32[2,80,512]{2,1,0:T(8,128)S(1)}, f32[2,80,512]{2,1,0:T(8,128)S(1)}, u32[]{:S(2)}, u32[]{:S(2)}) collective-permute-start(f32[2,80,512]{2,1,0:T(8,128)S(1)} %shard_map.91), channel_id=1, source_target_pairs={{0,8},{4,12},{8,0},{12,4},{1,9},{5,13},{9,1},{13,5},{2,10},{6,14},... | collective-permute-start | bytes 983048 | tf_op jit(solution)/shard_map/ppermute | solution.py:263
  (10 other events, 13.9 us)

commit v5 on v3

v5 whole, which is shorter than its diff:
```python
import functools

import jax
import jax.numpy as jnp
from jax import lax
from jax.experimental import pallas as pl
from jax.experimental.pallas import tpu as pltpu
from jax.sharding import PartitionSpec as P

KVH = 8
PROMPT_PER_HOLD = 512
LAYERS = 2
CHUNK = 8
ROWS = 16
UNROLL = 8
CUTS = 3
VMEM_BYTES = 16 * 1024 * 1024
FREE = pl.CostEstimate(flops=0, bytes_accessed=0, transcendentals=0)
PARAMS = pltpu.CompilerParams(vmem_limit_bytes=VMEM_BYTES)
WIDE = pltpu.CompilerParams(vmem_limit_bytes=60 * 1024 * 1024)
ANY = pl.BlockSpec(memory_space=pl.ANY)
VMEM = pl.BlockSpec(memory_space=pltpu.VMEM)
SMEM = pl.BlockSpec(memory_space=pltpu.SMEM)


def norm_kernel(at, rows_ref, gain_ref, *refs):
    own, outs, held = refs[0], refs[1:-1], refs[-1]
    rows = rows_ref[...].astype(jnp.float32)
    held[...] = lax.rsqrt(jnp.mean(rows * rows, axis=1, keepdims=True) + 1e-05)
    layer = pl.program_id(0) // (pl.num_programs(0) // gain_ref.shape[0])
    for i, out in enumerate((own,) + outs):
        columns = pl.ds(pl.multiple_of(at[i], 128), out.shape[1])
        gain = gain_ref[0:1, columns].astype(jnp.float32)
        for other in range(1, gain_ref.shape[0]):
            gain = jnp.where(
                layer == other, gain_ref[other : other + 1, columns].astype(jnp.float32), gain
            )
        part = rows_ref[:, columns].astype(jnp.float32)
        out[...] = (part * held[...] * gain).astype(jnp.bfloat16)


def normed_shares(hidden, gain, me, share, n, feats, part):
    layers, rec, width = hidden.shape
    rows = layers * rec
    at = jnp.stack([me * feats] + [((me + k) % n) * feats + share * part for k in range(1, n)])
    sizes = [feats] + [part] * (n - 1)
    return pl.pallas_call(
        norm_kernel,
        grid_spec=pltpu.PrefetchScalarGridSpec(
            num_scalar_prefetch=1,
            grid=(rows // ROWS,),
            in_specs=[
                pl.BlockSpec((ROWS, width), lambda i, at: (i, 0)),
                pl.BlockSpec(gain.shape, lambda i, at: (0, 0)),
            ],
            out_specs=[pl.BlockSpec((ROWS, size), lambda i, at: (i, 0)) for size in sizes],
            scratch_shapes=[pltpu.VMEM((ROWS, 1), jnp.float32)],
        ),
        out_shape=[jax.ShapeDtypeStruct((rows, size), jnp.bfloat16) for size in sizes],
        cost_estimate=FREE,
        compiler_params=PARAMS,
    )(at.astype(jnp.int32), hidden.reshape(rows, width), gain)


def tie_kernel(*refs):
    pass


def tie(value, *after):
    return pl.pallas_call(
        tie_kernel,
        in_specs=[ANY] * (1 + len(after)),
        out_specs=ANY,
        out_shape=jax.ShapeDtypeStruct(value.shape, value.dtype),
        input_output_aliases={0: 0},
        cost_estimate=FREE,
        compiler_params=PARAMS,
    )(value, *after)


def pick_kernel(wanted, at, store, *refs):
    outs, held, sems = refs[: len(wanted)], refs[-2], refs[-1]
    moves = []
    for i, (out, (k, layer)) in enumerate(zip(outs, wanted)):
        for j in range(out.shape[0]):
            slot = len(moves)
            source = store.at[j if layer is None else layer, at[k]]
            fetch = pltpu.make_async_copy(source, held.at[slot], sems.at[0, slot])
            fetch.start()
            moves.append((fetch, pltpu.make_async_copy(held.at[slot], out.at[j], sems.at[1, slot])))
    for fetch, place in moves:
        fetch.wait()
        place.start()
    for _, place in moves:
        place.wait()


def pick(store, at, wanted):
    if not wanted:
        return []
    counts = [store.shape[0] if layer is None else 1 for _, layer in wanted]
    total = sum(counts)
    return pl.pallas_call(
        functools.partial(pick_kernel, wanted),
        grid_spec=pltpu.PrefetchScalarGridSpec(
            num_scalar_prefetch=1,
            grid=(),
            in_specs=[ANY],
            out_specs=[ANY] * len(wanted),
            scratch_shapes=[
                pltpu.VMEM((total,) + store.shape[2:], store.dtype),
                pltpu.SemaphoreType.DMA((2, total)),
            ],
        ),
        out_shape=[
            jax.ShapeDtypeStruct((count,) + store.shape[2:], store.dtype) for count in counts
        ],
        cost_estimate=FREE,
        compiler_params=WIDE,
    )(jnp.stack(at).astype(jnp.int32), store)


def product_kernel(counts, at, *refs):
    weight, shares = refs[0], refs[1 : 1 + sum(counts)]
    held, loaded, sems, weight_sems = refs[-4:]
    outs = refs[-4 - len(counts) : -4]
    layers, rec, _ = outs[0].shape
    blocks = [i for i, count in enumerate(counts) for _ in range(count)]
    cuts = weight_sems.shape[1]
    chunk = weight.shape[1] // cuts
    placed, weights = [], []
    for layer in range(layers):
        placed.append([])
        for j, (share, i) in enumerate(zip(shares, blocks)):
            row = pl.ds(pl.multiple_of(at[i] * rec, 16), rec)
            column = pl.ds(pl.multiple_of(at[len(counts) + j], 128), share.shape[1])
            source, target = share.at[layer * rec : (layer + 1) * rec], held.at[layer, row, column]
            placed[layer].append(pltpu.make_async_copy(source, target, sems.at[j, layer]))
        weights.append([])
        for c in range(cuts):
            piece = pl.ds(c * chunk, chunk)
            source, target = weight.at[layer, piece], loaded.at[layer, piece]
            weights[layer].append(pltpu.make_async_copy(source, target, weight_sems.at[layer, c]))
        for copy in placed[layer] + weights[layer]:
            copy.start()
    for layer in range(layers):
        for copy in placed[layer]:
            copy.wait()
        total = None
        for c in range(cuts):
            weights[layer][c].wait()
            piece = slice(c * chunk, (c + 1) * chunk)
            result = jnp.dot(
                held[layer, :, piece], loaded[layer, piece], preferred_element_type=jnp.float32
            )
            total = result if total is None else total + result
        for i, out in enumerate(outs):
            out[layer] = total[i * rec : (i + 1) * rec]


def products(blocks, weight, order, columns, rec):
    counts = tuple(len(block) for block in blocks)
    at = jnp.stack(list(order) + [c for cs in columns for c in cs]).astype(jnp.int32)
    layers, feats, cols = weight.shape
    flat = [share for block in blocks for share in block]
    return pl.pallas_call(
        functools.partial(product_kernel, counts),
        in_specs=[SMEM] + [ANY] * (1 + len(flat)),
        out_specs=[VMEM] * len(blocks),
        out_shape=[jax.ShapeDtypeStruct((layers, rec, cols), jnp.float32)] * len(blocks),
        scratch_shapes=[
            pltpu.VMEM((layers, len(blocks) * rec, feats), jnp.bfloat16),
            pltpu.VMEM((layers, feats, cols), jnp.bfloat16),
            pltpu.SemaphoreType.DMA((len(flat), layers)),
            pltpu.SemaphoreType.DMA((layers, CUTS)),
        ],
        cost_estimate=FREE,
        compiler_params=WIDE,
    )(at, weight, *flat)


def add_kernel(count, *refs):
    outs = refs[len(refs) - count :]
    for left, right, out in zip(refs[:count], refs[count : 2 * count], outs):
        out[...] = left[...] + right[...]


def add_pairs(left, right):
    count = len(left)
    return pl.pallas_call(
        functools.partial(add_kernel, count),
        in_specs=[VMEM] * (2 * count),
        out_specs=[VMEM] * count,
        out_shape=[jax.ShapeDtypeStruct(value.shape, value.dtype) for value in left],
        cost_estimate=FREE,
        compiler_params=PARAMS,
    )(*left, *right)


def unite_kernel(counts, starts, lengths, spots, *refs):
    total = sum(counts)
    pages, (fresh, out, sums, held, squares, sems) = refs[:total], refs[total:]
    layers, rec = fresh.shape[:2]
    copies, base = [], 0
    for slot, count in enumerate(counts):
        copies.append([])
        for i in range(count):
            target = held.at[slot] if count == 1 else held.at[slot, pl.ds(i, 1)]
            copies[-1].append(pltpu.make_async_copy(pages[base + i], target, sems.at[base + i]))
            copies[-1][-1].start()
        base += count
    for slot in range(len(counts)):
        for copy in copies[slot]:
            copy.wait()
        start, length = starts[slot], lengths[slot]
        whole = length // CHUNK

        def many(i, carry, slot=slot, start=start):
            for layer in range(layers):
                out[layer, pl.ds(start + i * CHUNK, CHUNK)] = held[
                    slot, layer, pl.ds(i * CHUNK, CHUNK)
                ]
            return carry

        def one(i, carry, slot=slot, start=start):
            for layer in range(layers):
                out[layer, start + i] = held[slot, layer, i]
            return carry

        lax.fori_loop(0, whole, many, 0)
        lax.fori_loop(whole * CHUNK, length, one, 0)
    for layer in range(layers):

        def renew(j, carry, layer=layer):
            at = layer * rec + j
            spot = spots[at]
            old = out[layer, spot].astype(jnp.float32)
            new = fresh[layer, j]
            diff = new.astype(jnp.float32) - old
            squares[pl.ds(at, 1), :] = jnp.sum(jnp.sum(diff * diff, axis=0), axis=0, keepdims=True)
            squares[pl.ds(layers * rec + at, 1), :] = jnp.sum(
                jnp.sum(old * old, axis=0), axis=0, keepdims=True
            )
            out[layer, spot] = new
            return carry

        lax.fori_loop(0, rec, renew, 0, unroll=UNROLL)
    ones = jnp.ones((8, squares.shape[1]), jnp.float32)
    both = lax.dot_general(
        ones,
        squares[...],
        (((1,), (1,)), ((), ())),
        precision=lax.Precision.HIGHEST,
        preferred_element_type=jnp.float32,
    )
    sums[...] = both[0:1]


def unite(pages, fresh, starts, lengths, spots):
    counts = tuple(len(page) for page in pages)
    flat = [piece for page in pages for piece in page]
    layers, rec = fresh.shape[:2]
    rows = flat[0].shape[1:]
    return pl.pallas_call(
        functools.partial(unite_kernel, counts),
        in_specs=[SMEM] * 3 + [ANY] * len(flat) + [VMEM],
        out_specs=[VMEM, VMEM],
        out_shape=[
            jax.ShapeDtypeStruct((layers, PROMPT_PER_HOLD) + rows[1:], fresh.dtype),
            jax.ShapeDtypeStruct((1, 2 * layers * rec), jnp.float32),
        ],
        scratch_shapes=[
            pltpu.VMEM((len(pages), layers) + rows, fresh.dtype),
            pltpu.VMEM((2 * layers * rec, rows[-1]), jnp.float32),
            pltpu.SemaphoreType.DMA((len(flat),)),
        ],
        cost_estimate=FREE,
        compiler_params=PARAMS,
    )(starts, lengths, spots, *flat, fresh)


def make_local(n, tps):
    def shift(value, k):
        return lax.ppermute(value, "hold", [(i, (i + k) % n) for i in range(n)])

    def swap(value, axis, size, bit):
        return lax.ppermute(value, axis, [(i, i ^ bit) for i in range(size)])

    def local(cache_store, span_lengths, span_holder, rec_pos, hidden, norm_gain, kv_weight):
        me = lax.axis_index("hold")
        my_tp = lax.axis_index("tp")
        rec = hidden.shape[1]
        feats = kv_weight.shape[1]
        heads_here, head_size = kv_weight.shape[2], kv_weight.shape[4]
        cols = heads_here * 2 * head_size
        odds = sorted(range(1, n, 2), key=lambda k: min(k, n - k))
        evens = sorted(range(2, n, 2), key=lambda k: min(k, n - k))
        cuts = tps
        while feats % (cuts * 128):
            cuts //= 2
        part = feats // cuts
        share = my_tp % cuts

        own, *pieces = normed_shares(hidden, norm_gain, me, share, n, feats, part)
        arrived = {k: shift(pieces[k - 1], k) for k in odds + evens}
        at = [(me + k) % n for k in range(n)]
        names = [(k, None) for k in odds[::-1]] + [(k, i) for k in evens for i in range(LAYERS)]
        picked = pick(cache_store, at, names + [(0, None)])
        there, last = {}, ()
        for name, page in zip(names, picked):
            there[name] = shift(tie(page, *last) if last else page, name[0])
            last = (there[name],)
        pages = [[picked[-1]]] + [
            [there[name] for name in sorted(names, key=lambda x: x[1] or 0) if name[0] == k]
            for k in range(1, n)
        ]

        weight = kv_weight.reshape(LAYERS, feats, cols)
        arrived[odds[0]] = tie(arrived[odds[0]], weight[:1, :8, :128])

        def everyone(piece):
            shares, masks, bit = [piece], [0], cuts // 2
            while bit:
                shares = shares + [swap(value, "tp", tps, bit) for value in shares]
                masks = masks + [mask ^ bit for mask in masks]
                bit //= 2
            return shares, [(share ^ mask) * part for mask in masks]

        even = me % 2 == 0
        half = n // 2
        blocks = [everyone(arrived[k]) for k in odds + evens] + [([own], [jnp.int32(0)])]
        order = [jnp.where(even, (k + 1) // 2 % half, (k - 1) // 2) for k in odds]
        order += [jnp.int32(half + k // 2) for k in evens + [0]]
        partial = products(
            [a[0] for a in blocks], weight, order, [a[1] for a in blocks], rec
        )
        theirs = [swap(partial[i % half], "hold", n, 1) for i in range(1, half + 1)]
        mine = [*partial[half + 1 :], partial[half]]
        total = mine[-1] + theirs[-1]
        if n > 2:
            pairs = add_pairs(mine[:-1], theirs[:-1])
            for k, pair in zip(range(2, n, 2), pairs):
                total = total + shift(pair, -k)
        fresh = total.astype(jnp.bfloat16).reshape(LAYERS, rec, heads_here, 2, head_size)

        lengths = span_lengths[0]
        starts = jnp.cumsum(lengths) - lengths
        holders = (me - jnp.arange(n, dtype=jnp.int32)) % n
        held_here = span_holder[0][None, :] == holders[:, None]
        slot_starts = jnp.sum(jnp.where(held_here, starts[None, :], 0), axis=1)
        slot_lengths = jnp.sum(jnp.where(held_here, lengths[None, :], 0), axis=1)
        spots = (rec_pos - me * PROMPT_PER_HOLD).reshape(-1)
        united, sums = unite(pages, fresh, slot_starts, slot_lengths, spots)
        sums = lax.psum(sums, "tp").reshape(2, LAYERS, rec)
        entries = KVH * 2 * head_size
        deviation = sums[0] / entries / (sums[1] / entries + 1e-06)
        return (united, deviation)

    return local


def solution(mesh):
    return jax.shard_map(
        make_local(mesh.shape["hold"], mesh.shape["tp"]),
        mesh=mesh,
        in_specs=(
            P(None, ("groups", "hold"), None, "tp", None, None),
            P(("groups", "hold"), None),
            P(("groups", "hold"), None),
            P(None, ("groups", "hold")),
            P(None, ("groups", "hold"), None),
            P(),
            P(None, "hold", "tp", None, None),
        ),
        out_specs=(P(None, ("groups", "hold"), "tp", None, None), P(None, ("groups", "hold"))),
        check_vma=False,
    )
```

time: 123 us -> 115 us (0.935)
  starting transfers between devices: 38.1 us -> 23.8 us
  waiting for transfers between devices: 32.9 us -> 47 us
  local copies, waits for them, and re-layouts: 28.7 us -> 18 us
  Pallas kernels: 15.2 us -> 17.4 us
  other arithmetic: 0.71 us -> 2.18 us
    ppermute x11, starting transfers between devices: 18.1 us -> 6.67 us  [swap(): return lax.ppermute(value, axis, [(i, i ^ bit) for i in range(size)])]
    unnamed x36 -> x34, local copies, waits for them, and re-layouts: 16.4 us -> 5.59 us
    ppermute x11, waiting for transfers between devices: 14.6 us -> 23.4 us  [swap(): return lax.ppermute(value, axis, [(i, i ^ bit) for i in range(size)])]
    ppermute x7 -> x8, waiting for transfers between devices: 18.3 us -> 23.6 us  [shift(): return lax.ppermute(value, 'hold', [(i, (i + k) % n) for i in range(n)])]
    ppermute x7 -> x8, starting transfers between devices: 20 us -> 17.1 us  [shift(): return lax.ppermute(value, 'hold', [(i, (i + k) % n) for i in range(n)])]
    pallas_call x2 -> x1, Pallas kernels: 5.96 us -> 7.33 us  [products(): pl.pallas_call(functools.partial(product_kernel, counts), in_specs=[SMEM]...]
    pallas_call x2 -> x6, Pallas kernels: 5.37 us -> 6.27 us  [the longest x1 3.19 us: unite(): pl.pallas_call(functools.partial(unite_kernel, counts), in_specs=[SMEM] *...]
  transfers between devices with their start and end apart: 18 -> 19, of which waited for: 8 -> 7; matrix products, arithmetic and copies ran while one was open for 10% -> 12% of each run, Pallas kernels for 6% -> 10%
where the time goes in v5:
time: 115 us
  waiting for transfers between devices  47 us (41%)
  starting transfers between devices  23.8 us (21%)
  local copies, waits for them, and re-layouts  18 us (16%)
  Pallas kernels  17.4 us (15%)
  blocking collectives  5.67 us (5%)
  other arithmetic  2.18 us (2%)
    ppermute x8, waiting for transfers between devices, shift(): return lax.ppermute(value, 'hold', [(i, (i + k) % n) for i in range(n)])  23.6 us
    ppermute x11, waiting for transfers between devices, swap(): return lax.ppermute(value, axis, [(i, i ^ bit) for i in range(size)])  23.4 us
    ppermute x8, starting transfers between devices, shift(): return lax.ppermute(value, 'hold', [(i, (i + k) % n) for i in range(n)])  17.1 us
    reshape x1, local copies, waits for them, and re-layouts, local(): weight = kv_weight.reshape(LAYERS, feats, cols)  10.2 us
    pallas_call x1, Pallas kernels, products(): pl.pallas_call(functools.partial(product_kernel, counts), in_specs=[SMEM]...  7.33 us
    ppermute x11, starting transfers between devices, swap(): return lax.ppermute(value, axis, [(i, i ^ bit) for i in range(size)])  6.67 us
    psum x1, blocking collectives, local(): sums = lax.psum(sums, 'tp').reshape(2, LAYERS, rec)  5.67 us
    unnamed x34, local copies, waits for them, and re-layouts  5.59 us
  transfers between devices with their start and end apart: 19, of which 7 were waited for; matrix products, arithmetic and copies ran while one was open for 12% of the time, Pallas kernels for 10%

profile of v5, /device:TPU:0, one launch (start us, length us, event | category | flops | bytes accessed | tf_op | source)
XLA Modules:
  0.0 114.8 jit_solution(15206253528870935410)
XLA Ops:
  1.3 3.1 %shard_map.86 = (bf16[2,256,2,2,128]{4,3,2,1,0:T(2,128)(2,1)}, bf16[2,256,2,2,128]{4,3,2,1,0:T(2,128)(2,1)}, bf16[1,256,2,2,128]{4,3,2,1,0:T(2,128)(2,1)}, bf16[...) custom-call(s32[4]{0:T(128)} %pad_add_fusion.at, bf16[2,4,256,2,2,128]{5,4,3,2,1,0:T(2,128)(2,1)} %store.1), custom_call_target="tpu_custom_call" | custom-call | tf_op jit(solution)/shard_map/pallas_call | solution.py:103
  4.3 5.1 %collective-permute-start = (bf16[2,256,2,2,128]{4,3,2,1,0:T(2,128)(2,1)}, bf16[2,256,2,2,128]{4,3,2,1,0:T(2,128)(2,1)S(1)}, u32[]{:S(2)}, u32[]{:S(2)}) collective-permute-start(bf16[2,256,2,2,128]{4,3,2,1,0:T(2,128)(2,1)} %get-tuple-element.19), channel_id=1, source_target_pairs={{0,12},{4,0},{8,4},{12,8},{1,13},{5,1},{9,5},{13,9},{2,14},{6,2},{... | collective-permute-start | bytes 1572872 | tf_op jit(solution)/shard_map/ppermute | solution.py:284
  9.5 2.1 %copy-done = bf16[2,80,12288]{2,1,0:T(8,128)(2,1)S(1)} copy-done((bf16[2,80,12288]{2,1,0:T(8,128)(2,1)S(1)}, bf16[2,80,12288]{2,1,0:T(8,128)(2,1)}, u32[]{:S(2)}) %copy-start) | copy-done | bytes 3932184
  12.4 3.8 %shard_map.90 = (bf16[160,3072]{1,0:T(8,128)(2,1)S(1)}, bf16[160,768]{1,0:T(8,128)(2,1)S(1)}, bf16[160,768]{1,0:T(8,128)(2,1)S(1)}, bf16[160,768]{1,0:T(8,128)(2,1)S(1)}) custom-call(s32[4]{0:T(128)S(1)} %pad_add_fusion.1.at, bf16[160,12288]{1,0:T(8,128)(2,1)S(1)} %bitcast.19, bf16[2,12288]{1,0:T(2,128)(2,1)S(1)} %copy-done.8), custom_call_target="tpu_custom_call" | custom-call | tf_op jit(solution)/shard_map/pallas_call | solution.py:47
  16.3 0.9 copy-done.1
  17.2 3.8 %collective-permute-start.8 = (bf16[160,768]{1,0:T(8,128)(2,1)S(1)}, bf16[160,768]{1,0:T(8,128)(2,1)S(1)}, u32[]{:S(2)}, u32[]{:S(2)}) collective-permute-start(bf16[160,768]{1,0:T(8,128)(2,1)S(1)} %get-tuple-element.23), channel_id=1, source_target_pairs={{0,12},{4,0},{8,4},{12,8},{1,13},{5,1},{9,5},{13,9},{2,14},{6,2},{... | collective-permute-start | bytes 737288 | tf_op jit(solution)/shard_map/ppermute | solution.py:284
  21.0 10.2 %reshape.50.refs_0_ = bf16[2,3072,512]{2,1,0:T(8,128)(2,1)} reshape(bf16[2,3072,2,2,128]{4,3,2,1,0:T(2,128)(2,1)} %param.13) | data formatting | bytes 12582912 | tf_op jit(solution)/shard_map/reshape | solution.py:318
  32.0 1.5 %collective-permute-start.5 = (bf16[160,768]{1,0:T(8,128)(2,1)S(1)}, bf16[160,768]{1,0:T(8,128)(2,1)S(1)}, u32[]{:S(2)}, u32[]{:S(2)}) collective-permute-start(bf16[160,768]{1,0:T(8,128)(2,1)S(1)} %shard_map.91.refs_1_), channel_id=1, source_target_pairs={{0,2},{1,3},{2,0},{3,1},{4,6},{5,7},{6,4},{7,5},{8,10},{9,11},{10,... | collective-permute-start | bytes 737288 | tf_op jit(solution)/shard_map/ppermute | solution.py:287
  34.1 7.7 %collective-permute-done.12.refs_9_ = bf16[160,768]{1,0:T(8,128)(2,1)S(1)} collective-permute-done((bf16[160,768]{1,0:T(8,128)(2,1)S(1)}, bf16[160,768]{1,0:T(8,128)(2,1)S(1)}, u32[]{:S(2)}, u32[]{:S(2)}) %collective-permute-start.12) | collective-permute-done | bytes 245792 | tf_op jit(solution)/shard_map/ppermute | solution.py:284
  41.8 1.5 %collective-permute-start.13 = (bf16[160,768]{1,0:T(8,128)(2,1)S(1)}, bf16[160,768]{1,0:T(8,128)(2,1)}, u32[]{:S(2)}, u32[]{:S(2)}) collective-permute-start(bf16[160,768]{1,0:T(8,128)(2,1)S(1)} %collective-permute-done.12.refs_9_), channel_id=1, source_target_pairs={{0,2},{1,3},{2,0},{3,1},{4,6},{5,7},{6,4},{7,5},{8,10},{9,11},{10,... | collective-permute-start | bytes 737288 | tf_op jit(solution)/shard_map/ppermute | solution.py:287
  43.4 1.6 %collective-permute-start.1 = (bf16[2,256,2,2,128]{4,3,2,1,0:T(2,128)(2,1)S(1)}, bf16[2,256,2,2,128]{4,3,2,1,0:T(2,128)(2,1)S(1)}, u32[]{:S(2)}, u32[]{:S(2)}) collective-permute-start(bf16[2,256,2,2,128]{4,3,2,1,0:T(2,128)(2,1)S(1)} %shard_map.87), channel_id=1, source_target_pairs={{0,4},{4,8},{8,12},{12,0},{1,5},{5,9},{9,13},{13,1},{2,6},{6,10},{... | collective-permute-start | bytes 1572872 | tf_op jit(solution)/shard_map/ppermute | solution.py:284
  45.5 4.0 %collective-permute-done.13.refs_10_ = bf16[160,768]{1,0:T(8,128)(2,1)} collective-permute-done((bf16[160,768]{1,0:T(8,128)(2,1)S(1)}, bf16[160,768]{1,0:T(8,128)(2,1)}, u32[]{:S(2)}, u32[]{:S(2)}) %collective-permute-start.13) | collective-permute-done | bytes 245792 | tf_op jit(solution)/shard_map/ppermute | solution.py:287
  52.2 7.3 %shard_map.92 = (f32[2,80,512]{2,1,0:T(8,128)}, f32[2,80,512]{2,1,0:T(8,128)}, f32[2,80,512]{2,1,0:T(8,128)}, f32[2,80,512]{2,1,0:T(8,128)}) custom-call(s32[17]{0:T(128)} %stack.70.at, bf16[2,3072,512]{2,1,0:T(8,128)(2,1)} %reshape.50.refs_0_, bf16[160,768]{1,0:T(8,128)(2,1)} %copy-done.2, bf16[160,768]{1,0:T(8,128)(2,1)} %copy-done.11, ...), custom_call_target="tpu_custom_call" | custom-call | tf_op jit(solution)/shard_map/pallas_call | solution.py:166
  59.6 2.0 %collective-permute-start.17 = (f32[2,80,512]{2,1,0:T(8,128)}, f32[2,80,512]{2,1,0:T(8,128)S(1)}, u32[]{:S(2)}, u32[]{:S(2)}) collective-permute-start(f32[2,80,512]{2,1,0:T(8,128)} %get-tuple-element.29), channel_id=1, source_target_pairs={{0,4},{4,0},{8,12},{12,8},{1,5},{5,1},{9,13},{13,9},{2,6},{6,2},{1... | collective-permute-start | bytes 983048 | tf_op jit(solution)/shard_map/ppermute | solution.py:287
  61.6 3.4 %collective-permute-start.2 = (bf16[1,256,2,2,128]{4,3,2,1,0:T(2,128)(2,1)S(1)}, bf16[1,256,2,2,128]{4,3,2,1,0:T(2,128)(2,1)S(1)}, u32[]{:S(2)}, u32[]{:S(2)}) collective-permute-start(bf16[1,256,2,2,128]{4,3,2,1,0:T(2,128)(2,1)S(1)} %shard_map.88), channel_id=1, source_target_pairs={{0,8},{4,12},{8,0},{12,4},{1,9},{5,13},{9,1},{13,5},{2,10},{6,14},... | collective-permute-start | bytes 786440 | tf_op jit(solution)/shard_map/ppermute | solution.py:284
  65.2 10.7 %collective-permute-done.17.refs_1_ = f32[2,80,512]{2,1,0:T(8,128)S(1)} collective-permute-done((f32[2,80,512]{2,1,0:T(8,128)}, f32[2,80,512]{2,1,0:T(8,128)S(1)}, u32[]{:S(2)}, u32[]{:S(2)}) %collective-permute-start.17) | collective-permute-done | bytes 327712 | tf_op jit(solution)/shard_map/ppermute | solution.py:287
  76.0 1.0 copy-done.5
  77.0 3.0 %collective-permute-start.18 = (f32[2,80,512]{2,1,0:T(8,128)S(1)}, f32[2,80,512]{2,1,0:T(8,128)S(1)}, u32[]{:S(2)}, u32[]{:S(2)}) collective-permute-start(f32[2,80,512]{2,1,0:T(8,128)S(1)} %shard_map.93), channel_id=1, source_target_pairs={{0,8},{4,12},{8,0},{12,4},{1,9},{5,13},{9,1},{13,5},{2,10},{6,14},... | collective-permute-start | bytes 983048 | tf_op jit(solution)/shard_map/ppermute | solution.py:284
  80.4 7.9 %collective-permute-done.16 = f32[2,80,512]{2,1,0:T(8,128)S(1)} collective-permute-done((f32[2,80,512]{2,1,0:T(8,128)}, f32[2,80,512]{2,1,0:T(8,128)S(1)}, u32[]{:S(2)}, u32[]{:S(2)}) %collective-permute-start.16) | collective-permute-done | bytes 327712 | tf_op jit(solution)/shard_map/ppermute | solution.py:287
  88.2 13.0 %collective-permute-done.18 = f32[2,80,512]{2,1,0:T(8,128)S(1)} collective-permute-done((f32[2,80,512]{2,1,0:T(8,128)S(1)}, f32[2,80,512]{2,1,0:T(8,128)S(1)}, u32[]{:S(2)}, u32[]{:S(2)}) %collective-permute-start.18) | collective-permute-done | bytes 327712 | tf_op jit(solution)/shard_map/ppermute | solution.py:284
  101.2 1.0 add_convert_fusion
  102.3 2.9 %collective-permute-done.3.refs_3_ = bf16[1,256,2,2,128]{4,3,2,1,0:T(2,128)(2,1)S(1)} collective-permute-done((bf16[1,256,2,2,128]{4,3,2,1,0:T(2,128)(2,1)S(1)}, bf16[1,256,2,2,128]{4,3,2,1,0:T(2,128)(2,1)S(1)}, u32[]{:S(2)}, u32[]{:S(2)}) %collective-permute-start.3) | collective-permute-done | bytes 262176 | tf_op jit(solution)/shard_map/ppermute | solution.py:284
  105.2 3.2 %shard_map.94 = (bf16[2,512,2,2,128]{4,3,2,1,0:T(2,128)(2,1)}, f32[1,320]{1,0:T(1,128)S(1)}) custom-call(s32[4]{0:T(128)S(1)} %get-tuple-element.33.starts, s32[4]{0:T(128)S(1)} %get-tuple-element.32.lengths, s32[160]{0:T(256)S(1)} %reshape.49.spots, bf16[2,256,2,2,128]{4,3,2,1,0:T(2,128)(2,1)S(1)} %copy-done.3, ...), custom_call_target="tpu_custom_call" | custom-call | tf_op jit(solution)/shard_map/pallas_call | solution.py:264
  108.4 5.7 %psum.7 = f32[1,320]{1,0:T(1,128)S(1)} all-reduce(f32[1,320]{1,0:T(1,128)S(1)} %get-tuple-element.31), channel_id=1, replica_groups=mesh['groups'=2,'hold'=4,'tp'=4] {'tp'}, use_global_device_ids=true, to_apply=%region_3.4 | all-reduce | flops 320 | bytes 2560 | tf_op jit(solution)/shard_map/psum | solution.py:354
  (73 shorter events, 7.5 us)
Async XLA Ops:
  4.3 39.0 %collective-permute-start = (bf16[2,256,2,2,128]{4,3,2,1,0:T(2,128)(2,1)}, bf16[2,256,2,2,128]{4,3,2,1,0:T(2,128)(2,1)S(1)}, u32[]{:S(2)}, u32[]{:S(2)}) collective-permute-start(bf16[2,256,2,2,128]{4,3,2,1,0:T(2,128)(2,1)} %get-tuple-element.19), channel_id=1, source_target_pairs={{0,12},{4,0},{8,4},{12,8},{1,13},{5,1},{9,5},{13,9},{2,14},{6,2},{... | collective-permute-start | bytes 1572872 | tf_op jit(solution)/shard_map/ppermute | solution.py:284
  17.2 14.8 %collective-permute-start.4 = (bf16[160,768]{1,0:T(8,128)(2,1)S(1)}, bf16[160,768]{1,0:T(8,128)(2,1)S(1)}, u32[]{:S(2)}, u32[]{:S(2)}) collective-permute-start(bf16[160,768]{1,0:T(8,128)(2,1)S(1)} %get-tuple-element.22), channel_id=1, source_target_pairs={{0,4},{4,8},{8,12},{12,0},{1,5},{5,9},{9,13},{13,1},{2,6},{6,10},{... | collective-permute-start | bytes 737288 | tf_op jit(solution)/shard_map/ppermute | solution.py:284
  17.2 16.2 %collective-permute-start.8 = (bf16[160,768]{1,0:T(8,128)(2,1)S(1)}, bf16[160,768]{1,0:T(8,128)(2,1)S(1)}, u32[]{:S(2)}, u32[]{:S(2)}) collective-permute-start(bf16[160,768]{1,0:T(8,128)(2,1)S(1)} %get-tuple-element.23), channel_id=1, source_target_pairs={{0,12},{4,0},{8,4},{12,8},{1,13},{5,1},{9,5},{13,9},{2,14},{6,2},{... | collective-permute-start | bytes 737288 | tf_op jit(solution)/shard_map/ppermute | solution.py:284
  21.0 20.8 %collective-permute-start.12 = (bf16[160,768]{1,0:T(8,128)(2,1)S(1)}, bf16[160,768]{1,0:T(8,128)(2,1)S(1)}, u32[]{:S(2)}, u32[]{:S(2)}) collective-permute-start(bf16[160,768]{1,0:T(8,128)(2,1)S(1)} %get-tuple-element.24), channel_id=1, source_target_pairs={{0,8},{4,12},{8,0},{12,4},{1,9},{5,13},{9,1},{13,5},{2,10},{6,14},... | collective-permute-start | bytes 737288 | tf_op jit(solution)/shard_map/ppermute | solution.py:284
  31.2 30.3 %copy-start.14 = (s32[2,80]{1,0:T(2,128)S(1)}, s32[2,80]{1,0:T(2,128)}, u32[]{:S(2)}) copy-start(s32[2,80]{1,0:T(2,128)} %param.10) | copy-start | bytes 1924
  31.2 30.3 %copy-start.7 = (bf16[1,256,2,2,128]{4,3,2,1,0:T(2,128)(2,1)S(1)}, bf16[1,256,2,2,128]{4,3,2,1,0:T(2,128)(2,1)}, u32[]{:S(2)}) copy-start(bf16[1,256,2,2,128]{4,3,2,1,0:T(2,128)(2,1)} %get-tuple-element.20.refs_0_) | copy-start | bytes 786436
  32.0 11.4 %collective-permute-start.5 = (bf16[160,768]{1,0:T(8,128)(2,1)S(1)}, bf16[160,768]{1,0:T(8,128)(2,1)S(1)}, u32[]{:S(2)}, u32[]{:S(2)}) collective-permute-start(bf16[160,768]{1,0:T(8,128)(2,1)S(1)} %shard_map.91.refs_1_), channel_id=1, source_target_pairs={{0,2},{1,3},{2,0},{3,1},{4,6},{5,7},{6,4},{7,5},{8,10},{9,11},{10,... | collective-permute-start | bytes 737288 | tf_op jit(solution)/shard_map/ppermute | solution.py:287
  33.5 11.5 %collective-permute-start.6 = (bf16[160,768]{1,0:T(8,128)(2,1)S(1)}, bf16[160,768]{1,0:T(8,128)(2,1)S(1)}, u32[]{:S(2)}, u32[]{:S(2)}) collective-permute-start(bf16[160,768]{1,0:T(8,128)(2,1)S(1)} %shard_map.91.refs_1_), channel_id=1, source_target_pairs={{0,1},{1,0},{2,3},{3,2},{4,5},{5,4},{6,7},{7,6},{8,9},{9,8},{10,11... | collective-permute-start | bytes 737288 | tf_op jit(solution)/shard_map/ppermute | solution.py:287
  33.5 11.7 %collective-permute-start.9 = (bf16[160,768]{1,0:T(8,128)(2,1)S(1)}, bf16[160,768]{1,0:T(8,128)(2,1)}, u32[]{:S(2)}, u32[]{:S(2)}) collective-permute-start(bf16[160,768]{1,0:T(8,128)(2,1)S(1)} %collective-permute-done.8.refs_5_), channel_id=1, source_target_pairs={{0,2},{1,3},{2,0},{3,1},{4,6},{5,7},{6,4},{7,5},{8,10},{9,11},{10,... | collective-permute-start | bytes 737288 | tf_op jit(solution)/shard_map/ppermute | solution.py:287
  41.8 7.7 %collective-permute-start.13 = (bf16[160,768]{1,0:T(8,128)(2,1)S(1)}, bf16[160,768]{1,0:T(8,128)(2,1)}, u32[]{:S(2)}, u32[]{:S(2)}) collective-permute-start(bf16[160,768]{1,0:T(8,128)(2,1)S(1)} %collective-permute-done.12.refs_9_), channel_id=1, source_target_pairs={{0,2},{1,3},{2,0},{3,1},{4,6},{5,7},{6,4},{7,5},{8,10},{9,11},{10,... | collective-permute-start | bytes 737288 | tf_op jit(solution)/shard_map/ppermute | solution.py:287
  43.3 6.2 %collective-permute-start.10 = (bf16[160,768]{1,0:T(8,128)(2,1)S(1)}, bf16[160,768]{1,0:T(8,128)(2,1)S(1)}, u32[]{:S(2)}, u32[]{:S(2)}) collective-permute-start(bf16[160,768]{1,0:T(8,128)(2,1)S(1)} %collective-permute-done.8.refs_5_), channel_id=1, source_target_pairs={{0,1},{1,0},{2,3},{3,2},{4,5},{5,4},{6,7},{7,6},{8,9},{9,8},{10,11... | collective-permute-start | bytes 737288 | tf_op jit(solution)/shard_map/ppermute | solution.py:287
  43.3 36.7 %copy-start.6 = (bf16[1,256,2,2,128]{4,3,2,1,0:T(2,128)(2,1)S(1)}, bf16[1,256,2,2,128]{4,3,2,1,0:T(2,128)(2,1)}, u32[]{:S(2)}) copy-start(bf16[1,256,2,2,128]{4,3,2,1,0:T(2,128)(2,1)} %get-tuple-element.21.refs_0_) | copy-start | bytes 786436
  43.4 18.2 %collective-permute-start.1 = (bf16[2,256,2,2,128]{4,3,2,1,0:T(2,128)(2,1)S(1)}, bf16[2,256,2,2,128]{4,3,2,1,0:T(2,128)(2,1)S(1)}, u32[]{:S(2)}, u32[]{:S(2)}) collective-permute-start(bf16[2,256,2,2,128]{4,3,2,1,0:T(2,128)(2,1)S(1)} %shard_map.87), channel_id=1, source_target_pairs={{0,4},{4,8},{8,12},{12,0},{1,5},{5,9},{9,13},{13,1},{2,6},{6,10},{... | collective-permute-start | bytes 1572872 | tf_op jit(solution)/shard_map/ppermute | solution.py:284
  45.0 6.4 %collective-permute-start.14 = (bf16[160,768]{1,0:T(8,128)(2,1)S(1)}, bf16[160,768]{1,0:T(8,128)(2,1)}, u32[]{:S(2)}, u32[]{:S(2)}) collective-permute-start(bf16[160,768]{1,0:T(8,128)(2,1)S(1)} %collective-permute-done.12.refs_9_), channel_id=1, source_target_pairs={{0,1},{1,0},{2,3},{3,2},{4,5},{5,4},{6,7},{7,6},{8,9},{9,8},{10,11... | collective-permute-start | bytes 737288 | tf_op jit(solution)/shard_map/ppermute | solution.py:287
  45.2 6.2 %collective-permute-start.7 = (bf16[160,768]{1,0:T(8,128)(2,1)S(1)}, bf16[160,768]{1,0:T(8,128)(2,1)}, u32[]{:S(2)}, u32[]{:S(2)}) collective-permute-start(bf16[160,768]{1,0:T(8,128)(2,1)S(1)} %collective-permute-done.5.refs_2_), channel_id=1, source_target_pairs={{0,1},{1,0},{2,3},{3,2},{4,5},{5,4},{6,7},{7,6},{8,9},{9,8},{10,11... | collective-permute-start | bytes 737288 | tf_op jit(solution)/shard_map/ppermute | solution.py:287
  49.5 1.9 %collective-permute-start.11 = (bf16[160,768]{1,0:T(8,128)(2,1)}, bf16[160,768]{1,0:T(8,128)(2,1)}, u32[]{:S(2)}, u32[]{:S(2)}) collective-permute-start(bf16[160,768]{1,0:T(8,128)(2,1)} %collective-permute-done.9.refs_6_), channel_id=1, source_target_pairs={{0,1},{1,0},{2,3},{3,2},{4,5},{5,4},{6,7},{7,6},{8,9},{9,8},{10,11... | collective-permute-start | bytes 737288 | tf_op jit(solution)/shard_map/ppermute | solution.py:287
  50.2 2.0 %collective-permute-start.15 = (bf16[160,768]{1,0:T(8,128)(2,1)}, bf16[160,768]{1,0:T(8,128)(2,1)}, u32[]{:S(2)}, u32[]{:S(2)}) collective-permute-start(bf16[160,768]{1,0:T(8,128)(2,1)} %collective-permute-done.13.refs_10_), channel_id=1, source_target_pairs={{0,1},{1,0},{2,3},{3,2},{4,5},{5,4},{6,7},{7,6},{8,9},{9,8},{10,11... | collective-permute-start | bytes 737288 | tf_op jit(solution)/shard_map/ppermute | solution.py:287
  52.2 27.9 %copy-start.16 = (s32[1,4]{1,0:T(1,128)S(1)}, s32[1,4]{1,0:T(1,128)}, u32[]{:S(2)}) copy-start(s32[1,4]{1,0:T(1,128)} %param.9) | copy-start | bytes 52
  52.2 53.0 %copy-start.3 = (bf16[2,256,2,2,128]{4,3,2,1,0:T(2,128)(2,1)S(1)}, bf16[2,256,2,2,128]{4,3,2,1,0:T(2,128)(2,1)}, u32[]{:S(2)}) copy-start(bf16[2,256,2,2,128]{4,3,2,1,0:T(2,128)(2,1)} %get-tuple-element.17.refs_0_) | copy-start | bytes 1572868
  59.6 16.4 %collective-permute-start.17 = (f32[2,80,512]{2,1,0:T(8,128)}, f32[2,80,512]{2,1,0:T(8,128)S(1)}, u32[]{:S(2)}, u32[]{:S(2)}) collective-permute-start(f32[2,80,512]{2,1,0:T(8,128)} %get-tuple-element.29), channel_id=1, source_target_pairs={{0,4},{4,0},{8,12},{12,8},{1,5},{5,1},{9,13},{13,9},{2,6},{6,2},{1... | collective-permute-start | bytes 983048 | tf_op jit(solution)/shard_map/ppermute | solution.py:287
  61.6 18.4 %collective-permute-start.2 = (bf16[1,256,2,2,128]{4,3,2,1,0:T(2,128)(2,1)S(1)}, bf16[1,256,2,2,128]{4,3,2,1,0:T(2,128)(2,1)S(1)}, u32[]{:S(2)}, u32[]{:S(2)}) collective-permute-start(bf16[1,256,2,2,128]{4,3,2,1,0:T(2,128)(2,1)S(1)} %shard_map.88), channel_id=1, source_target_pairs={{0,8},{4,12},{8,0},{12,4},{1,9},{5,13},{9,1},{13,5},{2,10},{6,14},... | collective-permute-start | bytes 786440 | tf_op jit(solution)/shard_map/ppermute | solution.py:284
  65.2 23.0 %collective-permute-start.16 = (f32[2,80,512]{2,1,0:T(8,128)}, f32[2,80,512]{2,1,0:T(8,128)S(1)}, u32[]{:S(2)}, u32[]{:S(2)}) collective-permute-start(f32[2,80,512]{2,1,0:T(8,128)} %get-tuple-element.27), channel_id=1, source_target_pairs={{0,4},{4,0},{8,12},{12,8},{1,5},{5,1},{9,13},{13,9},{2,6},{6,2},{1... | collective-permute-start | bytes 983048 | tf_op jit(solution)/shard_map/ppermute | solution.py:287
  77.0 24.2 %collective-permute-start.18 = (f32[2,80,512]{2,1,0:T(8,128)S(1)}, f32[2,80,512]{2,1,0:T(8,128)S(1)}, u32[]{:S(2)}, u32[]{:S(2)}) collective-permute-start(f32[2,80,512]{2,1,0:T(8,128)S(1)} %shard_map.93), channel_id=1, source_target_pairs={{0,8},{4,12},{8,0},{12,4},{1,9},{5,13},{9,1},{13,5},{2,10},{6,14},... | collective-permute-start | bytes 983048 | tf_op jit(solution)/shard_map/ppermute | solution.py:284
  80.0 25.2 %collective-permute-start.3 = (bf16[1,256,2,2,128]{4,3,2,1,0:T(2,128)(2,1)S(1)}, bf16[1,256,2,2,128]{4,3,2,1,0:T(2,128)(2,1)S(1)}, u32[]{:S(2)}, u32[]{:S(2)}) collective-permute-start(bf16[1,256,2,2,128]{4,3,2,1,0:T(2,128)(2,1)S(1)} %shard_map.89), channel_id=1, source_target_pairs={{0,8},{4,12},{8,0},{12,4},{1,9},{5,13},{9,1},{13,5},{2,10},{6,14},... | collective-permute-start | bytes 786440 | tf_op jit(solution)/shard_map/ppermute | solution.py:284
  (12 other events, 114.9 us)

commit v6 on v5

--- a/solution.py
+++ b/solution.py
@@ -23,20 +23,23 @@
 SMEM = pl.BlockSpec(memory_space=pltpu.SMEM)
 
 
-def norm_kernel(at, rows_ref, gain_ref, *refs):
-    own, outs, held = refs[0], refs[1:-1], refs[-1]
-    rows = rows_ref[...].astype(jnp.float32)
-    held[...] = lax.rsqrt(jnp.mean(rows * rows, axis=1, keepdims=True) + 1e-05)
-    layer = pl.program_id(0) // (pl.num_programs(0) // gain_ref.shape[0])
-    for i, out in enumerate((own,) + outs):
-        columns = pl.ds(pl.multiple_of(at[i], 128), out.shape[1])
-        gain = gain_ref[0:1, columns].astype(jnp.float32)
-        for other in range(1, gain_ref.shape[0]):
-            gain = jnp.where(
-                layer == other, gain_ref[other : other + 1, columns].astype(jnp.float32), gain
-            )
-        part = rows_ref[:, columns].astype(jnp.float32)
-        out[...] = (part * held[...] * gain).astype(jnp.bfloat16)
+def norm_kernel(at, rows_ref, gain_ref, *outs):
+    layers = gain_ref.shape[0]
+    rec = rows_ref.shape[0] // layers
+    columns = [pl.ds(pl.multiple_of(at[i], 128), out.shape[1]) for i, out in enumerate(outs)]
+    for layer in range(layers):
+        gains = [gain_ref[layer : layer + 1, column].astype(jnp.float32) for column in columns]
+
+        def chunk(i, carry, layer=layer, gains=gains):
+            here = pl.ds(pl.multiple_of(layer * rec + i * ROWS, ROWS), ROWS)
+            rows = rows_ref[here, :].astype(jnp.float32)
+            scale = lax.rsqrt(jnp.mean(rows * rows, axis=1, keepdims=True) + 1e-05)
+            for out, column, gain in zip(outs, columns, gains):
+                part = rows_ref[here, column].astype(jnp.float32)
+                out[here, :] = (part * scale * gain).astype(jnp.bfloat16)
+            return carry
+
+        lax.fori_loop(0, rec // ROWS, chunk, 0)
 
 
 def normed_shares(hidden, gain, me, share, n, feats, part):
@@ -46,16 +49,8 @@
     sizes = [feats] + [part] * (n - 1)
     return pl.pallas_call(
         norm_kernel,
-        grid_spec=pltpu.PrefetchScalarGridSpec(
-            num_scalar_prefetch=1,
-            grid=(rows // ROWS,),
-            in_specs=[
-                pl.BlockSpec((ROWS, width), lambda i, at: (i, 0)),
-                pl.BlockSpec(gain.shape, lambda i, at: (0, 0)),
-            ],
-            out_specs=[pl.BlockSpec((ROWS, size), lambda i, at: (i, 0)) for size in sizes],
-            scratch_shapes=[pltpu.VMEM((ROWS, 1), jnp.float32)],
-        ),
+        in_specs=[SMEM, VMEM, VMEM],
+        out_specs=[VMEM] * n,
         out_shape=[jax.ShapeDtypeStruct((rows, size), jnp.bfloat16) for size in sizes],
         cost_estimate=FREE,
         compiler_params=PARAMS,
@@ -304,16 +299,13 @@
         own, *pieces = normed_shares(hidden, norm_gain, me, share, n, feats, part)
         arrived = {k: shift(pieces[k - 1], k) for k in odds + evens}
         at = [(me + k) % n for k in range(n)]
-        names = [(k, None) for k in odds[::-1]] + [(k, i) for k in evens for i in range(LAYERS)]
+        names = [(k, None) for k in odds[::-1] + evens]
         picked = pick(cache_store, at, names + [(0, None)])
         there, last = {}, ()
         for name, page in zip(names, picked):
             there[name] = shift(tie(page, *last) if last else page, name[0])
             last = (there[name],)
-        pages = [[picked[-1]]] + [
-            [there[name] for name in sorted(names, key=lambda x: x[1] or 0) if name[0] == k]
-            for k in range(1, n)
-        ]
+        pages = [[picked[-1]]] + [[there[k, None]] for k in range(1, n)]
 
         weight = kv_weight.reshape(LAYERS, feats, cols)
         arrived[odds[0]] = tie(arrived[odds[0]], weight[:1, :8, :128])
@@ -328,14 +320,13 @@
 
         even = me % 2 == 0
         half = n // 2
-        blocks = [everyone(arrived[k]) for k in odds + evens] + [([own], [jnp.int32(0)])]
+        blocks = [everyone(arrived[k]) for k in odds]
         order = [jnp.where(even, (k + 1) // 2 % half, (k - 1) // 2) for k in odds]
-        order += [jnp.int32(half + k // 2) for k in evens + [0]]
-        partial = products(
-            [a[0] for a in blocks], weight, order, [a[1] for a in blocks], rec
-        )
-        theirs = [swap(partial[i % half], "hold", n, 1) for i in range(1, half + 1)]
-        mine = [*partial[half + 1 :], partial[half]]
+        away = products([a[0] for a in blocks], weight, order, [a[1] for a in blocks], rec)
+        blocks = [everyone(arrived[k]) for k in range(2, n, 2)] + [([own], [jnp.int32(0)])]
+        order = [jnp.int32(i) for i in range(half)]
+        mine = products([a[0] for a in blocks], weight, order, [a[1] for a in blocks], rec)
+        theirs = [swap(away[i % half], "hold", n, 1) for i in range(1, half + 1)]
         total = mine[-1] + theirs[-1]
         if n > 2:
             pairs = add_pairs(mine[:-1], theirs[:-1])

time: 115 us -> 115 us (level)
  starting transfers between devices: 23.8 us -> 19.9 us
  Pallas kernels: 17.4 us -> 20.5 us
    pallas_call x1 -> x2, Pallas kernels: 7.33 us -> 11.4 us  [products(): pl.pallas_call(functools.partial(product_kernel, counts), in_specs=[SMEM]...]
    ppermute x8 -> x7, starting transfers between devices: 17.1 us -> 13.4 us  [shift(): return lax.ppermute(value, 'hold', [(i, (i + k) % n) for i in range(n)])]
    unnamed x34 -> x32, local copies, waits for them, and re-layouts: 5.59 us -> 4.87 us
    ppermute x8 -> x7, waiting for transfers between devices: 23.6 us -> 23.2 us  [shift(): return lax.ppermute(value, 'hold', [(i, (i + k) % n) for i in range(n)])]
  transfers between devices with their start and end apart: 19 -> 18, of which waited for: 7 -> 6; matrix products, arithmetic and copies ran while one was open for 12% -> 12% of each run, Pallas kernels for 10% -> 13%
where the time goes in v6:
time: 115 us; the launch traced here: 114 us
  waiting for transfers between devices  47 us (41%)
  Pallas kernels  20.5 us (18%)
  starting transfers between devices  19.9 us (17%)
  local copies, waits for them, and re-layouts  17.6 us (15%)
  blocking collectives  5.67 us (5%)
  other arithmetic  2.4 us (2%)
    ppermute x11, waiting for transfers between devices, swap(): return lax.ppermute(value, axis, [(i, i ^ bit) for i in range(size)])  23.8 us
    ppermute x7, waiting for transfers between devices, shift(): return lax.ppermute(value, 'hold', [(i, (i + k) % n) for i in range(n)])  23.2 us
    ppermute x7, starting transfers between devices, shift(): return lax.ppermute(value, 'hold', [(i, (i + k) % n) for i in range(n)])  13.4 us
    pallas_call x2, Pallas kernels, products(): pl.pallas_call(functools.partial(product_kernel, counts), in_specs=[SMEM]...  11.4 us
    reshape x1, local copies, waits for them, and re-layouts, local(): weight = kv_weight.reshape(LAYERS, feats, cols)  10.1 us
    ppermute x11, starting transfers between devices, swap(): return lax.ppermute(value, axis, [(i, i ^ bit) for i in range(size)])  6.48 us
    psum x1, blocking collectives, local(): sums = lax.psum(sums, 'tp').reshape(2, LAYERS, rec)  5.67 us
    unnamed x32, local copies, waits for them, and re-layouts  4.87 us
  transfers between devices with their start and end apart: 18, of which 6 were waited for; matrix products, arithmetic and copies ran while one was open for 12% of the time, Pallas kernels for 13%

profile of v6, /device:TPU:0, one launch (start us, length us, event | category | flops | bytes accessed | tf_op | source)
XLA Modules:
  0.0 114.1 jit_solution(9881965699937196734)
XLA Ops:
  1.3 3.1 %shard_map.86 = (bf16[2,256,2,2,128]{4,3,2,1,0:T(2,128)(2,1)}, bf16[2,256,2,2,128]{4,3,2,1,0:T(2,128)(2,1)}, bf16[2,256,2,2,128]{4,3,2,1,0:T(2,128)(2,1)}, bf16[2,256,2,2,128]{4,3,2,1,0:T(2,128)(2,1)}) custom-call(s32[4]{0:T(128)} %pad_add_fusion.at, bf16[2,4,256,2,2,128]{5,4,3,2,1,0:T(2,128)(2,1)} %store.1), custom_call_target="tpu_custom_call" | custom-call | tf_op jit(solution)/shard_map/pallas_call | solution.py:98
  4.4 5.1 %collective-permute-start = (bf16[2,256,2,2,128]{4,3,2,1,0:T(2,128)(2,1)}, bf16[2,256,2,2,128]{4,3,2,1,0:T(2,128)(2,1)S(1)}, u32[]{:S(2)}, u32[]{:S(2)}) collective-permute-start(bf16[2,256,2,2,128]{4,3,2,1,0:T(2,128)(2,1)} %get-tuple-element.18), channel_id=1, source_target_pairs={{0,12},{4,0},{8,4},{12,8},{1,13},{5,1},{9,5},{13,9},{2,14},{6,2},{... | collective-permute-start | bytes 1572872 | tf_op jit(solution)/shard_map/ppermute | solution.py:279
  9.6 2.1 %copy-done = bf16[2,80,12288]{2,1,0:T(8,128)(2,1)S(1)} copy-done((bf16[2,80,12288]{2,1,0:T(8,128)(2,1)S(1)}, bf16[2,80,12288]{2,1,0:T(8,128)(2,1)}, u32[]{:S(2)}) %copy-start) | copy-done | bytes 3932184
  12.5 2.9 %shard_map.89 = (bf16[160,3072]{1,0:T(8,128)(2,1)S(1)}, bf16[160,768]{1,0:T(8,128)(2,1)S(1)}, bf16[160,768]{1,0:T(8,128)(2,1)S(1)}, bf16[160,768]{1,0:T(8,128)(2,1)S(1)}) custom-call(s32[4]{0:T(128)S(1)} %pad_add_fusion.1.at, bf16[160,12288]{1,0:T(8,128)(2,1)S(1)} %bitcast.19, bf16[2,12288]{1,0:T(2,128)(2,1)S(1)} %copy-done.7), custom_call_target="tpu_custom_call" | custom-call | tf_op jit(solution)/shard_map/pallas_call | solution.py:50
  15.4 0.9 copy-done.2
  16.3 3.8 %collective-permute-start.11 = (bf16[160,768]{1,0:T(8,128)(2,1)S(1)}, bf16[160,768]{1,0:T(8,128)(2,1)S(1)}, u32[]{:S(2)}, u32[]{:S(2)}) collective-permute-start(bf16[160,768]{1,0:T(8,128)(2,1)S(1)} %get-tuple-element.24), channel_id=1, source_target_pairs={{0,12},{4,0},{8,4},{12,8},{1,13},{5,1},{9,5},{13,9},{2,14},{6,2},{... | collective-permute-start | bytes 737288 | tf_op jit(solution)/shard_map/ppermute | solution.py:279
  20.1 10.1 %reshape.50.refs_0_ = bf16[2,3072,512]{2,1,0:T(8,128)(2,1)} reshape(bf16[2,3072,2,2,128]{4,3,2,1,0:T(2,128)(2,1)} %param.13) | data formatting | bytes 12582912 | tf_op jit(solution)/shard_map/reshape | solution.py:310
  31.0 1.5 %collective-permute-start.8 = (bf16[160,768]{1,0:T(8,128)(2,1)S(1)}, bf16[160,768]{1,0:T(8,128)(2,1)S(1)}, u32[]{:S(2)}, u32[]{:S(2)}) collective-permute-start(bf16[160,768]{1,0:T(8,128)(2,1)S(1)} %shard_map.91.refs_1_), channel_id=1, source_target_pairs={{0,2},{1,3},{2,0},{3,1},{4,6},{5,7},{6,4},{7,5},{8,10},{9,11},{10,... | collective-permute-start | bytes 737288 | tf_op jit(solution)/shard_map/ppermute | solution.py:282
  33.0 1.4 %collective-permute-start.3 = (bf16[160,768]{1,0:T(8,128)(2,1)S(1)}, bf16[160,768]{1,0:T(8,128)(2,1)S(1)}, u32[]{:S(2)}, u32[]{:S(2)}) collective-permute-start(bf16[160,768]{1,0:T(8,128)(2,1)S(1)} %get-tuple-element.20), channel_id=1, source_target_pairs={{0,8},{4,12},{8,0},{12,4},{1,9},{5,13},{9,1},{13,5},{2,10},{6,14},... | collective-permute-start | bytes 737288 | tf_op jit(solution)/shard_map/ppermute | solution.py:279
  34.4 5.4 %collective-permute-done.8.refs_2_ = bf16[160,768]{1,0:T(8,128)(2,1)S(1)} collective-permute-done((bf16[160,768]{1,0:T(8,128)(2,1)S(1)}, bf16[160,768]{1,0:T(8,128)(2,1)S(1)}, u32[]{:S(2)}, u32[]{:S(2)}) %collective-permute-start.8) | collective-permute-done | bytes 245792 | tf_op jit(solution)/shard_map/ppermute | solution.py:282
  39.9 3.3 %collective-permute-done.12.refs_6_ = bf16[160,768]{1,0:T(8,128)(2,1)} collective-permute-done((bf16[160,768]{1,0:T(8,128)(2,1)S(1)}, bf16[160,768]{1,0:T(8,128)(2,1)}, u32[]{:S(2)}, u32[]{:S(2)}) %collective-permute-start.12) | collective-permute-done | bytes 245792 | tf_op jit(solution)/shard_map/ppermute | solution.py:282
  43.7 1.9 %collective-permute-done.3.refs_1_ = bf16[160,768]{1,0:T(8,128)(2,1)S(1)} collective-permute-done((bf16[160,768]{1,0:T(8,128)(2,1)S(1)}, bf16[160,768]{1,0:T(8,128)(2,1)S(1)}, u32[]{:S(2)}, u32[]{:S(2)}) %collective-permute-start.3) | collective-permute-done | bytes 245792 | tf_op jit(solution)/shard_map/ppermute | solution.py:279
  45.7 1.4 %collective-permute-start.4 = (bf16[160,768]{1,0:T(8,128)(2,1)S(1)}, bf16[160,768]{1,0:T(8,128)(2,1)S(1)}, u32[]{:S(2)}, u32[]{:S(2)}) collective-permute-start(bf16[160,768]{1,0:T(8,128)(2,1)S(1)} %collective-permute-done.3.refs_1_), channel_id=1, source_target_pairs={{0,2},{1,3},{2,0},{3,1},{4,6},{5,7},{6,4},{7,5},{8,10},{9,11},{10,... | collective-permute-start | bytes 737288 | tf_op jit(solution)/shard_map/ppermute | solution.py:282
  47.7 5.9 %shard_map.92 = (f32[2,80,512]{2,1,0:T(8,128)}, f32[2,80,512]{2,1,0:T(8,128)}) custom-call(s32[10]{0:T(128)} %stack.79.at, bf16[2,3072,512]{2,1,0:T(8,128)(2,1)} %reshape.50.refs_0_, bf16[160,768]{1,0:T(8,128)(2,1)} %copy-done.1, bf16[160,768]{1,0:T(8,128)(2,1)} %copy-done.10, bf16[160,768]{1,0:T(8,128)(2,1)} %copy-done.12, ...), custom_call_target="tpu_custom_call" | custom-call | tf_op jit(solution)/shard_map/pallas_call | solution.py:161
  55.0 1.9 %collective-permute-start.15 = (f32[2,80,512]{2,1,0:T(8,128)}, f32[2,80,512]{2,1,0:T(8,128)}, u32[]{:S(2)}, u32[]{:S(2)}) collective-permute-start(f32[2,80,512]{2,1,0:T(8,128)} %get-tuple-element.25), channel_id=1, source_target_pairs={{0,4},{4,0},{8,12},{12,8},{1,5},{5,1},{9,13},{13,9},{2,6},{6,2},{1... | collective-permute-start | bytes 983048 | tf_op jit(solution)/shard_map/ppermute | solution.py:282
  57.0 5.5 %shard_map.90 = (f32[2,80,512]{2,1,0:T(8,128)}, f32[2,80,512]{2,1,0:T(8,128)}) custom-call(s32[7]{0:T(128)} %stack.71.at, bf16[2,3072,512]{2,1,0:T(8,128)(2,1)} %reshape.50.refs_0_, bf16[160,768]{1,0:T(8,128)(2,1)} %copy-done.8, bf16[160,768]{1,0:T(8,128)(2,1)} %copy-done.11, bf16[160,768]{1,0:T(8,128)(2,1)} %collective-permute-done.5.refs_3_, ...), custom_call_target="tpu_custom_call" | custom-call | tf_op jit(solution)/shard_map/pallas_call | solution.py:161
  62.6 3.0 %collective-permute-start.2 = (bf16[2,256,2,2,128]{4,3,2,1,0:T(2,128)(2,1)S(1)}, bf16[2,256,2,2,128]{4,3,2,1,0:T(2,128)(2,1)S(1)}, u32[]{:S(2)}, u32[]{:S(2)}) collective-permute-start(bf16[2,256,2,2,128]{4,3,2,1,0:T(2,128)(2,1)S(1)} %shard_map.88), channel_id=1, source_target_pairs={{0,8},{4,12},{8,0},{12,4},{1,9},{5,13},{9,1},{13,5},{2,10},{6,14},... | collective-permute-start | bytes 1572872 | tf_op jit(solution)/shard_map/ppermute | solution.py:279
  65.6 7.7 %collective-permute-done.16.refs_1_ = f32[2,80,512]{2,1,0:T(8,128)S(1)} collective-permute-done((f32[2,80,512]{2,1,0:T(8,128)}, f32[2,80,512]{2,1,0:T(8,128)S(1)}, u32[]{:S(2)}, u32[]{:S(2)}) %collective-permute-start.16) | collective-permute-done | bytes 327712 | tf_op jit(solution)/shard_map/ppermute | solution.py:282
  73.3 1.0 copy-done.6
  74.7 7.3 %collective-permute-done.15 = f32[2,80,512]{2,1,0:T(8,128)} collective-permute-done((f32[2,80,512]{2,1,0:T(8,128)}, f32[2,80,512]{2,1,0:T(8,128)}, u32[]{:S(2)}, u32[]{:S(2)}) %collective-permute-start.15) | collective-permute-done | bytes 327712 | tf_op jit(solution)/shard_map/ppermute | solution.py:282
  82.0 21.3 %collective-permute-done.17 = f32[2,80,512]{2,1,0:T(8,128)} collective-permute-done((f32[2,80,512]{2,1,0:T(8,128)S(1)}, f32[2,80,512]{2,1,0:T(8,128)}, u32[]{:S(2)}, u32[]{:S(2)}) %collective-permute-start.17) | collective-permute-done | bytes 327712 | tf_op jit(solution)/shard_map/ppermute | solution.py:279
  103.3 1.2 %add_convert_fusion = bf16[2,80,512]{2,1,0:T(8,128)(2,1)S(1)} fusion(f32[2,80,512]{2,1,0:T(8,128)} %collective-permute-done.17, f32[2,80,512]{2,1,0:T(8,128)} %get-tuple-element.22, f32[2,80,512]{2,1,0:T(8,128)} %collective-permute-done.15), kind=kLoop, calls=%fused_computation | loop fusion | flops 245760 | bytes 1146880 | tf_op jit(solution)/shard_map/convert_element_type | solution.py:335
  104.6 3.1 %shard_map.94 = (bf16[2,512,2,2,128]{4,3,2,1,0:T(2,128)(2,1)}, f32[1,320]{1,0:T(1,128)S(1)}) custom-call(s32[4]{0:T(128)S(1)} %get-tuple-element.31.starts, s32[4]{0:T(128)S(1)} %get-tuple-element.30.lengths, s32[160]{0:T(256)S(1)} %reshape.49.spots, bf16[2,256,2,2,128]{4,3,2,1,0:T(2,128)(2,1)S(1)} %copy-done.3, ...), custom_call_target="tpu_custom_call" | custom-call | tf_op jit(solution)/shard_map/pallas_call | solution.py:259
  107.7 5.7 %psum.7 = f32[1,320]{1,0:T(1,128)S(1)} all-reduce(f32[1,320]{1,0:T(1,128)S(1)} %get-tuple-element.29), channel_id=1, replica_groups=mesh['groups'=2,'hold'=4,'tp'=4] {'tp'}, use_global_device_ids=true, to_apply=%region_3.4 | all-reduce | flops 320 | bytes 2560 | tf_op jit(solution)/shard_map/psum | solution.py:345
  (70 shorter events, 6.5 us)
Async XLA Ops:
  4.4 38.8 %collective-permute-start = (bf16[2,256,2,2,128]{4,3,2,1,0:T(2,128)(2,1)}, bf16[2,256,2,2,128]{4,3,2,1,0:T(2,128)(2,1)S(1)}, u32[]{:S(2)}, u32[]{:S(2)}) collective-permute-start(bf16[2,256,2,2,128]{4,3,2,1,0:T(2,128)(2,1)} %get-tuple-element.18), channel_id=1, source_target_pairs={{0,12},{4,0},{8,4},{12,8},{1,13},{5,1},{9,5},{13,9},{2,14},{6,2},{... | collective-permute-start | bytes 1572872 | tf_op jit(solution)/shard_map/ppermute | solution.py:279
  16.3 14.7 %collective-permute-start.7 = (bf16[160,768]{1,0:T(8,128)(2,1)S(1)}, bf16[160,768]{1,0:T(8,128)(2,1)S(1)}, u32[]{:S(2)}, u32[]{:S(2)}) collective-permute-start(bf16[160,768]{1,0:T(8,128)(2,1)S(1)} %get-tuple-element.23), channel_id=1, source_target_pairs={{0,4},{4,8},{8,12},{12,0},{1,5},{5,9},{9,13},{13,1},{2,6},{6,10},{... | collective-permute-start | bytes 737288 | tf_op jit(solution)/shard_map/ppermute | solution.py:279
  16.3 27.4 %copy-start.5 = (bf16[2,256,2,2,128]{4,3,2,1,0:T(2,128)(2,1)S(1)}, bf16[2,256,2,2,128]{4,3,2,1,0:T(2,128)(2,1)}, u32[]{:S(2)}) copy-start(bf16[2,256,2,2,128]{4,3,2,1,0:T(2,128)(2,1)} %get-tuple-element.17.refs_0_) | copy-start | bytes 1572868
  16.3 16.2 %collective-permute-start.11 = (bf16[160,768]{1,0:T(8,128)(2,1)S(1)}, bf16[160,768]{1,0:T(8,128)(2,1)S(1)}, u32[]{:S(2)}, u32[]{:S(2)}) collective-permute-start(bf16[160,768]{1,0:T(8,128)(2,1)S(1)} %get-tuple-element.24), channel_id=1, source_target_pairs={{0,12},{4,0},{8,4},{12,8},{1,13},{5,1},{9,5},{13,9},{2,14},{6,2},{... | collective-permute-start | bytes 737288 | tf_op jit(solution)/shard_map/ppermute | solution.py:279
  30.3 24.0 %copy-start.14 = (s32[1,4]{1,0:T(1,128)S(1)}, s32[1,4]{1,0:T(1,128)}, u32[]{:S(2)}) copy-start(s32[1,4]{1,0:T(1,128)} %param.8) | copy-start | bytes 52
  30.3 24.7 %copy-start.13 = (s32[2,80]{1,0:T(2,128)S(1)}, s32[2,80]{1,0:T(2,128)}, u32[]{:S(2)}) copy-start(s32[2,80]{1,0:T(2,128)} %param.10) | copy-start | bytes 1924
  31.0 16.7 %copy-start.1 = (bf16[160,768]{1,0:T(8,128)(2,1)}, bf16[160,768]{1,0:T(8,128)(2,1)S(1)}, u32[]{:S(2)}) copy-start(bf16[160,768]{1,0:T(8,128)(2,1)S(1)} %shard_map.91.refs_1_) | copy-start | bytes 737284
  31.0 8.9 %collective-permute-start.8 = (bf16[160,768]{1,0:T(8,128)(2,1)S(1)}, bf16[160,768]{1,0:T(8,128)(2,1)S(1)}, u32[]{:S(2)}, u32[]{:S(2)}) collective-permute-start(bf16[160,768]{1,0:T(8,128)(2,1)S(1)} %shard_map.91.refs_1_), channel_id=1, source_target_pairs={{0,2},{1,3},{2,0},{3,1},{4,6},{5,7},{6,4},{7,5},{8,10},{9,11},{10,... | collective-permute-start | bytes 737288 | tf_op jit(solution)/shard_map/ppermute | solution.py:282
  32.5 10.7 %collective-permute-start.12 = (bf16[160,768]{1,0:T(8,128)(2,1)S(1)}, bf16[160,768]{1,0:T(8,128)(2,1)}, u32[]{:S(2)}, u32[]{:S(2)}) collective-permute-start(bf16[160,768]{1,0:T(8,128)(2,1)S(1)} %collective-permute-done.11.refs_5_), channel_id=1, source_target_pairs={{0,2},{1,3},{2,0},{3,1},{4,6},{5,7},{6,4},{7,5},{8,10},{9,11},{10,... | collective-permute-start | bytes 737288 | tf_op jit(solution)/shard_map/ppermute | solution.py:282
  33.0 12.7 %collective-permute-start.3 = (bf16[160,768]{1,0:T(8,128)(2,1)S(1)}, bf16[160,768]{1,0:T(8,128)(2,1)S(1)}, u32[]{:S(2)}, u32[]{:S(2)}) collective-permute-start(bf16[160,768]{1,0:T(8,128)(2,1)S(1)} %get-tuple-element.20), channel_id=1, source_target_pairs={{0,8},{4,12},{8,0},{12,4},{1,9},{5,13},{9,1},{13,5},{2,10},{6,14},... | collective-permute-start | bytes 737288 | tf_op jit(solution)/shard_map/ppermute | solution.py:279
  34.4 11.2 %collective-permute-start.9 = (bf16[160,768]{1,0:T(8,128)(2,1)S(1)}, bf16[160,768]{1,0:T(8,128)(2,1)S(1)}, u32[]{:S(2)}, u32[]{:S(2)}) collective-permute-start(bf16[160,768]{1,0:T(8,128)(2,1)S(1)} %shard_map.91.refs_1_), channel_id=1, source_target_pairs={{0,1},{1,0},{2,3},{3,2},{4,5},{5,4},{6,7},{7,6},{8,9},{9,8},{10,11... | collective-permute-start | bytes 737288 | tf_op jit(solution)/shard_map/ppermute | solution.py:282
  39.9 7.8 %collective-permute-start.13 = (bf16[160,768]{1,0:T(8,128)(2,1)S(1)}, bf16[160,768]{1,0:T(8,128)(2,1)}, u32[]{:S(2)}, u32[]{:S(2)}) collective-permute-start(bf16[160,768]{1,0:T(8,128)(2,1)S(1)} %collective-permute-done.11.refs_5_), channel_id=1, source_target_pairs={{0,1},{1,0},{2,3},{3,2},{4,5},{5,4},{6,7},{7,6},{8,9},{9,8},{10,11... | collective-permute-start | bytes 737288 | tf_op jit(solution)/shard_map/ppermute | solution.py:282
  43.2 4.4 %collective-permute-start.10 = (bf16[160,768]{1,0:T(8,128)(2,1)S(1)}, bf16[160,768]{1,0:T(8,128)(2,1)}, u32[]{:S(2)}, u32[]{:S(2)}) collective-permute-start(bf16[160,768]{1,0:T(8,128)(2,1)S(1)} %collective-permute-done.8.refs_2_), channel_id=1, source_target_pairs={{0,1},{1,0},{2,3},{3,2},{4,5},{5,4},{6,7},{7,6},{8,9},{9,8},{10,11... | collective-permute-start | bytes 737288 | tf_op jit(solution)/shard_map/ppermute | solution.py:282
  43.2 4.4 %collective-permute-start.14 = (bf16[160,768]{1,0:T(8,128)(2,1)}, bf16[160,768]{1,0:T(8,128)(2,1)}, u32[]{:S(2)}, u32[]{:S(2)}) collective-permute-start(bf16[160,768]{1,0:T(8,128)(2,1)} %collective-permute-done.12.refs_6_), channel_id=1, source_target_pairs={{0,1},{1,0},{2,3},{3,2},{4,5},{5,4},{6,7},{7,6},{8,9},{9,8},{10,11... | collective-permute-start | bytes 737288 | tf_op jit(solution)/shard_map/ppermute | solution.py:282
  45.7 16.8 %collective-permute-start.1 = (bf16[2,256,2,2,128]{4,3,2,1,0:T(2,128)(2,1)S(1)}, bf16[2,256,2,2,128]{4,3,2,1,0:T(2,128)(2,1)S(1)}, u32[]{:S(2)}, u32[]{:S(2)}) collective-permute-start(bf16[2,256,2,2,128]{4,3,2,1,0:T(2,128)(2,1)S(1)} %shard_map.87), channel_id=1, source_target_pairs={{0,4},{4,8},{8,12},{12,0},{1,5},{5,9},{9,13},{13,1},{2,6},{6,10},{... | collective-permute-start | bytes 1572872 | tf_op jit(solution)/shard_map/ppermute | solution.py:279
  45.7 8.0 %collective-permute-start.4 = (bf16[160,768]{1,0:T(8,128)(2,1)S(1)}, bf16[160,768]{1,0:T(8,128)(2,1)S(1)}, u32[]{:S(2)}, u32[]{:S(2)}) collective-permute-start(bf16[160,768]{1,0:T(8,128)(2,1)S(1)} %collective-permute-done.3.refs_1_), channel_id=1, source_target_pairs={{0,2},{1,3},{2,0},{3,1},{4,6},{5,7},{6,4},{7,5},{8,10},{9,11},{10,... | collective-permute-start | bytes 737288 | tf_op jit(solution)/shard_map/ppermute | solution.py:282
  53.6 20.9 %copy-start.15 = (s32[1,4]{1,0:T(1,128)S(1)}, s32[1,4]{1,0:T(1,128)}, u32[]{:S(2)}) copy-start(s32[1,4]{1,0:T(1,128)} %param.9) | copy-start | bytes 52
  53.6 51.0 %copy-start.3 = (bf16[2,256,2,2,128]{4,3,2,1,0:T(2,128)(2,1)S(1)}, bf16[2,256,2,2,128]{4,3,2,1,0:T(2,128)(2,1)}, u32[]{:S(2)}) copy-start(bf16[2,256,2,2,128]{4,3,2,1,0:T(2,128)(2,1)} %get-tuple-element.16.refs_0_) | copy-start | bytes 1572868
  53.6 19.7 %collective-permute-start.16 = (f32[2,80,512]{2,1,0:T(8,128)}, f32[2,80,512]{2,1,0:T(8,128)S(1)}, u32[]{:S(2)}, u32[]{:S(2)}) collective-permute-start(f32[2,80,512]{2,1,0:T(8,128)} %get-tuple-element.27), channel_id=1, source_target_pairs={{0,4},{4,0},{8,12},{12,8},{1,5},{5,1},{9,13},{13,9},{2,6},{6,2},{1... | collective-permute-start | bytes 983048 | tf_op jit(solution)/shard_map/ppermute | solution.py:282
  53.7 3.3 %collective-permute-start.5 = (bf16[160,768]{1,0:T(8,128)(2,1)S(1)}, bf16[160,768]{1,0:T(8,128)(2,1)}, u32[]{:S(2)}, u32[]{:S(2)}) collective-permute-start(bf16[160,768]{1,0:T(8,128)(2,1)S(1)} %collective-permute-done.3.refs_1_), channel_id=1, source_target_pairs={{0,1},{1,0},{2,3},{3,2},{4,5},{5,4},{6,7},{7,6},{8,9},{9,8},{10,11... | collective-permute-start | bytes 737288 | tf_op jit(solution)/shard_map/ppermute | solution.py:282
  53.8 3.2 %collective-permute-start.6 = (bf16[160,768]{1,0:T(8,128)(2,1)S(1)}, bf16[160,768]{1,0:T(8,128)(2,1)}, u32[]{:S(2)}, u32[]{:S(2)}) collective-permute-start(bf16[160,768]{1,0:T(8,128)(2,1)S(1)} %collective-permute-done.4.refs_2_), channel_id=1, source_target_pairs={{0,1},{1,0},{2,3},{3,2},{4,5},{5,4},{6,7},{7,6},{8,9},{9,8},{10,11... | collective-permute-start | bytes 737288 | tf_op jit(solution)/shard_map/ppermute | solution.py:282
  55.0 26.9 %collective-permute-start.15 = (f32[2,80,512]{2,1,0:T(8,128)}, f32[2,80,512]{2,1,0:T(8,128)}, u32[]{:S(2)}, u32[]{:S(2)}) collective-permute-start(f32[2,80,512]{2,1,0:T(8,128)} %get-tuple-element.25), channel_id=1, source_target_pairs={{0,4},{4,0},{8,12},{12,8},{1,5},{5,1},{9,13},{13,9},{2,6},{6,2},{1... | collective-permute-start | bytes 983048 | tf_op jit(solution)/shard_map/ppermute | solution.py:282
  62.6 42.0 %collective-permute-start.2 = (bf16[2,256,2,2,128]{4,3,2,1,0:T(2,128)(2,1)S(1)}, bf16[2,256,2,2,128]{4,3,2,1,0:T(2,128)(2,1)S(1)}, u32[]{:S(2)}, u32[]{:S(2)}) collective-permute-start(bf16[2,256,2,2,128]{4,3,2,1,0:T(2,128)(2,1)S(1)} %shard_map.88), channel_id=1, source_target_pairs={{0,8},{4,12},{8,0},{12,4},{1,9},{5,13},{9,1},{13,5},{2,10},{6,14},... | collective-permute-start | bytes 1572872 | tf_op jit(solution)/shard_map/ppermute | solution.py:279
  74.3 29.0 %collective-permute-start.17 = (f32[2,80,512]{2,1,0:T(8,128)S(1)}, f32[2,80,512]{2,1,0:T(8,128)}, u32[]{:S(2)}, u32[]{:S(2)}) collective-permute-start(f32[2,80,512]{2,1,0:T(8,128)S(1)} %shard_map.93), channel_id=1, source_target_pairs={{0,8},{4,12},{8,0},{12,4},{1,9},{5,13},{9,1},{13,5},{2,10},{6,14},... | collective-permute-start | bytes 983048 | tf_op jit(solution)/shard_map/ppermute | solution.py:279
  (10 other events, 58.6 us)

commit v7 on v6

--- a/solution.py
+++ b/solution.py
@@ -15,7 +15,6 @@
 UNROLL = 8
 CUTS = 3
 VMEM_BYTES = 16 * 1024 * 1024
-FREE = pl.CostEstimate(flops=0, bytes_accessed=0, transcendentals=0)
 PARAMS = pltpu.CompilerParams(vmem_limit_bytes=VMEM_BYTES)
 WIDE = pltpu.CompilerParams(vmem_limit_bytes=60 * 1024 * 1024)
 ANY = pl.BlockSpec(memory_space=pl.ANY)
@@ -52,7 +51,6 @@
         in_specs=[SMEM, VMEM, VMEM],
         out_specs=[VMEM] * n,
         out_shape=[jax.ShapeDtypeStruct((rows, size), jnp.bfloat16) for size in sizes],
-        cost_estimate=FREE,
         compiler_params=PARAMS,
     )(at.astype(jnp.int32), hidden.reshape(rows, width), gain)
 
@@ -68,7 +66,6 @@
         out_specs=ANY,
         out_shape=jax.ShapeDtypeStruct(value.shape, value.dtype),
         input_output_aliases={0: 0},
-        cost_estimate=FREE,
         compiler_params=PARAMS,
     )(value, *after)
 
@@ -110,7 +107,6 @@
         out_shape=[
             jax.ShapeDtypeStruct((count,) + store.shape[2:], store.dtype) for count in counts
         ],
-        cost_estimate=FREE,
         compiler_params=WIDE,
     )(jnp.stack(at).astype(jnp.int32), store)
 
@@ -169,7 +165,6 @@
             pltpu.SemaphoreType.DMA((len(flat), layers)),
             pltpu.SemaphoreType.DMA((layers, CUTS)),
         ],
-        cost_estimate=FREE,
         compiler_params=WIDE,
     )(at, weight, *flat)
 
@@ -187,7 +182,6 @@
         in_specs=[VMEM] * (2 * count),
         out_specs=[VMEM] * count,
         out_shape=[jax.ShapeDtypeStruct(value.shape, value.dtype) for value in left],
-        cost_estimate=FREE,
         compiler_params=PARAMS,
     )(*left, *right)
 
@@ -269,7 +263,6 @@
             pltpu.VMEM((2 * layers * rec, rows[-1]), jnp.float32),
             pltpu.SemaphoreType.DMA((len(flat),)),
         ],
-        cost_estimate=FREE,
         compiler_params=PARAMS,
     )(starts, lengths, spots, *flat, fresh)
 

time: 115 us -> 115 us (level)
  no operation moved by 1% of the time
where the time goes in v7:
time: 115 us; the launch traced here: 114 us
  waiting for transfers between devices  47 us (41%)
  Pallas kernels  20.5 us (18%)
  starting transfers between devices  19.9 us (17%)
  local copies, waits for them, and re-layouts  17.6 us (15%)
  blocking collectives  5.67 us (5%)
  other arithmetic  2.4 us (2%)
    ppermute x11, waiting for transfers between devices, swap(): return lax.ppermute(value, axis, [(i, i ^ bit) for i in range(size)])  23.8 us
    ppermute x7, waiting for transfers between devices, shift(): return lax.ppermute(value, 'hold', [(i, (i + k) % n) for i in range(n)])  23.2 us
    ppermute x7, starting transfers between devices, shift(): return lax.ppermute(value, 'hold', [(i, (i + k) % n) for i in range(n)])  13.4 us
    pallas_call x2, Pallas kernels, products(): pl.pallas_call(functools.partial(product_kernel, counts), in_specs=[SMEM]...  11.4 us
    reshape x1, local copies, waits for them, and re-layouts, local(): weight = kv_weight.reshape(LAYERS, feats, cols)  10.1 us
    ppermute x11, starting transfers between devices, swap(): return lax.ppermute(value, axis, [(i, i ^ bit) for i in range(size)])  6.48 us
    psum x1, blocking collectives, local(): sums = lax.psum(sums, 'tp').reshape(2, LAYERS, rec)  5.67 us
    unnamed x32, local copies, waits for them, and re-layouts  4.87 us
  transfers between devices with their start and end apart: 18, of which 6 were waited for; matrix products, arithmetic and copies ran while one was open for 12% of the time, Pallas kernels for 13%

profile of v7, /device:TPU:0, one launch (start us, length us, event | category | flops | bytes accessed | tf_op | source)
XLA Modules:
  0.0 114.1 jit_solution(9881965699937196734)
XLA Ops:
  1.3 3.1 %shard_map.86 = (bf16[2,256,2,2,128]{4,3,2,1,0:T(2,128)(2,1)}, bf16[2,256,2,2,128]{4,3,2,1,0:T(2,128)(2,1)}, bf16[2,256,2,2,128]{4,3,2,1,0:T(2,128)(2,1)}, bf16[2,256,2,2,128]{4,3,2,1,0:T(2,128)(2,1)}) custom-call(s32[4]{0:T(128)} %pad_add_fusion.at, bf16[2,4,256,2,2,128]{5,4,3,2,1,0:T(2,128)(2,1)} %store.1), custom_call_target="tpu_custom_call" | custom-call | tf_op jit(solution)/shard_map/pallas_call | solution.py:95
  4.4 5.1 %collective-permute-start = (bf16[2,256,2,2,128]{4,3,2,1,0:T(2,128)(2,1)}, bf16[2,256,2,2,128]{4,3,2,1,0:T(2,128)(2,1)S(1)}, u32[]{:S(2)}, u32[]{:S(2)}) collective-permute-start(bf16[2,256,2,2,128]{4,3,2,1,0:T(2,128)(2,1)} %get-tuple-element.18), channel_id=1, source_target_pairs={{0,12},{4,0},{8,4},{12,8},{1,13},{5,1},{9,5},{13,9},{2,14},{6,2},{... | collective-permute-start | bytes 1572872 | tf_op jit(solution)/shard_map/ppermute | solution.py:272
  9.6 2.1 %copy-done = bf16[2,80,12288]{2,1,0:T(8,128)(2,1)S(1)} copy-done((bf16[2,80,12288]{2,1,0:T(8,128)(2,1)S(1)}, bf16[2,80,12288]{2,1,0:T(8,128)(2,1)}, u32[]{:S(2)}) %copy-start) | copy-done | bytes 3932184
  12.5 2.9 %shard_map.89 = (bf16[160,3072]{1,0:T(8,128)(2,1)S(1)}, bf16[160,768]{1,0:T(8,128)(2,1)S(1)}, bf16[160,768]{1,0:T(8,128)(2,1)S(1)}, bf16[160,768]{1,0:T(8,128)(2,1)S(1)}) custom-call(s32[4]{0:T(128)S(1)} %pad_add_fusion.1.at, bf16[160,12288]{1,0:T(8,128)(2,1)S(1)} %bitcast.19, bf16[2,12288]{1,0:T(2,128)(2,1)S(1)} %copy-done.7), custom_call_target="tpu_custom_call" | custom-call | tf_op jit(solution)/shard_map/pallas_call | solution.py:49
  15.4 0.9 copy-done.2
  16.3 3.8 %collective-permute-start.11 = (bf16[160,768]{1,0:T(8,128)(2,1)S(1)}, bf16[160,768]{1,0:T(8,128)(2,1)S(1)}, u32[]{:S(2)}, u32[]{:S(2)}) collective-permute-start(bf16[160,768]{1,0:T(8,128)(2,1)S(1)} %get-tuple-element.24), channel_id=1, source_target_pairs={{0,12},{4,0},{8,4},{12,8},{1,13},{5,1},{9,5},{13,9},{2,14},{6,2},{... | collective-permute-start | bytes 737288 | tf_op jit(solution)/shard_map/ppermute | solution.py:272
  20.1 10.1 %reshape.50.refs_0_ = bf16[2,3072,512]{2,1,0:T(8,128)(2,1)} reshape(bf16[2,3072,2,2,128]{4,3,2,1,0:T(2,128)(2,1)} %param.13) | data formatting | bytes 12582912 | tf_op jit(solution)/shard_map/reshape | solution.py:303
  31.0 1.5 %collective-permute-start.8 = (bf16[160,768]{1,0:T(8,128)(2,1)S(1)}, bf16[160,768]{1,0:T(8,128)(2,1)S(1)}, u32[]{:S(2)}, u32[]{:S(2)}) collective-permute-start(bf16[160,768]{1,0:T(8,128)(2,1)S(1)} %shard_map.91.refs_1_), channel_id=1, source_target_pairs={{0,2},{1,3},{2,0},{3,1},{4,6},{5,7},{6,4},{7,5},{8,10},{9,11},{10,... | collective-permute-start | bytes 737288 | tf_op jit(solution)/shard_map/ppermute | solution.py:275
  33.0 1.4 %collective-permute-start.3 = (bf16[160,768]{1,0:T(8,128)(2,1)S(1)}, bf16[160,768]{1,0:T(8,128)(2,1)S(1)}, u32[]{:S(2)}, u32[]{:S(2)}) collective-permute-start(bf16[160,768]{1,0:T(8,128)(2,1)S(1)} %get-tuple-element.20), channel_id=1, source_target_pairs={{0,8},{4,12},{8,0},{12,4},{1,9},{5,13},{9,1},{13,5},{2,10},{6,14},... | collective-permute-start | bytes 737288 | tf_op jit(solution)/shard_map/ppermute | solution.py:272
  34.4 5.4 %collective-permute-done.8.refs_2_ = bf16[160,768]{1,0:T(8,128)(2,1)S(1)} collective-permute-done((bf16[160,768]{1,0:T(8,128)(2,1)S(1)}, bf16[160,768]{1,0:T(8,128)(2,1)S(1)}, u32[]{:S(2)}, u32[]{:S(2)}) %collective-permute-start.8) | collective-permute-done | bytes 245792 | tf_op jit(solution)/shard_map/ppermute | solution.py:275
  39.9 3.3 %collective-permute-done.12.refs_6_ = bf16[160,768]{1,0:T(8,128)(2,1)} collective-permute-done((bf16[160,768]{1,0:T(8,128)(2,1)S(1)}, bf16[160,768]{1,0:T(8,128)(2,1)}, u32[]{:S(2)}, u32[]{:S(2)}) %collective-permute-start.12) | collective-permute-done | bytes 245792 | tf_op jit(solution)/shard_map/ppermute | solution.py:275
  43.7 1.9 %collective-permute-done.3.refs_1_ = bf16[160,768]{1,0:T(8,128)(2,1)S(1)} collective-permute-done((bf16[160,768]{1,0:T(8,128)(2,1)S(1)}, bf16[160,768]{1,0:T(8,128)(2,1)S(1)}, u32[]{:S(2)}, u32[]{:S(2)}) %collective-permute-start.3) | collective-permute-done | bytes 245792 | tf_op jit(solution)/shard_map/ppermute | solution.py:272
  45.7 1.4 %collective-permute-start.4 = (bf16[160,768]{1,0:T(8,128)(2,1)S(1)}, bf16[160,768]{1,0:T(8,128)(2,1)S(1)}, u32[]{:S(2)}, u32[]{:S(2)}) collective-permute-start(bf16[160,768]{1,0:T(8,128)(2,1)S(1)} %collective-permute-done.3.refs_1_), channel_id=1, source_target_pairs={{0,2},{1,3},{2,0},{3,1},{4,6},{5,7},{6,4},{7,5},{8,10},{9,11},{10,... | collective-permute-start | bytes 737288 | tf_op jit(solution)/shard_map/ppermute | solution.py:275
  47.7 5.9 %shard_map.92 = (f32[2,80,512]{2,1,0:T(8,128)}, f32[2,80,512]{2,1,0:T(8,128)}) custom-call(s32[10]{0:T(128)} %stack.79.at, bf16[2,3072,512]{2,1,0:T(8,128)(2,1)} %reshape.50.refs_0_, bf16[160,768]{1,0:T(8,128)(2,1)} %copy-done.1, bf16[160,768]{1,0:T(8,128)(2,1)} %copy-done.10, bf16[160,768]{1,0:T(8,128)(2,1)} %copy-done.12, ...), custom_call_target="tpu_custom_call" | custom-call | tf_op jit(solution)/shard_map/pallas_call | solution.py:157
  55.0 1.9 %collective-permute-start.15 = (f32[2,80,512]{2,1,0:T(8,128)}, f32[2,80,512]{2,1,0:T(8,128)}, u32[]{:S(2)}, u32[]{:S(2)}) collective-permute-start(f32[2,80,512]{2,1,0:T(8,128)} %get-tuple-element.25), channel_id=1, source_target_pairs={{0,4},{4,0},{8,12},{12,8},{1,5},{5,1},{9,13},{13,9},{2,6},{6,2},{1... | collective-permute-start | bytes 983048 | tf_op jit(solution)/shard_map/ppermute | solution.py:275
  57.0 5.5 %shard_map.90 = (f32[2,80,512]{2,1,0:T(8,128)}, f32[2,80,512]{2,1,0:T(8,128)}) custom-call(s32[7]{0:T(128)} %stack.71.at, bf16[2,3072,512]{2,1,0:T(8,128)(2,1)} %reshape.50.refs_0_, bf16[160,768]{1,0:T(8,128)(2,1)} %copy-done.8, bf16[160,768]{1,0:T(8,128)(2,1)} %copy-done.11, bf16[160,768]{1,0:T(8,128)(2,1)} %collective-permute-done.5.refs_3_, ...), custom_call_target="tpu_custom_call" | custom-call | tf_op jit(solution)/shard_map/pallas_call | solution.py:157
  62.6 3.0 %collective-permute-start.2 = (bf16[2,256,2,2,128]{4,3,2,1,0:T(2,128)(2,1)S(1)}, bf16[2,256,2,2,128]{4,3,2,1,0:T(2,128)(2,1)S(1)}, u32[]{:S(2)}, u32[]{:S(2)}) collective-permute-start(bf16[2,256,2,2,128]{4,3,2,1,0:T(2,128)(2,1)S(1)} %shard_map.88), channel_id=1, source_target_pairs={{0,8},{4,12},{8,0},{12,4},{1,9},{5,13},{9,1},{13,5},{2,10},{6,14},... | collective-permute-start | bytes 1572872 | tf_op jit(solution)/shard_map/ppermute | solution.py:272
  65.6 7.7 %collective-permute-done.16.refs_1_ = f32[2,80,512]{2,1,0:T(8,128)S(1)} collective-permute-done((f32[2,80,512]{2,1,0:T(8,128)}, f32[2,80,512]{2,1,0:T(8,128)S(1)}, u32[]{:S(2)}, u32[]{:S(2)}) %collective-permute-start.16) | collective-permute-done | bytes 327712 | tf_op jit(solution)/shard_map/ppermute | solution.py:275
  73.3 1.0 copy-done.6
  74.7 7.3 %collective-permute-done.15 = f32[2,80,512]{2,1,0:T(8,128)} collective-permute-done((f32[2,80,512]{2,1,0:T(8,128)}, f32[2,80,512]{2,1,0:T(8,128)}, u32[]{:S(2)}, u32[]{:S(2)}) %collective-permute-start.15) | collective-permute-done | bytes 327712 | tf_op jit(solution)/shard_map/ppermute | solution.py:275
  82.0 21.3 %collective-permute-done.17 = f32[2,80,512]{2,1,0:T(8,128)} collective-permute-done((f32[2,80,512]{2,1,0:T(8,128)S(1)}, f32[2,80,512]{2,1,0:T(8,128)}, u32[]{:S(2)}, u32[]{:S(2)}) %collective-permute-start.17) | collective-permute-done | bytes 327712 | tf_op jit(solution)/shard_map/ppermute | solution.py:272
  103.3 1.2 %add_convert_fusion = bf16[2,80,512]{2,1,0:T(8,128)(2,1)S(1)} fusion(f32[2,80,512]{2,1,0:T(8,128)} %collective-permute-done.17, f32[2,80,512]{2,1,0:T(8,128)} %get-tuple-element.22, f32[2,80,512]{2,1,0:T(8,128)} %collective-permute-done.15), kind=kLoop, calls=%fused_computation | loop fusion | flops 245760 | bytes 1146880 | tf_op jit(solution)/shard_map/convert_element_type | solution.py:328
  104.6 3.1 %shard_map.94 = (bf16[2,512,2,2,128]{4,3,2,1,0:T(2,128)(2,1)}, f32[1,320]{1,0:T(1,128)S(1)}) custom-call(s32[4]{0:T(128)S(1)} %get-tuple-element.31.starts, s32[4]{0:T(128)S(1)} %get-tuple-element.30.lengths, s32[160]{0:T(256)S(1)} %reshape.49.spots, bf16[2,256,2,2,128]{4,3,2,1,0:T(2,128)(2,1)S(1)} %copy-done.3, ...), custom_call_target="tpu_custom_call" | custom-call | tf_op jit(solution)/shard_map/pallas_call | solution.py:253
  107.7 5.7 %psum.7 = f32[1,320]{1,0:T(1,128)S(1)} all-reduce(f32[1,320]{1,0:T(1,128)S(1)} %get-tuple-element.29), channel_id=1, replica_groups=mesh['groups'=2,'hold'=4,'tp'=4] {'tp'}, use_global_device_ids=true, to_apply=%region_3.4 | all-reduce | flops 320 | bytes 2560 | tf_op jit(solution)/shard_map/psum | solution.py:338
  (70 shorter events, 6.5 us)
Async XLA Ops:
  4.4 38.8 %collective-permute-start = (bf16[2,256,2,2,128]{4,3,2,1,0:T(2,128)(2,1)}, bf16[2,256,2,2,128]{4,3,2,1,0:T(2,128)(2,1)S(1)}, u32[]{:S(2)}, u32[]{:S(2)}) collective-permute-start(bf16[2,256,2,2,128]{4,3,2,1,0:T(2,128)(2,1)} %get-tuple-element.18), channel_id=1, source_target_pairs={{0,12},{4,0},{8,4},{12,8},{1,13},{5,1},{9,5},{13,9},{2,14},{6,2},{... | collective-permute-start | bytes 1572872 | tf_op jit(solution)/shard_map/ppermute | solution.py:272
  16.3 14.7 %collective-permute-start.7 = (bf16[160,768]{1,0:T(8,128)(2,1)S(1)}, bf16[160,768]{1,0:T(8,128)(2,1)S(1)}, u32[]{:S(2)}, u32[]{:S(2)}) collective-permute-start(bf16[160,768]{1,0:T(8,128)(2,1)S(1)} %get-tuple-element.23), channel_id=1, source_target_pairs={{0,4},{4,8},{8,12},{12,0},{1,5},{5,9},{9,13},{13,1},{2,6},{6,10},{... | collective-permute-start | bytes 737288 | tf_op jit(solution)/shard_map/ppermute | solution.py:272
  16.3 27.4 %copy-start.5 = (bf16[2,256,2,2,128]{4,3,2,1,0:T(2,128)(2,1)S(1)}, bf16[2,256,2,2,128]{4,3,2,1,0:T(2,128)(2,1)}, u32[]{:S(2)}) copy-start(bf16[2,256,2,2,128]{4,3,2,1,0:T(2,128)(2,1)} %get-tuple-element.17.refs_0_) | copy-start | bytes 1572868
  16.3 16.2 %collective-permute-start.11 = (bf16[160,768]{1,0:T(8,128)(2,1)S(1)}, bf16[160,768]{1,0:T(8,128)(2,1)S(1)}, u32[]{:S(2)}, u32[]{:S(2)}) collective-permute-start(bf16[160,768]{1,0:T(8,128)(2,1)S(1)} %get-tuple-element.24), channel_id=1, source_target_pairs={{0,12},{4,0},{8,4},{12,8},{1,13},{5,1},{9,5},{13,9},{2,14},{6,2},{... | collective-permute-start | bytes 737288 | tf_op jit(solution)/shard_map/ppermute | solution.py:272
  30.3 24.0 %copy-start.14 = (s32[1,4]{1,0:T(1,128)S(1)}, s32[1,4]{1,0:T(1,128)}, u32[]{:S(2)}) copy-start(s32[1,4]{1,0:T(1,128)} %param.8) | copy-start | bytes 52
  30.3 24.7 %copy-start.13 = (s32[2,80]{1,0:T(2,128)S(1)}, s32[2,80]{1,0:T(2,128)}, u32[]{:S(2)}) copy-start(s32[2,80]{1,0:T(2,128)} %param.10) | copy-start | bytes 1924
  31.0 16.7 %copy-start.1 = (bf16[160,768]{1,0:T(8,128)(2,1)}, bf16[160,768]{1,0:T(8,128)(2,1)S(1)}, u32[]{:S(2)}) copy-start(bf16[160,768]{1,0:T(8,128)(2,1)S(1)} %shard_map.91.refs_1_) | copy-start | bytes 737284
  31.0 8.9 %collective-permute-start.8 = (bf16[160,768]{1,0:T(8,128)(2,1)S(1)}, bf16[160,768]{1,0:T(8,128)(2,1)S(1)}, u32[]{:S(2)}, u32[]{:S(2)}) collective-permute-start(bf16[160,768]{1,0:T(8,128)(2,1)S(1)} %shard_map.91.refs_1_), channel_id=1, source_target_pairs={{0,2},{1,3},{2,0},{3,1},{4,6},{5,7},{6,4},{7,5},{8,10},{9,11},{10,... | collective-permute-start | bytes 737288 | tf_op jit(solution)/shard_map/ppermute | solution.py:275
  32.5 10.7 %collective-permute-start.12 = (bf16[160,768]{1,0:T(8,128)(2,1)S(1)}, bf16[160,768]{1,0:T(8,128)(2,1)}, u32[]{:S(2)}, u32[]{:S(2)}) collective-permute-start(bf16[160,768]{1,0:T(8,128)(2,1)S(1)} %collective-permute-done.11.refs_5_), channel_id=1, source_target_pairs={{0,2},{1,3},{2,0},{3,1},{4,6},{5,7},{6,4},{7,5},{8,10},{9,11},{10,... | collective-permute-start | bytes 737288 | tf_op jit(solution)/shard_map/ppermute | solution.py:275
  33.0 12.7 %collective-permute-start.3 = (bf16[160,768]{1,0:T(8,128)(2,1)S(1)}, bf16[160,768]{1,0:T(8,128)(2,1)S(1)}, u32[]{:S(2)}, u32[]{:S(2)}) collective-permute-start(bf16[160,768]{1,0:T(8,128)(2,1)S(1)} %get-tuple-element.20), channel_id=1, source_target_pairs={{0,8},{4,12},{8,0},{12,4},{1,9},{5,13},{9,1},{13,5},{2,10},{6,14},... | collective-permute-start | bytes 737288 | tf_op jit(solution)/shard_map/ppermute | solution.py:272
  34.4 11.2 %collective-permute-start.9 = (bf16[160,768]{1,0:T(8,128)(2,1)S(1)}, bf16[160,768]{1,0:T(8,128)(2,1)S(1)}, u32[]{:S(2)}, u32[]{:S(2)}) collective-permute-start(bf16[160,768]{1,0:T(8,128)(2,1)S(1)} %shard_map.91.refs_1_), channel_id=1, source_target_pairs={{0,1},{1,0},{2,3},{3,2},{4,5},{5,4},{6,7},{7,6},{8,9},{9,8},{10,11... | collective-permute-start | bytes 737288 | tf_op jit(solution)/shard_map/ppermute | solution.py:275
  39.9 7.8 %collective-permute-start.13 = (bf16[160,768]{1,0:T(8,128)(2,1)S(1)}, bf16[160,768]{1,0:T(8,128)(2,1)}, u32[]{:S(2)}, u32[]{:S(2)}) collective-permute-start(bf16[160,768]{1,0:T(8,128)(2,1)S(1)} %collective-permute-done.11.refs_5_), channel_id=1, source_target_pairs={{0,1},{1,0},{2,3},{3,2},{4,5},{5,4},{6,7},{7,6},{8,9},{9,8},{10,11... | collective-permute-start | bytes 737288 | tf_op jit(solution)/shard_map/ppermute | solution.py:275
  43.2 4.4 %collective-permute-start.10 = (bf16[160,768]{1,0:T(8,128)(2,1)S(1)}, bf16[160,768]{1,0:T(8,128)(2,1)}, u32[]{:S(2)}, u32[]{:S(2)}) collective-permute-start(bf16[160,768]{1,0:T(8,128)(2,1)S(1)} %collective-permute-done.8.refs_2_), channel_id=1, source_target_pairs={{0,1},{1,0},{2,3},{3,2},{4,5},{5,4},{6,7},{7,6},{8,9},{9,8},{10,11... | collective-permute-start | bytes 737288 | tf_op jit(solution)/shard_map/ppermute | solution.py:275
  43.2 4.4 %collective-permute-start.14 = (bf16[160,768]{1,0:T(8,128)(2,1)}, bf16[160,768]{1,0:T(8,128)(2,1)}, u32[]{:S(2)}, u32[]{:S(2)}) collective-permute-start(bf16[160,768]{1,0:T(8,128)(2,1)} %collective-permute-done.12.refs_6_), channel_id=1, source_target_pairs={{0,1},{1,0},{2,3},{3,2},{4,5},{5,4},{6,7},{7,6},{8,9},{9,8},{10,11... | collective-permute-start | bytes 737288 | tf_op jit(solution)/shard_map/ppermute | solution.py:275
  45.7 16.8 %collective-permute-start.1 = (bf16[2,256,2,2,128]{4,3,2,1,0:T(2,128)(2,1)S(1)}, bf16[2,256,2,2,128]{4,3,2,1,0:T(2,128)(2,1)S(1)}, u32[]{:S(2)}, u32[]{:S(2)}) collective-permute-start(bf16[2,256,2,2,128]{4,3,2,1,0:T(2,128)(2,1)S(1)} %shard_map.87), channel_id=1, source_target_pairs={{0,4},{4,8},{8,12},{12,0},{1,5},{5,9},{9,13},{13,1},{2,6},{6,10},{... | collective-permute-start | bytes 1572872 | tf_op jit(solution)/shard_map/ppermute | solution.py:272
  45.7 8.0 %collective-permute-start.4 = (bf16[160,768]{1,0:T(8,128)(2,1)S(1)}, bf16[160,768]{1,0:T(8,128)(2,1)S(1)}, u32[]{:S(2)}, u32[]{:S(2)}) collective-permute-start(bf16[160,768]{1,0:T(8,128)(2,1)S(1)} %collective-permute-done.3.refs_1_), channel_id=1, source_target_pairs={{0,2},{1,3},{2,0},{3,1},{4,6},{5,7},{6,4},{7,5},{8,10},{9,11},{10,... | collective-permute-start | bytes 737288 | tf_op jit(solution)/shard_map/ppermute | solution.py:275
  53.6 20.9 %copy-start.15 = (s32[1,4]{1,0:T(1,128)S(1)}, s32[1,4]{1,0:T(1,128)}, u32[]{:S(2)}) copy-start(s32[1,4]{1,0:T(1,128)} %param.9) | copy-start | bytes 52
  53.6 51.0 %copy-start.3 = (bf16[2,256,2,2,128]{4,3,2,1,0:T(2,128)(2,1)S(1)}, bf16[2,256,2,2,128]{4,3,2,1,0:T(2,128)(2,1)}, u32[]{:S(2)}) copy-start(bf16[2,256,2,2,128]{4,3,2,1,0:T(2,128)(2,1)} %get-tuple-element.16.refs_0_) | copy-start | bytes 1572868
  53.6 19.7 %collective-permute-start.16 = (f32[2,80,512]{2,1,0:T(8,128)}, f32[2,80,512]{2,1,0:T(8,128)S(1)}, u32[]{:S(2)}, u32[]{:S(2)}) collective-permute-start(f32[2,80,512]{2,1,0:T(8,128)} %get-tuple-element.27), channel_id=1, source_target_pairs={{0,4},{4,0},{8,12},{12,8},{1,5},{5,1},{9,13},{13,9},{2,6},{6,2},{1... | collective-permute-start | bytes 983048 | tf_op jit(solution)/shard_map/ppermute | solution.py:275
  53.7 3.3 %collective-permute-start.5 = (bf16[160,768]{1,0:T(8,128)(2,1)S(1)}, bf16[160,768]{1,0:T(8,128)(2,1)}, u32[]{:S(2)}, u32[]{:S(2)}) collective-permute-start(bf16[160,768]{1,0:T(8,128)(2,1)S(1)} %collective-permute-done.3.refs_1_), channel_id=1, source_target_pairs={{0,1},{1,0},{2,3},{3,2},{4,5},{5,4},{6,7},{7,6},{8,9},{9,8},{10,11... | collective-permute-start | bytes 737288 | tf_op jit(solution)/shard_map/ppermute | solution.py:275
  53.8 3.2 %collective-permute-start.6 = (bf16[160,768]{1,0:T(8,128)(2,1)S(1)}, bf16[160,768]{1,0:T(8,128)(2,1)}, u32[]{:S(2)}, u32[]{:S(2)}) collective-permute-start(bf16[160,768]{1,0:T(8,128)(2,1)S(1)} %collective-permute-done.4.refs_2_), channel_id=1, source_target_pairs={{0,1},{1,0},{2,3},{3,2},{4,5},{5,4},{6,7},{7,6},{8,9},{9,8},{10,11... | collective-permute-start | bytes 737288 | tf_op jit(solution)/shard_map/ppermute | solution.py:275
  55.0 26.9 %collective-permute-start.15 = (f32[2,80,512]{2,1,0:T(8,128)}, f32[2,80,512]{2,1,0:T(8,128)}, u32[]{:S(2)}, u32[]{:S(2)}) collective-permute-start(f32[2,80,512]{2,1,0:T(8,128)} %get-tuple-element.25), channel_id=1, source_target_pairs={{0,4},{4,0},{8,12},{12,8},{1,5},{5,1},{9,13},{13,9},{2,6},{6,2},{1... | collective-permute-start | bytes 983048 | tf_op jit(solution)/shard_map/ppermute | solution.py:275
  62.6 42.0 %collective-permute-start.2 = (bf16[2,256,2,2,128]{4,3,2,1,0:T(2,128)(2,1)S(1)}, bf16[2,256,2,2,128]{4,3,2,1,0:T(2,128)(2,1)S(1)}, u32[]{:S(2)}, u32[]{:S(2)}) collective-permute-start(bf16[2,256,2,2,128]{4,3,2,1,0:T(2,128)(2,1)S(1)} %shard_map.88), channel_id=1, source_target_pairs={{0,8},{4,12},{8,0},{12,4},{1,9},{5,13},{9,1},{13,5},{2,10},{6,14},... | collective-permute-start | bytes 1572872 | tf_op jit(solution)/shard_map/ppermute | solution.py:272
  74.3 29.0 %collective-permute-start.17 = (f32[2,80,512]{2,1,0:T(8,128)S(1)}, f32[2,80,512]{2,1,0:T(8,128)}, u32[]{:S(2)}, u32[]{:S(2)}) collective-permute-start(f32[2,80,512]{2,1,0:T(8,128)S(1)} %shard_map.93), channel_id=1, source_target_pairs={{0,8},{4,12},{8,0},{12,4},{1,9},{5,13},{9,1},{13,5},{2,10},{6,14},... | collective-permute-start | bytes 983048 | tf_op jit(solution)/shard_map/ppermute | solution.py:272
  (10 other events, 58.6 us)

commit v8 on v7

--- a/solution.py
+++ b/solution.py
@@ -12,7 +12,7 @@
 LAYERS = 2
 CHUNK = 8
 ROWS = 16
-UNROLL = 8
+UNROLL = 20
 CUTS = 3
 VMEM_BYTES = 16 * 1024 * 1024
 PARAMS = pltpu.CompilerParams(vmem_limit_bytes=VMEM_BYTES)

time: 115 us -> 115 us (level)
  no operation moved by 1% of the time
where the time goes in v8:
time: 115 us; the launch traced here: 114 us
  waiting for transfers between devices  47 us (41%)
  Pallas kernels  20.4 us (18%)
  starting transfers between devices  19.9 us (17%)
  local copies, waits for them, and re-layouts  17.6 us (15%)
  blocking collectives  5.67 us (5%)
  other arithmetic  2.4 us (2%)
    ppermute x11, waiting for transfers between devices, swap(): return lax.ppermute(value, axis, [(i, i ^ bit) for i in range(size)])  23.8 us
    ppermute x7, waiting for transfers between devices, shift(): return lax.ppermute(value, 'hold', [(i, (i + k) % n) for i in range(n)])  23.2 us
    ppermute x7, starting transfers between devices, shift(): return lax.ppermute(value, 'hold', [(i, (i + k) % n) for i in range(n)])  13.4 us
    pallas_call x2, Pallas kernels, products(): pl.pallas_call(functools.partial(product_kernel, counts), in_specs=[SMEM]...  11.4 us
    reshape x1, local copies, waits for them, and re-layouts, local(): weight = kv_weight.reshape(LAYERS, feats, cols)  10.1 us
    ppermute x11, starting transfers between devices, swap(): return lax.ppermute(value, axis, [(i, i ^ bit) for i in range(size)])  6.48 us
    psum x1, blocking collectives, local(): sums = lax.psum(sums, 'tp').reshape(2, LAYERS, rec)  5.67 us
    unnamed x32, local copies, waits for them, and re-layouts  4.87 us
  transfers between devices with their start and end apart: 18, of which 6 were waited for; matrix products, arithmetic and copies ran while one was open for 12% of the time, Pallas kernels for 13%

profile of v8, /device:TPU:0, one launch (start us, length us, event | category | flops | bytes accessed | tf_op | source)
XLA Modules:
  0.0 114.0 jit_solution(3495258521711607694)
XLA Ops:
  1.3 3.1 %shard_map.86 = (bf16[2,256,2,2,128]{4,3,2,1,0:T(2,128)(2,1)}, bf16[2,256,2,2,128]{4,3,2,1,0:T(2,128)(2,1)}, bf16[2,256,2,2,128]{4,3,2,1,0:T(2,128)(2,1)}, bf16[2,256,2,2,128]{4,3,2,1,0:T(2,128)(2,1)}) custom-call(s32[4]{0:T(128)} %pad_add_fusion.at, bf16[2,4,256,2,2,128]{5,4,3,2,1,0:T(2,128)(2,1)} %store.1), custom_call_target="tpu_custom_call" | custom-call | tf_op jit(solution)/shard_map/pallas_call | solution.py:95
  4.4 5.1 %collective-permute-start = (bf16[2,256,2,2,128]{4,3,2,1,0:T(2,128)(2,1)}, bf16[2,256,2,2,128]{4,3,2,1,0:T(2,128)(2,1)S(1)}, u32[]{:S(2)}, u32[]{:S(2)}) collective-permute-start(bf16[2,256,2,2,128]{4,3,2,1,0:T(2,128)(2,1)} %get-tuple-element.18), channel_id=1, source_target_pairs={{0,12},{4,0},{8,4},{12,8},{1,13},{5,1},{9,5},{13,9},{2,14},{6,2},{... | collective-permute-start | bytes 1572872 | tf_op jit(solution)/shard_map/ppermute | solution.py:272
  9.6 2.1 %copy-done = bf16[2,80,12288]{2,1,0:T(8,128)(2,1)S(1)} copy-done((bf16[2,80,12288]{2,1,0:T(8,128)(2,1)S(1)}, bf16[2,80,12288]{2,1,0:T(8,128)(2,1)}, u32[]{:S(2)}) %copy-start) | copy-done | bytes 3932184
  12.5 2.9 %shard_map.89 = (bf16[160,3072]{1,0:T(8,128)(2,1)S(1)}, bf16[160,768]{1,0:T(8,128)(2,1)S(1)}, bf16[160,768]{1,0:T(8,128)(2,1)S(1)}, bf16[160,768]{1,0:T(8,128)(2,1)S(1)}) custom-call(s32[4]{0:T(128)S(1)} %pad_add_fusion.1.at, bf16[160,12288]{1,0:T(8,128)(2,1)S(1)} %bitcast.19, bf16[2,12288]{1,0:T(2,128)(2,1)S(1)} %copy-done.7), custom_call_target="tpu_custom_call" | custom-call | tf_op jit(solution)/shard_map/pallas_call | solution.py:49
  15.4 0.9 copy-done.2
  16.3 3.8 %collective-permute-start.11 = (bf16[160,768]{1,0:T(8,128)(2,1)S(1)}, bf16[160,768]{1,0:T(8,128)(2,1)S(1)}, u32[]{:S(2)}, u32[]{:S(2)}) collective-permute-start(bf16[160,768]{1,0:T(8,128)(2,1)S(1)} %get-tuple-element.24), channel_id=1, source_target_pairs={{0,12},{4,0},{8,4},{12,8},{1,13},{5,1},{9,5},{13,9},{2,14},{6,2},{... | collective-permute-start | bytes 737288 | tf_op jit(solution)/shard_map/ppermute | solution.py:272
  20.1 10.1 %reshape.50.refs_0_ = bf16[2,3072,512]{2,1,0:T(8,128)(2,1)} reshape(bf16[2,3072,2,2,128]{4,3,2,1,0:T(2,128)(2,1)} %param.13) | data formatting | bytes 12582912 | tf_op jit(solution)/shard_map/reshape | solution.py:303
  31.0 1.5 %collective-permute-start.8 = (bf16[160,768]{1,0:T(8,128)(2,1)S(1)}, bf16[160,768]{1,0:T(8,128)(2,1)S(1)}, u32[]{:S(2)}, u32[]{:S(2)}) collective-permute-start(bf16[160,768]{1,0:T(8,128)(2,1)S(1)} %shard_map.91.refs_1_), channel_id=1, source_target_pairs={{0,2},{1,3},{2,0},{3,1},{4,6},{5,7},{6,4},{7,5},{8,10},{9,11},{10,... | collective-permute-start | bytes 737288 | tf_op jit(solution)/shard_map/ppermute | solution.py:275
  33.0 1.4 %collective-permute-start.3 = (bf16[160,768]{1,0:T(8,128)(2,1)S(1)}, bf16[160,768]{1,0:T(8,128)(2,1)S(1)}, u32[]{:S(2)}, u32[]{:S(2)}) collective-permute-start(bf16[160,768]{1,0:T(8,128)(2,1)S(1)} %get-tuple-element.20), channel_id=1, source_target_pairs={{0,8},{4,12},{8,0},{12,4},{1,9},{5,13},{9,1},{13,5},{2,10},{6,14},... | collective-permute-start | bytes 737288 | tf_op jit(solution)/shard_map/ppermute | solution.py:272
  34.4 5.4 %collective-permute-done.8.refs_2_ = bf16[160,768]{1,0:T(8,128)(2,1)S(1)} collective-permute-done((bf16[160,768]{1,0:T(8,128)(2,1)S(1)}, bf16[160,768]{1,0:T(8,128)(2,1)S(1)}, u32[]{:S(2)}, u32[]{:S(2)}) %collective-permute-start.8) | collective-permute-done | bytes 245792 | tf_op jit(solution)/shard_map/ppermute | solution.py:275
  39.9 3.3 %collective-permute-done.12.refs_6_ = bf16[160,768]{1,0:T(8,128)(2,1)} collective-permute-done((bf16[160,768]{1,0:T(8,128)(2,1)S(1)}, bf16[160,768]{1,0:T(8,128)(2,1)}, u32[]{:S(2)}, u32[]{:S(2)}) %collective-permute-start.12) | collective-permute-done | bytes 245792 | tf_op jit(solution)/shard_map/ppermute | solution.py:275
  43.7 1.9 %collective-permute-done.3.refs_1_ = bf16[160,768]{1,0:T(8,128)(2,1)S(1)} collective-permute-done((bf16[160,768]{1,0:T(8,128)(2,1)S(1)}, bf16[160,768]{1,0:T(8,128)(2,1)S(1)}, u32[]{:S(2)}, u32[]{:S(2)}) %collective-permute-start.3) | collective-permute-done | bytes 245792 | tf_op jit(solution)/shard_map/ppermute | solution.py:272
  45.7 1.4 %collective-permute-start.4 = (bf16[160,768]{1,0:T(8,128)(2,1)S(1)}, bf16[160,768]{1,0:T(8,128)(2,1)S(1)}, u32[]{:S(2)}, u32[]{:S(2)}) collective-permute-start(bf16[160,768]{1,0:T(8,128)(2,1)S(1)} %collective-permute-done.3.refs_1_), channel_id=1, source_target_pairs={{0,2},{1,3},{2,0},{3,1},{4,6},{5,7},{6,4},{7,5},{8,10},{9,11},{10,... | collective-permute-start | bytes 737288 | tf_op jit(solution)/shard_map/ppermute | solution.py:275
  47.7 5.9 %shard_map.92 = (f32[2,80,512]{2,1,0:T(8,128)}, f32[2,80,512]{2,1,0:T(8,128)}) custom-call(s32[10]{0:T(128)} %stack.79.at, bf16[2,3072,512]{2,1,0:T(8,128)(2,1)} %reshape.50.refs_0_, bf16[160,768]{1,0:T(8,128)(2,1)} %copy-done.1, bf16[160,768]{1,0:T(8,128)(2,1)} %copy-done.10, bf16[160,768]{1,0:T(8,128)(2,1)} %copy-done.12, ...), custom_call_target="tpu_custom_call" | custom-call | tf_op jit(solution)/shard_map/pallas_call | solution.py:157
  55.0 1.9 %collective-permute-start.15 = (f32[2,80,512]{2,1,0:T(8,128)}, f32[2,80,512]{2,1,0:T(8,128)}, u32[]{:S(2)}, u32[]{:S(2)}) collective-permute-start(f32[2,80,512]{2,1,0:T(8,128)} %get-tuple-element.25), channel_id=1, source_target_pairs={{0,4},{4,0},{8,12},{12,8},{1,5},{5,1},{9,13},{13,9},{2,6},{6,2},{1... | collective-permute-start | bytes 983048 | tf_op jit(solution)/shard_map/ppermute | solution.py:275
  57.0 5.5 %shard_map.90 = (f32[2,80,512]{2,1,0:T(8,128)}, f32[2,80,512]{2,1,0:T(8,128)}) custom-call(s32[7]{0:T(128)} %stack.71.at, bf16[2,3072,512]{2,1,0:T(8,128)(2,1)} %reshape.50.refs_0_, bf16[160,768]{1,0:T(8,128)(2,1)} %copy-done.8, bf16[160,768]{1,0:T(8,128)(2,1)} %copy-done.11, bf16[160,768]{1,0:T(8,128)(2,1)} %collective-permute-done.5.refs_3_, ...), custom_call_target="tpu_custom_call" | custom-call | tf_op jit(solution)/shard_map/pallas_call | solution.py:157
  62.6 3.0 %collective-permute-start.2 = (bf16[2,256,2,2,128]{4,3,2,1,0:T(2,128)(2,1)S(1)}, bf16[2,256,2,2,128]{4,3,2,1,0:T(2,128)(2,1)S(1)}, u32[]{:S(2)}, u32[]{:S(2)}) collective-permute-start(bf16[2,256,2,2,128]{4,3,2,1,0:T(2,128)(2,1)S(1)} %shard_map.88), channel_id=1, source_target_pairs={{0,8},{4,12},{8,0},{12,4},{1,9},{5,13},{9,1},{13,5},{2,10},{6,14},... | collective-permute-start | bytes 1572872 | tf_op jit(solution)/shard_map/ppermute | solution.py:272
  65.6 7.7 %collective-permute-done.16.refs_1_ = f32[2,80,512]{2,1,0:T(8,128)S(1)} collective-permute-done((f32[2,80,512]{2,1,0:T(8,128)}, f32[2,80,512]{2,1,0:T(8,128)S(1)}, u32[]{:S(2)}, u32[]{:S(2)}) %collective-permute-start.16) | collective-permute-done | bytes 327712 | tf_op jit(solution)/shard_map/ppermute | solution.py:275
  73.3 1.0 copy-done.6
  74.7 7.3 %collective-permute-done.15 = f32[2,80,512]{2,1,0:T(8,128)} collective-permute-done((f32[2,80,512]{2,1,0:T(8,128)}, f32[2,80,512]{2,1,0:T(8,128)}, u32[]{:S(2)}, u32[]{:S(2)}) %collective-permute-start.15) | collective-permute-done | bytes 327712 | tf_op jit(solution)/shard_map/ppermute | solution.py:275
  82.0 21.3 %collective-permute-done.17 = f32[2,80,512]{2,1,0:T(8,128)} collective-permute-done((f32[2,80,512]{2,1,0:T(8,128)S(1)}, f32[2,80,512]{2,1,0:T(8,128)}, u32[]{:S(2)}, u32[]{:S(2)}) %collective-permute-start.17) | collective-permute-done | bytes 327712 | tf_op jit(solution)/shard_map/ppermute | solution.py:272
  103.3 1.2 %add_convert_fusion = bf16[2,80,512]{2,1,0:T(8,128)(2,1)S(1)} fusion(f32[2,80,512]{2,1,0:T(8,128)} %collective-permute-done.17, f32[2,80,512]{2,1,0:T(8,128)} %get-tuple-element.22, f32[2,80,512]{2,1,0:T(8,128)} %collective-permute-done.15), kind=kLoop, calls=%fused_computation | loop fusion | flops 245760 | bytes 1146880 | tf_op jit(solution)/shard_map/convert_element_type | solution.py:328
  104.6 3.0 %shard_map.94 = (bf16[2,512,2,2,128]{4,3,2,1,0:T(2,128)(2,1)}, f32[1,320]{1,0:T(1,128)S(1)}) custom-call(s32[4]{0:T(128)S(1)} %get-tuple-element.31.starts, s32[4]{0:T(128)S(1)} %get-tuple-element.30.lengths, s32[160]{0:T(256)S(1)} %reshape.49.spots, bf16[2,256,2,2,128]{4,3,2,1,0:T(2,128)(2,1)S(1)} %copy-done.3, ...), custom_call_target="tpu_custom_call" | custom-call | tf_op jit(solution)/shard_map/pallas_call | solution.py:253
  107.6 5.7 %psum.7 = f32[1,320]{1,0:T(1,128)S(1)} all-reduce(f32[1,320]{1,0:T(1,128)S(1)} %get-tuple-element.29), channel_id=1, replica_groups=mesh['groups'=2,'hold'=4,'tp'=4] {'tp'}, use_global_device_ids=true, to_apply=%region_3.4 | all-reduce | flops 320 | bytes 2560 | tf_op jit(solution)/shard_map/psum | solution.py:338
  (70 shorter events, 6.5 us)
Async XLA Ops:
  4.4 38.8 %collective-permute-start = (bf16[2,256,2,2,128]{4,3,2,1,0:T(2,128)(2,1)}, bf16[2,256,2,2,128]{4,3,2,1,0:T(2,128)(2,1)S(1)}, u32[]{:S(2)}, u32[]{:S(2)}) collective-permute-start(bf16[2,256,2,2,128]{4,3,2,1,0:T(2,128)(2,1)} %get-tuple-element.18), channel_id=1, source_target_pairs={{0,12},{4,0},{8,4},{12,8},{1,13},{5,1},{9,5},{13,9},{2,14},{6,2},{... | collective-permute-start | bytes 1572872 | tf_op jit(solution)/shard_map/ppermute | solution.py:272
  16.3 14.7 %collective-permute-start.7 = (bf16[160,768]{1,0:T(8,128)(2,1)S(1)}, bf16[160,768]{1,0:T(8,128)(2,1)S(1)}, u32[]{:S(2)}, u32[]{:S(2)}) collective-permute-start(bf16[160,768]{1,0:T(8,128)(2,1)S(1)} %get-tuple-element.23), channel_id=1, source_target_pairs={{0,4},{4,8},{8,12},{12,0},{1,5},{5,9},{9,13},{13,1},{2,6},{6,10},{... | collective-permute-start | bytes 737288 | tf_op jit(solution)/shard_map/ppermute | solution.py:272
  16.3 27.4 %copy-start.5 = (bf16[2,256,2,2,128]{4,3,2,1,0:T(2,128)(2,1)S(1)}, bf16[2,256,2,2,128]{4,3,2,1,0:T(2,128)(2,1)}, u32[]{:S(2)}) copy-start(bf16[2,256,2,2,128]{4,3,2,1,0:T(2,128)(2,1)} %get-tuple-element.17.refs_0_) | copy-start | bytes 1572868
  16.3 16.2 %collective-permute-start.11 = (bf16[160,768]{1,0:T(8,128)(2,1)S(1)}, bf16[160,768]{1,0:T(8,128)(2,1)S(1)}, u32[]{:S(2)}, u32[]{:S(2)}) collective-permute-start(bf16[160,768]{1,0:T(8,128)(2,1)S(1)} %get-tuple-element.24), channel_id=1, source_target_pairs={{0,12},{4,0},{8,4},{12,8},{1,13},{5,1},{9,5},{13,9},{2,14},{6,2},{... | collective-permute-start | bytes 737288 | tf_op jit(solution)/shard_map/ppermute | solution.py:272
  30.3 24.0 %copy-start.14 = (s32[1,4]{1,0:T(1,128)S(1)}, s32[1,4]{1,0:T(1,128)}, u32[]{:S(2)}) copy-start(s32[1,4]{1,0:T(1,128)} %param.8) | copy-start | bytes 52
  30.3 24.7 %copy-start.13 = (s32[2,80]{1,0:T(2,128)S(1)}, s32[2,80]{1,0:T(2,128)}, u32[]{:S(2)}) copy-start(s32[2,80]{1,0:T(2,128)} %param.10) | copy-start | bytes 1924
  31.0 16.7 %copy-start.1 = (bf16[160,768]{1,0:T(8,128)(2,1)}, bf16[160,768]{1,0:T(8,128)(2,1)S(1)}, u32[]{:S(2)}) copy-start(bf16[160,768]{1,0:T(8,128)(2,1)S(1)} %shard_map.91.refs_1_) | copy-start | bytes 737284
  31.0 8.9 %collective-permute-start.8 = (bf16[160,768]{1,0:T(8,128)(2,1)S(1)}, bf16[160,768]{1,0:T(8,128)(2,1)S(1)}, u32[]{:S(2)}, u32[]{:S(2)}) collective-permute-start(bf16[160,768]{1,0:T(8,128)(2,1)S(1)} %shard_map.91.refs_1_), channel_id=1, source_target_pairs={{0,2},{1,3},{2,0},{3,1},{4,6},{5,7},{6,4},{7,5},{8,10},{9,11},{10,... | collective-permute-start | bytes 737288 | tf_op jit(solution)/shard_map/ppermute | solution.py:275
  32.5 10.7 %collective-permute-start.12 = (bf16[160,768]{1,0:T(8,128)(2,1)S(1)}, bf16[160,768]{1,0:T(8,128)(2,1)}, u32[]{:S(2)}, u32[]{:S(2)}) collective-permute-start(bf16[160,768]{1,0:T(8,128)(2,1)S(1)} %collective-permute-done.11.refs_5_), channel_id=1, source_target_pairs={{0,2},{1,3},{2,0},{3,1},{4,6},{5,7},{6,4},{7,5},{8,10},{9,11},{10,... | collective-permute-start | bytes 737288 | tf_op jit(solution)/shard_map/ppermute | solution.py:275
  33.0 12.7 %collective-permute-start.3 = (bf16[160,768]{1,0:T(8,128)(2,1)S(1)}, bf16[160,768]{1,0:T(8,128)(2,1)S(1)}, u32[]{:S(2)}, u32[]{:S(2)}) collective-permute-start(bf16[160,768]{1,0:T(8,128)(2,1)S(1)} %get-tuple-element.20), channel_id=1, source_target_pairs={{0,8},{4,12},{8,0},{12,4},{1,9},{5,13},{9,1},{13,5},{2,10},{6,14},... | collective-permute-start | bytes 737288 | tf_op jit(solution)/shard_map/ppermute | solution.py:272
  34.4 11.2 %collective-permute-start.9 = (bf16[160,768]{1,0:T(8,128)(2,1)S(1)}, bf16[160,768]{1,0:T(8,128)(2,1)S(1)}, u32[]{:S(2)}, u32[]{:S(2)}) collective-permute-start(bf16[160,768]{1,0:T(8,128)(2,1)S(1)} %shard_map.91.refs_1_), channel_id=1, source_target_pairs={{0,1},{1,0},{2,3},{3,2},{4,5},{5,4},{6,7},{7,6},{8,9},{9,8},{10,11... | collective-permute-start | bytes 737288 | tf_op jit(solution)/shard_map/ppermute | solution.py:275
  39.9 7.8 %collective-permute-start.13 = (bf16[160,768]{1,0:T(8,128)(2,1)S(1)}, bf16[160,768]{1,0:T(8,128)(2,1)}, u32[]{:S(2)}, u32[]{:S(2)}) collective-permute-start(bf16[160,768]{1,0:T(8,128)(2,1)S(1)} %collective-permute-done.11.refs_5_), channel_id=1, source_target_pairs={{0,1},{1,0},{2,3},{3,2},{4,5},{5,4},{6,7},{7,6},{8,9},{9,8},{10,11... | collective-permute-start | bytes 737288 | tf_op jit(solution)/shard_map/ppermute | solution.py:275
  43.2 4.4 %collective-permute-start.10 = (bf16[160,768]{1,0:T(8,128)(2,1)S(1)}, bf16[160,768]{1,0:T(8,128)(2,1)}, u32[]{:S(2)}, u32[]{:S(2)}) collective-permute-start(bf16[160,768]{1,0:T(8,128)(2,1)S(1)} %collective-permute-done.8.refs_2_), channel_id=1, source_target_pairs={{0,1},{1,0},{2,3},{3,2},{4,5},{5,4},{6,7},{7,6},{8,9},{9,8},{10,11... | collective-permute-start | bytes 737288 | tf_op jit(solution)/shard_map/ppermute | solution.py:275
  43.2 4.4 %collective-permute-start.14 = (bf16[160,768]{1,0:T(8,128)(2,1)}, bf16[160,768]{1,0:T(8,128)(2,1)}, u32[]{:S(2)}, u32[]{:S(2)}) collective-permute-start(bf16[160,768]{1,0:T(8,128)(2,1)} %collective-permute-done.12.refs_6_), channel_id=1, source_target_pairs={{0,1},{1,0},{2,3},{3,2},{4,5},{5,4},{6,7},{7,6},{8,9},{9,8},{10,11... | collective-permute-start | bytes 737288 | tf_op jit(solution)/shard_map/ppermute | solution.py:275
  45.7 16.8 %collective-permute-start.1 = (bf16[2,256,2,2,128]{4,3,2,1,0:T(2,128)(2,1)S(1)}, bf16[2,256,2,2,128]{4,3,2,1,0:T(2,128)(2,1)S(1)}, u32[]{:S(2)}, u32[]{:S(2)}) collective-permute-start(bf16[2,256,2,2,128]{4,3,2,1,0:T(2,128)(2,1)S(1)} %shard_map.87), channel_id=1, source_target_pairs={{0,4},{4,8},{8,12},{12,0},{1,5},{5,9},{9,13},{13,1},{2,6},{6,10},{... | collective-permute-start | bytes 1572872 | tf_op jit(solution)/shard_map/ppermute | solution.py:272
  45.7 8.0 %collective-permute-start.4 = (bf16[160,768]{1,0:T(8,128)(2,1)S(1)}, bf16[160,768]{1,0:T(8,128)(2,1)S(1)}, u32[]{:S(2)}, u32[]{:S(2)}) collective-permute-start(bf16[160,768]{1,0:T(8,128)(2,1)S(1)} %collective-permute-done.3.refs_1_), channel_id=1, source_target_pairs={{0,2},{1,3},{2,0},{3,1},{4,6},{5,7},{6,4},{7,5},{8,10},{9,11},{10,... | collective-permute-start | bytes 737288 | tf_op jit(solution)/shard_map/ppermute | solution.py:275
  53.6 20.9 %copy-start.15 = (s32[1,4]{1,0:T(1,128)S(1)}, s32[1,4]{1,0:T(1,128)}, u32[]{:S(2)}) copy-start(s32[1,4]{1,0:T(1,128)} %param.9) | copy-start | bytes 52
  53.6 51.0 %copy-start.3 = (bf16[2,256,2,2,128]{4,3,2,1,0:T(2,128)(2,1)S(1)}, bf16[2,256,2,2,128]{4,3,2,1,0:T(2,128)(2,1)}, u32[]{:S(2)}) copy-start(bf16[2,256,2,2,128]{4,3,2,1,0:T(2,128)(2,1)} %get-tuple-element.16.refs_0_) | copy-start | bytes 1572868
  53.6 19.7 %collective-permute-start.16 = (f32[2,80,512]{2,1,0:T(8,128)}, f32[2,80,512]{2,1,0:T(8,128)S(1)}, u32[]{:S(2)}, u32[]{:S(2)}) collective-permute-start(f32[2,80,512]{2,1,0:T(8,128)} %get-tuple-element.27), channel_id=1, source_target_pairs={{0,4},{4,0},{8,12},{12,8},{1,5},{5,1},{9,13},{13,9},{2,6},{6,2},{1... | collective-permute-start | bytes 983048 | tf_op jit(solution)/shard_map/ppermute | solution.py:275
  53.7 3.3 %collective-permute-start.5 = (bf16[160,768]{1,0:T(8,128)(2,1)S(1)}, bf16[160,768]{1,0:T(8,128)(2,1)}, u32[]{:S(2)}, u32[]{:S(2)}) collective-permute-start(bf16[160,768]{1,0:T(8,128)(2,1)S(1)} %collective-permute-done.3.refs_1_), channel_id=1, source_target_pairs={{0,1},{1,0},{2,3},{3,2},{4,5},{5,4},{6,7},{7,6},{8,9},{9,8},{10,11... | collective-permute-start | bytes 737288 | tf_op jit(solution)/shard_map/ppermute | solution.py:275
  53.8 3.2 %collective-permute-start.6 = (bf16[160,768]{1,0:T(8,128)(2,1)S(1)}, bf16[160,768]{1,0:T(8,128)(2,1)}, u32[]{:S(2)}, u32[]{:S(2)}) collective-permute-start(bf16[160,768]{1,0:T(8,128)(2,1)S(1)} %collective-permute-done.4.refs_2_), channel_id=1, source_target_pairs={{0,1},{1,0},{2,3},{3,2},{4,5},{5,4},{6,7},{7,6},{8,9},{9,8},{10,11... | collective-permute-start | bytes 737288 | tf_op jit(solution)/shard_map/ppermute | solution.py:275
  55.0 26.9 %collective-permute-start.15 = (f32[2,80,512]{2,1,0:T(8,128)}, f32[2,80,512]{2,1,0:T(8,128)}, u32[]{:S(2)}, u32[]{:S(2)}) collective-permute-start(f32[2,80,512]{2,1,0:T(8,128)} %get-tuple-element.25), channel_id=1, source_target_pairs={{0,4},{4,0},{8,12},{12,8},{1,5},{5,1},{9,13},{13,9},{2,6},{6,2},{1... | collective-permute-start | bytes 983048 | tf_op jit(solution)/shard_map/ppermute | solution.py:275
  62.6 42.0 %collective-permute-start.2 = (bf16[2,256,2,2,128]{4,3,2,1,0:T(2,128)(2,1)S(1)}, bf16[2,256,2,2,128]{4,3,2,1,0:T(2,128)(2,1)S(1)}, u32[]{:S(2)}, u32[]{:S(2)}) collective-permute-start(bf16[2,256,2,2,128]{4,3,2,1,0:T(2,128)(2,1)S(1)} %shard_map.88), channel_id=1, source_target_pairs={{0,8},{4,12},{8,0},{12,4},{1,9},{5,13},{9,1},{13,5},{2,10},{6,14},... | collective-permute-start | bytes 1572872 | tf_op jit(solution)/shard_map/ppermute | solution.py:272
  74.3 29.0 %collective-permute-start.17 = (f32[2,80,512]{2,1,0:T(8,128)S(1)}, f32[2,80,512]{2,1,0:T(8,128)}, u32[]{:S(2)}, u32[]{:S(2)}) collective-permute-start(f32[2,80,512]{2,1,0:T(8,128)S(1)} %shard_map.93), channel_id=1, source_target_pairs={{0,8},{4,12},{8,0},{12,4},{1,9},{5,13},{9,1},{13,5},{2,10},{6,14},... | collective-permute-start | bytes 983048 | tf_op jit(solution)/shard_map/ppermute | solution.py:272
  (10 other events, 58.6 us)
